TPU v7x, 32 devices: a whole 2x2x4 slice. The times are simulated.
32 devices in a mesh: dp: 8 (over y, x, core), tensor: 4 (over z).
Axes of the slice: x: 2, y: 2, z: 4, core: 2. Of those that a mesh axis runs over, the one named last changes fastest.
Arguments:
- hidden_in: bfloat16 [24576, 1536], P('dp', 'tensor'), may hold values from -6 to 6, as said below
- out_grad: bfloat16 [24576, 1536], P('dp', 'tensor'), may hold values from -6 to 6, as said below
- seq_lengths: int32 [16], replicated, may hold values from 256 to 3072, as said below
- seq_device: int32 [16], replicated, may hold values from 0 to 7, as said below
- seq_offset: int32 [16], replicated, may hold values from 0 to 2048, as said below
- norm_gain: float32 [1536], replicated, may hold values from 0.5 to 1.5
- w_gate: bfloat16 [1536, 3072], P(None, 'tensor'), may hold values from -0.15625 to 0.15625
- w_input: bfloat16 [1536, 3072], P(None, 'tensor'), may hold values from -0.15625 to 0.15625
- w_shared: bfloat16 [1536, 256], replicated, may hold values from -0.15625 to 0.15625
- w_step: bfloat16 [1536, 48], P(None, 'tensor'), may hold values from -0.15625 to 0.15625
- conv_inner: float32 [4, 3072], P(None, 'tensor'), may hold values from -3 to 3
- conv_shared: float32 [4, 256], replicated, may hold values from -3 to 3
- conv_inner_bias: float32 [3072], P('tensor'), may hold values from -0.5 to 0.5
- conv_shared_bias: float32 [256], replicated, may hold values from -0.5 to 0.5
- step_bias: float32 [48], P('tensor'), may hold values from -6 to -2
- decay_log: float32 [48], P('tensor'), may hold values from -7 to 1
- skip_gain: float32 [48], P('tensor'), may hold values from 0.5 to 2
- gate_norm_gain: float32 [3072], P('tensor'), may hold values from 0.5 to 1.5
- w_output: bfloat16 [3072, 1536], P('tensor'), may hold values from -0.109375 to 0.109375
Outputs:
- mixed_out: bfloat16 [24576, 1536], P('dp', 'tensor')
- hidden_grad: float32 [24576, 1536], P('dp', 'tensor')
- norm_gain_grad: float32 [1536], replicated
- w_gate_grad: float32 [1536, 3072], P(None, 'tensor')
- w_input_grad: float32 [1536, 3072], P(None, 'tensor')
- w_shared_grad: float32 [1536, 256], replicated
- w_step_grad: float32 [1536, 48], P(None, 'tensor')
- conv_inner_grad: float32 [4, 3072], P(None, 'tensor')
- conv_shared_grad: float32 [4, 256], replicated
- conv_inner_bias_grad: float32 [3072], P('tensor')
- conv_shared_bias_grad: float32 [256], replicated
- step_bias_grad: float32 [48], P('tensor')
- decay_log_grad: float32 [48], P('tensor')
- skip_gain_grad: float32 [48], P('tensor')
- gate_norm_gain_grad: float32 [3072], P('tensor')
- w_output_grad: float32 [3072, 1536], P('tensor')
Inputs may be any that keep to these rules, and one draw needn't show every extreme that they name: `hidden_in`: entries are independent, of deviation one. `out_grad`: entries are independent, of deviation one. `seq_lengths`: lengths are multiples of 256; some sequence has exactly 3072 rows. `seq_device`: half of the dp indices hold one sequence and half hold three; every index holds one or more. Sequence numbers follow no order. `seq_offset`: offsets are multiples of 256; the sequences of one dp index lie end to end from its row 0, and offset plus length is at most 3072; the largest offset is reached.
All inputs are finite; a program needn't handle non-finite values.
Results may differ from a plain program's by a relative error of at most 0.012.
The roundings to bfloat16 on the way count: a program that leaves them out, or rounds other values in their place, can miss the bound.
Values may be sent and summed in bfloat16 or wider, within the bound.
No kernel may reach another device: no remote copies, remote signals or barrier semaphores. Data moves between devices by JAX's collectives and lax.ppermute only.
A program may use at most 320 MiB of HBM per device.

v0:
```python
import jax
import jax.numpy as jnp
from jax import lax
from jax.sharding import PartitionSpec as P

BLOCK_LEN = 256
DINNER = 3072


PRECISE = lax.Precision.HIGHEST
epsilon = 1e-05


def product(left_side, right_side):
    return jnp.dot(left_side, right_side, preferred_element_type=jnp.float32)


def transpose_dot(left_side, right_side):
    return lax.dot_general(
        left_side, right_side, (((0,), (0,)), ((), ())), preferred_element_type=jnp.float32
    )


def back_dot(left_side, right_side):
    return lax.dot_general(
        left_side, right_side, (((1,), (1,)), ((), ())), preferred_element_type=jnp.float32
    )


def swish_act(values):
    return values * jax.nn.sigmoid(values)


def row_layout(lengths, owners, offsets, device_index, row_count):
    row_ids = jnp.arange(row_count, dtype=jnp.int32)[:, None]
    inside = (
        (owners[None, :] == device_index)
        & (row_ids >= offsets[None, :])
        & (row_ids < offsets[None, :] + lengths[None, :])
    )
    positions = jnp.sum(jnp.where(inside, row_ids - offsets[None, :], 0), axis=1)
    live_rows = jnp.sum(inside.astype(jnp.float32), axis=1)
    return (positions, live_rows)


def causal_conv(values, kernel, offset_bias, positions):
    row_count = values.shape[0]
    taps = kernel.shape[0]
    summed = offset_bias[None, :] + kernel[taps - 1][None, :] * values
    for lag_steps in range(1, taps):
        shifted = jnp.pad(values, ((lag_steps, 0), (0, 0)))[:row_count]
        allowed = (positions >= lag_steps).astype(jnp.float32)[:, None]
        summed = summed + kernel[taps - 1 - lag_steps][None, :] * shifted * allowed
    return swish_act(summed)


def state_space(inner_vals, step_sizes, decays, input_map, output_map, fresh_block):
    row_count, head_count, head_width = inner_vals.shape
    block_count = row_count // BLOCK_LEN
    values = inner_vals.reshape(block_count, BLOCK_LEN, head_count, head_width)
    deltas = step_sizes.reshape(block_count, BLOCK_LEN, head_count)
    cumulative = jnp.cumsum(decays.reshape(block_count, BLOCK_LEN, head_count), axis=1)
    inputs_b = input_map.reshape(block_count, BLOCK_LEN, -1)
    outputs_c = output_map.reshape(block_count, BLOCK_LEN, -1)
    causal = (jnp.arange(BLOCK_LEN)[:, None] >= jnp.arange(BLOCK_LEN)[None, :])[None, None]
    by_head = jnp.swapaxes(cumulative, 1, 2)
    spread = by_head[:, :, :, None] - by_head[:, :, None, :]
    decay_map = jnp.where(causal, jnp.exp(jnp.where(causal, spread, 0.0)), 0.0)
    intersection = jnp.einsum("ctn,csn->cts", outputs_c, inputs_b, precision=PRECISE)
    mixing = decay_map * intersection[:, None] * jnp.swapaxes(deltas, 1, 2)[:, :, None, :]
    within = jnp.einsum("chts,cshp->cthp", mixing, values, precision=PRECISE)
    to_end = jnp.exp(cumulative[:, -1:, :] - cumulative) * deltas
    block_states = jnp.einsum("csn,csh,cshp->chnp", inputs_b, to_end, values, precision=PRECISE)
    block_decay = jnp.exp(cumulative[:, -1, :])

    def carry_step(carried, carry_item):
        is_fresh, decay_total, state_add = carry_item
        entering = jnp.where(is_fresh, jnp.zeros_like(carried), carried)
        return (decay_total[:, None, None] * entering + state_add, entering)

    initial = jnp.zeros(block_states.shape[1:], jnp.float32)
    final_state, entering_all = lax.scan(
        carry_step, initial, (fresh_block, block_decay, block_states)
    )
    across = jnp.einsum(
        "ctn,cth,chnp->cthp", outputs_c, jnp.exp(cumulative), entering_all, precision=PRECISE
    )
    return (within + across).reshape(row_count, head_count, head_width)


def mixer_core(
    inner_proj,
    shared_proj,
    raw_step,
    conv_inner,
    conv_shared,
    conv_inner_bias,
    conv_shared_bias,
    step_bias,
    decay_log,
    skip_gain,
    positions,
):
    head_count = raw_step.shape[1]
    row_count = inner_proj.shape[0]
    inner_conv = causal_conv(inner_proj, conv_inner, conv_inner_bias, positions)
    shared_conv = causal_conv(shared_proj, conv_shared, conv_shared_bias, positions)
    state_width = shared_conv.shape[1] // 2
    step_sizes = jax.nn.softplus(raw_step + step_bias[None, :])
    decays = -step_sizes * jnp.exp(decay_log)[None, :]
    fresh_block = positions[::BLOCK_LEN] == 0
    by_heads = inner_conv.reshape(row_count, head_count, -1)
    scanned = state_space(
        by_heads,
        step_sizes,
        decays,
        shared_conv[:, :state_width],
        shared_conv[:, state_width:],
        fresh_block,
    )
    return (scanned + skip_gain[None, :, None] * by_heads).reshape(row_count, -1)


def local(
    hidden_in,
    out_grad,
    seq_lengths,
    seq_device,
    seq_offset,
    norm_gain,
    w_gate,
    w_input,
    w_shared,
    w_step,
    conv_inner,
    conv_shared,
    conv_inner_bias,
    conv_shared_bias,
    step_bias,
    decay_log,
    skip_gain,
    gate_norm_gain,
    w_output,
):
    model_width = norm_gain.shape[0]
    piece_width = hidden_in.shape[1]
    column = lax.axis_index("tensor")
    positions, live_rows = row_layout(
        seq_lengths, seq_device, seq_offset, lax.axis_index("dp"), hidden_in.shape[0]
    )
    full_in, full_grad = (
        lax.all_gather(hidden_in, "tensor", axis=1, tiled=True),
        lax.all_gather(out_grad, "tensor", axis=1, tiled=True),
    )
    source = full_in.astype(jnp.float32)
    factor = lax.rsqrt(jnp.mean(source * source, axis=1, keepdims=True) + epsilon)
    normed = (source * factor * norm_gain[None, :]).astype(jnp.bfloat16)
    gate_proj = product(normed, w_gate)
    inner_proj = product(normed, w_input)
    shared_proj = product(normed, w_shared)
    raw_step = product(normed, w_step)

    def local_mix(*pieces):
        return mixer_core(*pieces, positions)

    scan_out, pullback = jax.vjp(
        local_mix,
        inner_proj,
        shared_proj,
        raw_step,
        conv_inner,
        conv_shared,
        conv_inner_bias,
        conv_shared_bias,
        step_bias,
        decay_log,
        skip_gain,
    )
    gate_act = swish_act(gate_proj)
    gated = scan_out * gate_act
    squares = lax.psum(jnp.sum(gated * gated, axis=1, keepdims=True), "tensor")
    gate_scale = lax.rsqrt(squares / DINNER + epsilon)
    normed_y = (gated * gate_scale * gate_norm_gain[None, :]).astype(jnp.bfloat16)
    contribution = product(normed_y, w_output)
    mixer_part = lax.psum_scatter(
        contribution.astype(jnp.bfloat16), "tensor", scatter_dimension=1, tiled=True
    ).astype(jnp.float32)
    mixed_out = (hidden_in.astype(jnp.float32) + live_rows[:, None] * mixer_part).astype(
        jnp.bfloat16
    )
    masked = full_grad * live_rows[:, None].astype(jnp.bfloat16)
    w_output_grad = transpose_dot(normed_y, masked)
    normed_y_grad = back_dot(masked, w_output)
    gate_norm_gain_grad = jnp.sum(normed_y_grad * gated * gate_scale, axis=0)
    weighted = normed_y_grad * gate_norm_gain[None, :]
    back_stat = lax.psum(jnp.sum(weighted * gated, axis=1, keepdims=True), "tensor")
    gated_grad = (
        gate_scale * weighted - gated * gate_scale * gate_scale * gate_scale * back_stat / DINNER
    )
    scan_grad = gated_grad * gate_act
    sigmoid_gate = jax.nn.sigmoid(gate_proj)
    gate_grad = (
        gated_grad * scan_out * sigmoid_gate * (1.0 + gate_proj * (1.0 - sigmoid_gate))
    ).astype(jnp.bfloat16)
    (
        inner_full,
        shared_part,
        step_full,
        conv_inner_grad,
        conv_shared_part,
        conv_inner_bias_grad,
        conv_shared_bias_part,
        step_bias_grad,
        decay_log_grad,
        skip_gain_grad,
    ) = pullback(scan_grad)
    shared_grad = lax.psum_scatter(shared_part, "tensor", scatter_dimension=1, tiled=True).astype(
        jnp.bfloat16
    )
    inner_grad = inner_full.astype(jnp.bfloat16)
    step_grad = step_full.astype(jnp.bfloat16)
    slice_width = shared_grad.shape[1]
    shared_cols = lax.dynamic_slice_in_dim(w_shared, column * slice_width, slice_width, 1)
    w_gate_grad = transpose_dot(normed, gate_grad)
    w_input_grad = transpose_dot(normed, inner_grad)
    w_step_grad = transpose_dot(normed, step_grad)
    shared_piece = transpose_dot(normed, shared_grad)
    w_shared_part = lax.dynamic_update_slice_in_dim(
        jnp.zeros(w_shared.shape, jnp.float32), shared_piece, column * slice_width, 1
    )
    normed_grad = (
        back_dot(gate_grad, w_gate)
        + back_dot(inner_grad, w_input)
        + back_dot(step_grad, w_step)
        + back_dot(shared_grad, shared_cols)
    )
    normed_full = lax.psum(normed_grad.astype(jnp.bfloat16), "tensor").astype(jnp.float32)
    weighted_in = normed_full * norm_gain[None, :]
    row_stat = jnp.sum(weighted_in * source, axis=1, keepdims=True)
    full_input_grad = (
        factor * weighted_in - source * factor * factor * factor * row_stat / model_width
    )
    hidden_grad = lax.dynamic_slice_in_dim(
        full_input_grad, column * piece_width, piece_width, 1
    ) + out_grad.astype(jnp.float32)
    gain_full = jnp.sum(normed_full * source * factor, axis=0)
    gain_piece = lax.dynamic_slice_in_dim(gain_full, column * piece_width, piece_width, 0)
    norm_gain_part = lax.dynamic_update_slice_in_dim(
        jnp.zeros((model_width,), jnp.float32), gain_piece, column * piece_width, 0
    )
    (
        w_gate_grad,
        w_input_grad,
        w_step_grad,
        conv_inner_grad,
        conv_inner_bias_grad,
        step_bias_grad,
        decay_log_grad,
        skip_gain_grad,
        gate_norm_gain_grad,
        w_output_grad,
    ) = lax.psum(
        (
            w_gate_grad,
            w_input_grad,
            w_step_grad,
            conv_inner_grad,
            conv_inner_bias_grad,
            step_bias_grad,
            decay_log_grad,
            skip_gain_grad,
            gate_norm_gain_grad,
            w_output_grad,
        ),
        "dp",
    )
    norm_gain_grad, w_shared_grad, conv_shared_grad, conv_shared_bias_grad = lax.psum(
        (norm_gain_part, w_shared_part, conv_shared_part, conv_shared_bias_part), ("dp", "tensor")
    )
    return (
        mixed_out,
        hidden_grad,
        norm_gain_grad,
        w_gate_grad,
        w_input_grad,
        w_shared_grad,
        w_step_grad,
        conv_inner_grad,
        conv_shared_grad,
        conv_inner_bias_grad,
        conv_shared_bias_grad,
        step_bias_grad,
        decay_log_grad,
        skip_gain_grad,
        gate_norm_gain_grad,
        w_output_grad,
    )


def solution(mesh):
    in_specs = (
        P("dp", "tensor"),
        P("dp", "tensor"),
        P(),
        P(),
        P(),
        P(),
        P(None, "tensor"),
        P(None, "tensor"),
        P(),
        P(None, "tensor"),
        P(None, "tensor"),
        P(),
        P("tensor"),
        P(),
        P("tensor"),
        P("tensor"),
        P("tensor"),
        P("tensor"),
        P("tensor", None),
    )
    out_specs = (
        P("dp", "tensor"),
        P("dp", "tensor"),
        P(),
        P(None, "tensor"),
        P(None, "tensor"),
        P(),
        P(None, "tensor"),
        P(None, "tensor"),
        P(),
        P("tensor"),
        P(),
        P("tensor"),
        P("tensor"),
        P("tensor"),
        P("tensor"),
        P("tensor", None),
    )
    return jax.shard_map(local, mesh=mesh, in_specs=in_specs, out_specs=out_specs, check_vma=False)
```

profile of v0, /device:TPU:0, one launch (start us, length us, event | category | flops | bytes accessed | tf_op | source)
XLA Modules:
  0.0 2037.3 jit_solution(13487780838274401223)
XLA Ops:
  19.2 160.0 %all-gather.3.cloned.1.call-done = bf16[3072,1536]{1,0:T(8,128)(2,1)} async-done(((bf16[3072,384]{1,0:T(8,128)(2,1)}), bf16[3072,1536]{1,0:T(8,128)(2,1)}) %all-gather.3.cloned.1.call-update) | async-done | bytes 9437200 | tf_op jit(solution)/shard_map/all_gather | solution.py:152
  278.6 19.3 fusion.90
  302.6 99.0 %while.34 = (s32[]{:T(128)}, f32[12,128,64]{2,1,0:T(8,128)S(1)}, f32[12,12,128,64]{3,2,1,0:T(8,128)}, f32[12,12,1,1]{1,3,2,0:T(1,128)}, f32[12,12]{1,0:T(8,128)}...) while((s32[]{:T(128)}, f32[12,128,64]{2,1,0:T(8,128)S(1)}, ...), condition=%wide.region_6.7_spmd.clone, body=%wide.region_5.6_spmd.clone.sunk | while | flops 589827 | bytes 3933975 | solution.py:82
  407.6 19.4 fusion.131
  430.8 49.4 %fusion.43 = f32[12,256,12,64]{1,3,2,0:T(8,128)} fusion(f32[12,12,64,256]{3,2,1,0:T(8,128)S(1)} %fusion.131, f32[12,256,12]{1,2,0:T(8,128)S(1)} %copy-done.18, f32[12,12,256]{2,1,0:T(8,128)S(1)} %copy.190, f32[12,256,256]{2,1,0:T(8,128)S(1)} %fusion.130, f32[12,12,256]{2,1,0:T(8,128)S(1)} %copy-done.13, pred[256,256]{1,0:T(8,128)(4,1)S(1)} %copy-done.41, ...), kind=kOutput, calls=%fused_computation.75 | convolution fusion | flops 7299661824 | bytes 31965184 | tf_op jit(solution)/shard_map/jvp(chts,cshp->cthp)/dot_general | solution.py:71
  480.1 19.4 copy.238
  499.5 19.0 reshape.284
  518.5 21.8 %multiply_reduce_fusion.10 = (f32[3072]{0:T(1024)S(1)}, f32[3072,768]{1,0:T(8,128)}, f32[3072,768]{1,0:T(8,128)}) fusion(f32[3072,768]{1,0:T(8,128)} %reshape.284, f32[3072,768]{1,0:T(8,128)} %get-tuple-element.434, f32[768]{0:T(1024)S(1)} %copy-done.53, bf16[3072,1536]{1,0:T(8,128)(2,1)} %multiply_convert_fusion, bf16[1536,768]{1,0:T(8,128)(2,1)S(1)} %copy-done), kind=kOutput, calls=%fused_computation.87 | convolution fusion | flops 7278425088 | bytes 49560576 | tf_op jit(solution)/shard_map/dot_general | solution.py:15
  540.3 15.5 psum.119
  556.0 17.5 multiply_reduce_fusion.3
  573.5 16.7 psum.120
  590.2 22.0 %multiply_reduce_fusion.4 = (f32[768]{0:T(1024)}, f32[3072,768]{1,0:T(8,128)}, bf16[3072,768]{1,0:T(8,128)(2,1)}) fusion(f32[3072,768]{1,0:T(8,128)} %get-tuple-element.434, f32[3072,768]{1,0:T(8,128)} %get-tuple-element.465, f32[3072]{0:T(1024)S(1)} %psum.120, f32[3072,768]{1,0:T(8,128)} %get-tuple-element.432, f32[3072,768]{1,0:T(8,128)} %get-tuple-element.466, ...), kind=kLoop, calls=%fused_computation.78 | loop fusion | flops 66059520 | bytes 61375488 | tf_op jit(solution)/shard_map/transpose(jvp())/reduce_sum | solution.py:121
  648.0 76.4 %fusion.12 = (f32[12,12,256]{2,1,0:T(8,128)}, f32[12,12,256]{2,1,0:T(8,128)}, f32[12,12,256]{2,1,0:T(8,128)}, f32[12,256,256]{2,1,0:T(8,128)S(1)}) fusion(f32[12,12,256]{2,1,0:T(8,128)S(1)} %copy.190, f32[12,256,256]{2,1,0:T(8,128)} %copy-done.15, f32[12,12,256]{2,1,0:T(8,128)S(1)} %copy-done.13, pred[256,256]{1,0:T(8,128)(4,1)S(1)} %copy-done.41, ...), kind=kOutput, calls=%fused_computation.30 | convolution fusion | flops 7388418048 | bytes 25968640 | tf_op jit(solution)/shard_map/transpose(jvp(chts,cshp->cthp))/dot_general | solution.py:71
  734.7 19.2 fusion.93
  758.8 92.7 %while.35 = (s32[]{:T(128)}, f32[12,128,64]{2,1,0:T(8,128)}, f32[12,12]{1,0:T(8,128)S(1)}, f32[12,12,128,64]{3,2,1,0:T(8,128)}, pred[12]{0:T(512)(128)(4,1)S(1)}...) while((s32[]{:T(128)}, f32[12,128,64]{2,1,0:T(8,128)}, ...), condition=%wide.region_14.15_spmd.clone, body=%wide.region_12.14_spmd.clone.sunk | while | flops 688120 | bytes 4719047 | solution.py:82
  851.5 20.7 %fusion.37 = f32[12,256,12,64]{1,3,2,0:T(8,128)} fusion(f32[12,256,128,1]{2,1,3,0:T(8,128)} %bitcast.207, f32[12,12,128,64]{3,2,1,0:T(8,128)} %get-tuple-element.217), kind=kOutput, calls=%fused_computation.67 | convolution fusion | flops 3623878656 | bytes 15728640 | tf_op jit(solution)/shard_map/transpose(jvp(csn,csh,cshp->chnp))/dot_general | solution.py:73
  887.5 43.0 %bitcast_add_fusion.2 = f32[12,256,12,64]{1,3,2,0:T(8,128)} fusion(f32[12,256,12,64]{1,3,2,0:T(8,128)} %fusion.37, f32[12,256,12]{1,2,0:T(8,128)} %get-tuple-element.454, f32[12,12,256]{2,1,0:T(8,128)} %copy-done.33, f32[12,256,256]{2,1,0:T(8,128)} %copy-done.15, f32[12,12,256]{2,1,0:T(8,128)} %copy-done.12, pred[256,256]{1,0:T(8,128)(4,1)S(1)} %copy-done.42, ...), kind=kOutput, calls=%fused_computation.64 | convolution fusion | flops 7299661824 | bytes 31965184 | tf_op jit(solution)/shard_map/transpose(jvp(chts,cshp->cthp))/dot_general | solution.py:71
  930.6 36.6 %bitcast_add_fusion.4 = f32[12,256,128]{2,1,0:T(8,128)} fusion(f32[12,256,128]{2,1,0:T(8,128)S(1)} %copy-done.7, f32[12,12,128,64]{3,2,1,0:T(8,128)S(1)} %bitcast.200, f32[12,256,12,64]{1,0,3,2:T(8,128)} %reshape.256, f32[12,256,12]{1,2,0:T(8,128)S(1)} %copy-done.20), kind=kOutput, calls=%fused_computation.157 | convolution fusion | flops 3626631168 | bytes 17448960 | tf_op jit(solution)/shard_map/transpose(jvp(ctn,cth,chnp->cthp))/dot_general | solution.py:85
  967.4 38.5 %bitcast_add_fusion.3 = f32[12,256,128]{2,1,0:T(8,128)} fusion(f32[12,256,128]{2,1,0:T(8,128)S(1)} %copy-done.6, f32[12,12,128,64]{3,2,1,0:T(8,128)} %get-tuple-element.217, f32[12,256,12]{1,2,0:T(8,128)S(1)} %copy-done.17, f32[12,256,12,64]{1,0,3,2:T(8,128)} %reshape.248), kind=kOutput, calls=%fused_computation.156 | convolution fusion | flops 3626631168 | bytes 17448960 | tf_op jit(solution)/shard_map/transpose(jvp(csn,csh,cshp->chnp))/dot_general | solution.py:73
  1009.4 29.8 %reduce-window.16 = f32[12,12,2,128]{3,1,2,0:T(8,128)S(1)} reduce-window(f32[12,12,2,128]{3,1,2,0:T(8,128)S(1)} %copy.211, f32[]{:T(128)} %constant.126.clone.1), window={size=1x1x1x128 pad=0_0x0_0x0_0x0_127}, to_apply=%region_19.20 | reduce-window | flops 4681728 | bytes 294916 | tf_op jit(solution)/shard_map/reduce-window.2
  1058.7 19.5 copy.239
  1078.2 19.1 reshape.285
  1097.3 24.8 %multiply_reduce_fusion.8 = (f32[768]{0:T(1024)S(1)}, f32[768]{0:T(1024)S(1)}, f32[768]{0:T(1024)S(1)}, f32[768]{0:T(1024)S(1)}, f32[768]{0:T(1024)S(1)}, /*index=5*/f32[3072,768]{1,0:T(8,128)S(1)}) fusion(f32[3072,768]{1,0:T(8,128)} %copy-done.4, f32[3072]{0:T(1024)S(1)} %copy-done.28, f32[3072]{0:T(1024)S(1)} %copy-done.30, f32[3072]{0:T(1024)S(1)} %copy-done.26, ...), kind=kLoop, calls=%fused_computation.82 | loop fusion | flops 54259968 | bytes 47241216 | tf_op jit(solution)/shard_map/transpose(jvp())/reduce_sum | solution.py:53
  1174.8 22.5 %add_convert_fusion = bf16[3072,1536]{1,0:T(8,128)(2,1)} fusion(f32[3072,1536]{1,0:T(8,128)} %fusion.114, f32[3072,1536]{1,0:T(8,128)} %fusion.132, f32[3072,1536]{1,0:T(8,128)} %fusion.133, bf16[1536,256]{1,0:T(8,128)(2,1)} %param.31, s32[]{:T(128)S(6)} %select_n.75, bf16[3072,64]{1,0:T(8,128)(2,1)S(1)} %copy.243), kind=kOutput, calls=%fused_computation.35 | convolution fusion | flops 622854144 | bytes 66846724 | tf_op jit(solution)/shard_map/dot_general | solution.py:25
  1237.8 16.6 fusion.52
  1284.2 24.6 %all-reduce.25 = (f32[4,768]{1,0:T(4,128)}, f32[768]{0:T(1024)}, f32[12]{0:T(128)}, f32[12]{0:T(128)}, f32[12]{0:T(128)}, /*index=5*/f32[768]{0:T(1024)}) all-reduce(f32[4,768]{1,0:T(4,128)S(1)} %pad_add_fusion, f32[768]{0:T(1024)S(1)} %get-tuple-element.372, ...), channel_id=1, replica_groups=mesh['dp'=8,'tensor'=4] {'dp'}, use_global_device_ids=true, to_apply=%region_35.36 | all-reduce | flops 4644 | bytes 37152 | tf_op jit(solution)/shard_map/psum | solution.py:262
  1308.8 211.6 %all-reduce.31.cloned.1.call-done = bf16[3072,1536]{1,0:T(8,128)(2,1)} async-done(((bf16[3072,1536]{1,0:T(8,128)(2,1)}), bf16[3072,1536]{1,0:T(8,128)(2,1)}) %all-reduce.31.cloned.1.call-update) | async-done | bytes 9437200 | tf_op jit(solution)/shard_map/psum | solution.py:237
  1520.4 21.2 %fusion.16 = (f32[1536]{0:T(1024)S(1)}, f32[3072]{0:T(1024)S(1)}, f32[3072,1536]{1,0:T(8,128)}, f32[3072,1536]{1,0:T(8,128)}) fusion(bf16[3072,1536]{1,0:T(8,128)(2,1)} %all-gather.3.cloned.1.call-done, bf16[3072,1536]{1,0:T(8,128)(2,1)} %all-reduce.31.cloned.1.call-done, f32[3072]{0:T(1024)S(1)} %copy-done.37, f32[1536]{0:T(1024)S(1)} %copy-done.56), kind=kLoop, calls=%fused_computation.34 | loop fusion | flops 42462720 | bytes 56659968 | tf_op jit(solution)/shard_map/reduce_sum | solution.py:246
  1541.7 43.8 %all-reduce.24 = (f32[1536]{0:T(1024)}, f32[4,256]{1,0:T(4,128)}, f32[256]{0:T(256)}) all-reduce(f32[1536]{0:T(1024)S(1)} %dynamic-slice_dynamic-update-slice_fusion, f32[4,256]{1,0:T(4,128)S(1)} %pad_add_fusion.1, f32[256]{0:T(256)S(1)} %copy-done.74), channel_id=1, replica_groups=mesh['dp'=8,'tensor'=4] {'dp','tensor'}, use_global_device_ids=true, to_apply=%region_26.27 | all-reduce | flops 2816 | bytes 22528 | tf_op jit(solution)/shard_map/psum | solution.py:277
  1592.6 91.3 %reduce-scatter.7.cloned.1.call-done = bf16[384,3072]{1,0:T(8,128)(2,1)} async-done(((bf16[1536,3072]{1,0:T(8,128)(2,1)}), bf16[384,3072]{1,0:T(8,128)(2,1)}) %reduce-scatter.7.cloned.1.call-update) | async-done | bytes 2359312
  1692.2 130.2 %all-reduce.33.cloned.1.call-done = f32[1536,256]{1,0:T(8,128)} async-done(((f32[1536,256]{1,0:T(8,128)}), f32[1536,256]{1,0:T(8,128)}) %all-reduce.33.cloned.1.call-update) | async-done | bytes 1572880 | tf_op jit(solution)/shard_map/psum | solution.py:277
  1822.4 196.0 %all-reduce.35.cloned.1.call-done = (f32[1536,768]{1,0:T(8,128)}, f32[1536,768]{1,0:T(8,128)}, f32[1536,12]{0,1:T(8,128)}, f32[768,1536]{1,0:T(8,128)}) async-done(((f32[1536,768]{1,0:T(8,128)}, f32[1536,768]{1,0:T(8,128)}, f32[1536,12]{0,1:T(8,128)}, f32[768,1536]{1,0:T(8,128)}), (f32[1536,768]{1,0:T(8,128)}, f32[1536,768]{1,0:T(8,128)}, f32[1536,12]{0,1:T(8,128)}, ...) | async-done | bytes 14229520 | tf_op jit(solution)/shard_map/psum | solution.py:262
  (506 shorter events, 555.5 us)
Async XLA Ops:
  7.2 511.3 %copy-start = (bf16[1536,768]{1,0:T(8,128)(2,1)S(1)}, bf16[1536,768]{1,0:T(8,128)(2,1)}, u32[]{:S(2)}) copy-start(bf16[1536,768]{1,0:T(8,128)(2,1)} %param.29) | copy-start | bytes 7077892
  7.2 177.6 %copy-start.55 = (f32[1536]{0:T(1024)S(1)}, f32[1536]{0:T(1024)}, u32[]{:S(2)}) copy-start(f32[1536]{0:T(1024)} %param.28) | copy-start | bytes 18436
  7.2 171.9 %all-gather.3.cloned.1.call-start = ((), (), s32[]{:S(2)}) async-start(), calls=%async_computation.2 | async-start | bytes 11796480 | tf_op jit(solution)/shard_map/all_gather | solution.py:152
  7.9 548.0 %all-gather.5.cloned.1.call-start = ((), (), s32[]{:S(2)}) async-start(), calls=%async_computation.3 | async-start | bytes 11796480 | tf_op jit(solution)/shard_map/all_gather | solution.py:153
  8.7 1164.6 %reduce-scatter.9.cloned.1.call-start = ((), (), s32[]{:S(2)}) async-start(), calls=%async_computation.7 | async-start | bytes 3932160
  11.7 173.0 %copy-start.38 = (f32[3072]{0:T(1024)}, f32[3072]{0:T(1024)S(1)}, u32[]{:S(2)}) copy-start(f32[3072]{0:T(1024)S(1)} %convert_reduce_fusion) | copy-start | bytes 36868
  12.4 234.3 %copy-start.25 = (f32[3072]{0:T(1024)}, f32[3072]{0:T(1024)S(1)}, u32[]{:S(2)}) copy-start(f32[3072]{0:T(1024)S(1)} %get-tuple-element.457) | copy-start | bytes 36868
  13.7 182.0 %copy-start.66 = (f32[12]{0:T(128)}, f32[12]{0:T(128)S(1)}, u32[]{:S(2)}) copy-start(f32[12]{0:T(128)S(1)} %exp.35) | copy-start | bytes 148
  19.2 227.6 %copy-start.45 = (f32[768]{0:T(1024)}, f32[768]{0:T(1024)S(1)}, u32[]{:S(2)}) copy-start(f32[768]{0:T(1024)S(1)} %get-tuple-element.378) | copy-start | bytes 9220
  402.6 245.3 %copy-start.33 = (f32[12,12,256]{2,1,0:T(8,128)}, f32[12,12,256]{2,1,0:T(8,128)S(1)}, u32[]{:S(2)}) copy-start(f32[12,12,256]{2,1,0:T(8,128)S(1)} %copy.190) | copy-start | bytes 442372
  648.0 76.4 %copy-start.2 = (f32[3072,128]{1,0:T(8,128)S(1)}, f32[3072,128]{1,0:T(8,128)}, u32[]{:S(2)}) copy-start(f32[3072,128]{1,0:T(8,128)} %get-tuple-element.448) | copy-start | bytes 4718596
  648.0 82.6 %copy-start.1 = (f32[3072,128]{1,0:T(8,128)S(1)}, f32[3072,128]{1,0:T(8,128)}, u32[]{:S(2)}) copy-start(f32[3072,128]{1,0:T(8,128)} %get-tuple-element.449) | copy-start | bytes 4718596
  872.3 58.3 %slice-start.3 = ((s8[9437184]{0:T(1024)(128)(4,1)}), s8[1048576]{0:T(1024)(128)(4,1)S(1)}, s32[]{:S(2)}) async-start(s8[9437184]{0:T(1024)(128)(4,1)} %bitcast.199), calls=%async_computation.12 | async-start | bytes 2097152
  887.5 43.0 %slice-start.4 = ((s8[9437184]{0:T(1024)(128)(4,1)}), s8[4194304]{0:T(1024)(128)(4,1)S(1)}, s32[]{:S(2)}) async-start(s8[9437184]{0:T(1024)(128)(4,1)} %bitcast.199), calls=%async_computation.13 | async-start | bytes 8388608
  887.5 43.0 %slice-start.5 = ((s8[9437184]{0:T(1024)(128)(4,1)}), s8[4194304]{0:T(1024)(128)(4,1)S(1)}, s32[]{:S(2)}) async-start(s8[9437184]{0:T(1024)(128)(4,1)} %bitcast.199), calls=%async_computation.14 | async-start | bytes 8388608
  887.5 43.0 %copy-start.7 = (f32[12,256,128]{2,1,0:T(8,128)S(1)}, f32[12,256,128]{2,1,0:T(8,128)}, u32[]{:S(2)}) copy-start(f32[12,256,128]{2,1,0:T(8,128)} %fusion.134) | copy-start | bytes 4718596
  887.5 43.0 %copy-start.20 = (f32[12,256,12]{1,2,0:T(8,128)S(1)}, f32[12,256,12]{1,2,0:T(8,128)}, u32[]{:S(2)}) copy-start(f32[12,256,12]{1,2,0:T(8,128)} %get-tuple-element.453) | copy-start | bytes 442372
  967.4 40.4 %copy-start.24 = (f32[12,256,12]{1,2,0:T(8,128)S(1)}, f32[12,256,12]{1,2,0:T(8,128)}, u32[]{:S(2)}) copy-start(f32[12,256,12]{1,2,0:T(8,128)} %fusion.44) | copy-start | bytes 442372
  967.4 72.9 %copy-start.26 = (f32[3072]{0:T(1024)S(1)}, f32[3072]{0:T(1024)}, u32[]{:S(2)}) copy-start(f32[3072]{0:T(1024)} %copy-done.25) | copy-start | bytes 36868
  1007.8 42.6 %copy-start.61 = (f32[1,256]{1,0:T(1,128)S(1)}, f32[1,256]{1,0:T(1,128)}, u32[]{:S(2)}) copy-start(f32[1,256]{1,0:T(1,128)} %get-tuple-element.461) | copy-start | bytes 3076
  1009.3 41.1 %copy-start.28 = (f32[3072]{0:T(1024)S(1)}, f32[3072]{0:T(1024)}, u32[]{:S(2)}) copy-start(f32[3072]{0:T(1024)} %get-tuple-element.458) | copy-start | bytes 36868
  1009.3 41.1 %copy-start.30 = (f32[3072]{0:T(1024)S(1)}, f32[3072]{0:T(1024)}, u32[]{:S(2)}) copy-start(f32[3072]{0:T(1024)} %get-tuple-element.459) | copy-start | bytes 36868
  1009.3 41.1 %copy-start.63 = (f32[1,256]{1,0:T(1,128)S(1)}, f32[1,256]{1,0:T(1,128)}, u32[]{:S(2)}) copy-start(f32[1,256]{1,0:T(1,128)} %get-tuple-element.462) | copy-start | bytes 3076
  1009.3 41.1 %copy-start.65 = (f32[1,256]{1,0:T(1,128)S(1)}, f32[1,256]{1,0:T(1,128)}, u32[]{:S(2)}) copy-start(f32[1,256]{1,0:T(1,128)} %get-tuple-element.463) | copy-start | bytes 3076
  1058.6 461.7 %all-reduce.31.cloned.1.call-start = ((), (), s32[]{:S(2)}) async-start(), calls=%async_computation.4 | async-start | bytes 18874368 | tf_op jit(solution)/shard_map/psum | solution.py:237
  1197.3 486.6 %reduce-scatter.7.cloned.1.call-start = ((), (), s32[]{:S(2)}) async-start(), calls=%async_computation.6 | async-start | bytes 11796480
  1224.4 598.1 %all-reduce.33.cloned.1.call-start = ((), (), s32[]{:S(2)}) async-start(), calls=%async_computation.5 | async-start | bytes 3145728 | tf_op jit(solution)/shard_map/psum | solution.py:277
  1264.3 754.1 %all-reduce.35.cloned.1.call-start = ((), (), s32[]{:S(2)}) async-start(), calls=%async_computation.8 | async-start | bytes 28508160 | tf_op jit(solution)/shard_map/psum | solution.py:262
  1283.3 237.1 %copy-start.37 = (f32[3072]{0:T(1024)S(1)}, f32[3072]{0:T(1024)}, u32[]{:S(2)}) copy-start(f32[3072]{0:T(1024)} %copy-done.36) | copy-start | bytes 36868
  1283.3 237.1 %copy-start.56 = (f32[1536]{0:T(1024)S(1)}, f32[1536]{0:T(1024)}, u32[]{:S(2)}) copy-start(f32[1536]{0:T(1024)} %param.28) | copy-start | bytes 18436
  1308.8 232.9 %copy-start.74 = (f32[256]{0:T(256)S(1)}, f32[256]{0:T(256)}, u32[]{:S(2)}) copy-start(f32[256]{0:T(256)} %get-tuple-element.377) | copy-start | bytes 3076
  1585.6 102.6 %copy-start.39 = (f32[3072]{0:T(1024)S(1)}, f32[3072]{0:T(1024)}, u32[]{:S(2)}) copy-start(f32[3072]{0:T(1024)} %copy-done.38) | copy-start | bytes 36868
  (77 other events, 1192.3 us)
Sparse Core Ops, SparseCore 0:
  9.6 169.4 all-gather.2
  180.7 164.9 all-gather.4
  1058.8 58.4 reduce-scatter.8
  1197.5 322.8 all-reduce.30
  1522.6 161.3 reduce-scatter.6
  1689.6 132.7 all-reduce.32
  1827.6 190.7 all-reduce.34
where the time goes:
time: 2050 us; the launch traced here: 2040 us
  waiting for transfers between devices  790 us (39%)
  matrix products  516 us (25%)
  other arithmetic  331 us (16%)
  local copies, waits for them, and re-layouts  282 us (14%)
  blocking collectives  101 us (5%)
    psum x1, waiting for transfers between devices, local(): lax.psum(normed_grad.astype(jnp.bfloat16), 'tensor').astype(jnp.float32)  212 us
    psum x1, waiting for transfers between devices, local(): lax.psum((w_gate_grad, w_input_grad, w_step_grad, conv_inner_grad, conv_i...  196 us
    dot_general x3, matrix products, state_space(): within = jnp.einsum('chts,cshp->cthp', mixing, values, precision=PRECISE)  169 us
    all_gather x1, waiting for transfers between devices, local(): lax.all_gather(hidden_in, 'tensor', axis=1, tiled=True)  160 us
    psum x1, waiting for transfers between devices, local(): lax.psum((norm_gain_part, w_shared_part, conv_shared_part, conv_shared_bi...  130 us
    unnamed x9, waiting for transfers between devices  92.8 us
    dot_general x3, matrix products, state_space(): jnp.einsum('csn,csh,cshp->chnp', inputs_b, to_end, values, precision=PREC...  78.5 us
    dot_general x3, matrix products, state_space(): jnp.einsum('ctn,cth,chnp->cthp', outputs_c, jnp.exp(cumulative), entering...  75.3 us
  transfers between devices with their start and end apart: 7, of which 5 were waited for; matrix products, arithmetic and copies ran while one was open for 30% of the time, Pallas kernels for 0%

commit v1 on v0

v1 whole, which is shorter than its diff:
```python
import functools

import jax
import jax.numpy as jnp
from jax import lax
from jax.experimental import pallas as pl
from jax.experimental.pallas import tpu as pltpu
from jax.sharding import PartitionSpec as P

F32 = jnp.float32
BF16 = jnp.bfloat16
PRECISE = lax.Precision.HIGHEST
EPSILON = 1e-05
LEN = 128
HALO = 16
WIDE = 256
VMEM = 52 * 1024 * 1024


def dot_nn(a, b):
    return jnp.dot(a, b, preferred_element_type=F32)


def dot_nt(a, b):
    return lax.dot_general(a, b, (((1,), (1,)), ((), ())), preferred_element_type=F32)


def dot_tn(a, b):
    return lax.dot_general(a, b, (((0,), (0,)), ((), ())), preferred_element_type=F32)


def sigmoid(v):
    return 1.0 / (1.0 + jnp.exp(-v))


def split_pair(v):
    lane = lax.broadcasted_iota(jnp.int32, v.shape, 1)
    high = v.astype(BF16).astype(F32)
    return jnp.where(lane < 64, high, v - high).astype(BF16)


def split_triple(v):
    lane = lax.broadcasted_iota(jnp.int32, v.shape, 1)
    high = v.astype(BF16).astype(F32)
    rest = v - high
    middle = rest.astype(BF16).astype(F32)
    return jnp.where(lane < 64, high, jnp.where(lane < 128, middle, rest - middle)).astype(BF16)


def head_sums(v, select):
    high = v.astype(BF16)
    low = (v - high.astype(F32)).astype(BF16)
    return dot_nn(high, select) + dot_nn(low, select)


def halves(v):
    high = v.astype(BF16)
    return high, (v - high.astype(F32)).astype(BF16)


def finer(dot, a, b):
    a_high, a_low = halves(a)
    b_high, b_low = halves(b)
    return dot(a_high, b_high) + (dot(a_high, b_low) + dot(a_low, b_high))


def fold(v):
    total = v[:, :128]
    for i in range(1, v.shape[1] // 128):
        total = total + v[:, i * 128 : (i + 1) * 128]
    return total


def chunk(i, width):
    return pl.ds(pl.multiple_of(i * width, width), width)


def conv_states_kernel(
    keep_ref, ip_ref, halo_ref, taps_ref, bias_ref, b_ref, coef_ref, dec_ref, spread_ref,
    u_ref, local_ref, out_ref, ext_ref, state_ref,
):
    c = pl.program_id(0)
    keep = keep_ref[c].astype(F32)

    @pl.when(c == 0)
    def _():
        state_ref[...] = jnp.zeros_like(state_ref)
        ext_ref[0:8, :] = halo_ref[8:16, :] * keep

    @pl.when(c > 0)
    def _():
        ext_ref[0:8, :] = ext_ref[LEN : LEN + 8, :] * keep

    ext_ref[8 : LEN + 8, :] = ip_ref[...]
    coef = split_pair(coef_ref[...])
    b_map, b_low = halves(b_ref[...])

    def step(i, carry):
        at = chunk(i, WIDE)
        u = bias_ref[:, at] + taps_ref[3:4, at] * ext_ref[8 : 8 + LEN, at]
        for lag in range(1, 4):
            u = u + taps_ref[3 - lag : 4 - lag, at] * ext_ref[8 - lag : 8 - lag + LEN, at]
        u_ref[:, at] = u
        w = u * sigmoid(u) * dot_nn(coef, spread_ref[:, at])
        state = state_ref[:, at] * keep
        local_ref[0, :, at] = state.astype(BF16)
        state_ref[:, at] = dec_ref[0, :, at] * state + (dot_tn(b_map, w.astype(BF16))+dot_tn(b_low, w.astype(BF16)))
        return carry

    lax.fori_loop(0, u_ref.shape[1] // WIDE, step, 0)

    @pl.when(c == pl.num_programs(0) - 1)
    def _():
        out_ref[...] = state_ref[...]


def within_kernel(
    u_ref, cum_ref, cum_t_ref, step_ref, b_ref, c_ref, columns_ref, spread_ref, y_ref
):
    scores = finer(dot_nt, c_ref[...], b_ref[...])
    row = lax.broadcasted_iota(jnp.int32, (LEN, LEN), 0)
    col = lax.broadcasted_iota(jnp.int32, (LEN, LEN), 1)
    scores = jnp.where(row >= col, scores, 0.0)
    scores = jnp.concatenate([scores, scores], axis=1)
    cum = split_triple(cum_ref[...])
    steps = split_pair(step_ref[...])
    first = col < 64

    def pair(p, carry):
        at = chunk(p, 128)
        left = dot_nn(cum, columns_ref[:, chunk(p, 256)])
        right = jnp.concatenate(
            [cum_t_ref[pl.ds(2 * p, 1), :], cum_t_ref[pl.ds(2 * p + 1, 1), :]], axis=1
        )
        mixing = (jnp.exp(jnp.minimum(left - right, 0.0)) * scores).astype(BF16)
        u = u_ref[:, at]
        v = u * sigmoid(u) * dot_nn(steps, spread_ref[:, at])
        stacked = jnp.concatenate(
            [jnp.where(first, v, 0.0).astype(BF16), jnp.where(first, 0.0, v).astype(BF16)], axis=0
        )
        y_ref[:, at] = dot_nn(mixing, stacked)
        return carry

    lax.fori_loop(0, u_ref.shape[1] // 128, pair, 0, unroll=2)


def gate_kernel(
    keep_ref, y_ref, u_ref, gate_ref, ng_ref, local_ref, enter_ref, pref_ref, c_ref, grow_ref,
    skip_ref, gain_ref, dec_ref, spread_ref, select_ref,
    ny_ref, dy_ref, gg_ref, q_ref, dc_ref, gain_grad_ref, skip_grad_ref, out_ref,
    scan_ref, carried_ref, state_ref,
):
    g = pl.program_id(0)
    c = pl.num_programs(0) - 1 - g
    width = y_ref.shape[1]
    keep = keep_ref[c].astype(F32)

    @pl.when(g == 0)
    def _():
        state_ref[...] = jnp.zeros_like(state_ref)
        gain_grad_ref[...] = jnp.zeros_like(gain_grad_ref)
        skip_grad_ref[...] = jnp.zeros_like(skip_grad_ref)

    c_map, c_low = halves(c_ref[...])
    grow = split_pair(grow_ref[...])

    def forward(i, sums):
        squares, stat = sums
        at = chunk(i, WIDE)
        carried = (
            local_ref[0, :, at].astype(F32) + pref_ref[0, :, at] * enter_ref[:, at].astype(F32)
        ).astype(BF16)
        carried_ref[:, at] = carried
        scanned = y_ref[:, at] + dot_nn(grow, spread_ref[:, at]) * (dot_nn(c_map, carried)+dot_nn(c_low,carried))
        scan_ref[:, at] = scanned
        u = u_ref[:, at]
        y = scanned + skip_ref[:, at] * (u * sigmoid(u))
        gate = gate_ref[:, at]
        gated = y * (gate * sigmoid(gate))
        squares = squares + fold(gated * gated)
        stat = stat + fold(ng_ref[:, at] * gain_ref[:, at] * gated)
        return (squares, stat)

    nothing = jnp.zeros((LEN, 128), F32)
    squares, stat = lax.fori_loop(0, width // WIDE, forward, (nothing, nothing))
    scale = lax.rsqrt(jnp.sum(squares, axis=1, keepdims=True) / width + EPSILON)
    back = scale * scale * scale * (jnp.sum(stat, axis=1, keepdims=True) / width)

    def backward(i, sums):
        q, dc = sums
        at = chunk(i, WIDE)
        scanned = scan_ref[:, at]
        u = u_ref[:, at]
        x = u * sigmoid(u)
        y = scanned + skip_ref[:, at] * x
        gate = gate_ref[:, at]
        open_ = sigmoid(gate)
        act = gate * open_
        gated = y * act
        scaled = gated * scale
        ng = ng_ref[:, at]
        gain = gain_ref[:, at]
        ny_ref[:, at] = (scaled * gain).astype(BF16)
        gain_grad_ref[:, at] += jnp.sum(ng * scaled, axis=0, keepdims=True)
        gated_grad = scale * (ng * gain) - gated * back
        gg_ref[:, at] = (gated_grad * y * open_ * (1.0 + gate * (1.0 - open_))).astype(BF16)
        dy_low = (gated_grad * act).astype(BF16)
        dy_ref[:, at] = dy_low
        dy = dy_low.astype(F32)
        skip_grad_ref[:, at] += jnp.sum(dy * x, axis=0, keepdims=True)
        q = q + head_sums(dy * scanned, select_ref[chunk(i, WIDE), :])
        z = (dot_nn(grow, spread_ref[:, at]) * dy).astype(BF16)
        dc = dc + dot_nt(z, carried_ref[:, at])
        state_ref[:, at] = keep * (dec_ref[0, :, at] * state_ref[:, at] + (dot_tn(c_map, z)+dot_tn(c_low,z)))
        return (q, dc)

    q, dc = lax.fori_loop(0, width // WIDE, backward, (nothing, nothing))
    q_ref[...] = q
    dc_ref[...] = dc

    @pl.when(c == 0)
    def _():
        out_ref[...] = state_ref[...]


def within_back_kernel(
    u_ref, dy_ref, cum_ref, cum_t_ref, step_ref, b_ref, c_ref, columns_ref, spread_ref,
    dv_ref, db_ref, dc_ref,
):
    scores = finer(dot_nt, b_ref[...], c_ref[...])
    row = lax.broadcasted_iota(jnp.int32, (LEN, LEN), 0)
    col = lax.broadcasted_iota(jnp.int32, (LEN, LEN), 1)
    scores = jnp.where(row <= col, scores, 0.0)
    scores = jnp.concatenate([scores, scores], axis=1)
    cum = split_triple(cum_ref[...])
    steps = split_pair(step_ref[...])
    first = col < 64

    def pair(p, total):
        at = chunk(p, 128)
        left = dot_nn(cum, columns_ref[:, chunk(p, 256)])
        right = jnp.concatenate(
            [cum_t_ref[pl.ds(2 * p, 1), :], cum_t_ref[pl.ds(2 * p + 1, 1), :]], axis=1
        )
        decay = jnp.exp(jnp.minimum(right - left, 0.0))
        mixing = (decay * scores).astype(BF16)
        dy_low = dy_ref[:, at]
        dy = dy_low.astype(F32)
        dy_stack = jnp.concatenate(
            [jnp.where(first, dy, 0.0).astype(BF16), jnp.where(first, 0.0, dy).astype(BF16)], axis=0
        )
        dv_ref[:, at] = dot_nn(mixing, dy_stack)
        u = u_ref[:, at]
        v = u * sigmoid(u) * dot_nn(steps, spread_ref[:, at])
        v_stack = jnp.concatenate(
            [jnp.where(first, v, 0.0).astype(BF16), jnp.where(first, 0.0, v).astype(BF16)], axis=0
        )
        dw = dot_nt(v_stack, dy_low)
        return total + decay[:, :LEN] * dw[:LEN] + decay[:, LEN:] * dw[LEN:]

    total = lax.fori_loop(
        0, u_ref.shape[1] // 128, pair, jnp.zeros((LEN, LEN), F32), unroll=2
    )
    total = jnp.where(row <= col, total, 0.0)
    db_ref[...] = finer(dot_nn, total, c_ref[...])
    dc_ref[...] = finer(dot_tn, total, b_ref[...])


def across_back_kernel(
    keep_ref, u_ref, dy_ref, dv_ref, ip_ref, halo_ref, local_ref, enter_ref, pref_ref, leave_ref,
    b_ref, c_ref, grow_ref, fall_ref, step_ref, skip_ref, dec_ref, taps_ref, spread_ref, select_ref,
    ig_ref, db_ref, q_ref, r_ref, end_ref, taps_grad_ref, bias_grad_ref, head_ref,
    state_ref, ext_ref,
):
    g = pl.program_id(0)
    c = pl.num_programs(0) - 1 - g
    width = u_ref.shape[1]
    keep = keep_ref[c].astype(F32)

    @pl.when(g == 0)
    def _():
        state_ref[...] = leave_ref[...].astype(F32)
        taps_grad_ref[...] = jnp.zeros_like(taps_grad_ref)
        bias_grad_ref[...] = jnp.zeros_like(bias_grad_ref)
        ext_ref[LEN : LEN + 8, :] = jnp.zeros((8, width), F32)

    @pl.when(g > 0)
    def _():
        ext_ref[LEN : LEN + 8, :] = ext_ref[0:8, :] * keep_ref[c + 1].astype(F32)

    b_map, b_low = halves(b_ref[...])
    c_map, c_low = halves(c_ref[...])
    grow = split_pair(grow_ref[...])
    fall = split_pair(fall_ref[...])
    steps = split_pair(step_ref[...])

    def step(i, sums):
        db, q, r = sums
        at = chunk(i, WIDE)
        spread = spread_ref[:, at]
        state = state_ref[:, at]
        state_low = state.astype(BF16)
        falling = dot_nn(fall, spread)
        across = falling * (dot_nn(b_map, state_low)+dot_nn(b_low, state_low))
        dv = dv_ref[:, at] + across
        u = u_ref[:, at]
        open_ = sigmoid(u)
        x = u * open_
        delta = dot_nn(steps, spread)
        v = x * delta
        v_low = v.astype(BF16).astype(F32)
        dy = dy_ref[:, at].astype(F32)
        dx = delta * dv + skip_ref[:, at] * dy
        ext_ref[0:LEN, at] = dx * (open_ * (1.0 + u * (1.0 - open_)))
        select = select_ref[chunk(i, WIDE), :]
        q = q + head_sums(v_low * dv, select)
        r = r + head_sums(x * dv, select)
        carried = (
            local_ref[0, :, at].astype(F32) + pref_ref[0, :, at] * enter_ref[:, at].astype(F32)
        ).astype(BF16)
        decay = dec_ref[0, :, at]
        end_ref[0, :, at] = jnp.sum(v_low * across, axis=0, keepdims=True) + decay * jnp.sum(
            state * carried.astype(F32), axis=0, keepdims=True
        )
        db = db + dot_nt((falling * v).astype(BF16), state_low)
        z = (dot_nn(grow, spread) * dy).astype(BF16)
        state_ref[:, at] = keep * (decay * state + (dot_tn(c_map, z)+dot_tn(c_low,z)))
        return (db, q, r)

    nothing = jnp.zeros((LEN, 128), F32)
    db, q, r = lax.fori_loop(0, width // WIDE, step, (nothing, nothing, nothing))
    db_ref[...] = db
    q_ref[...] = q
    r_ref[...] = r

    def conv(i, carry):
        at = chunk(i, WIDE)
        ip = ip_ref[:, at]
        du = ext_ref[0:LEN, at]
        bias_grad_ref[:, at] += jnp.sum(du, axis=0, keepdims=True)
        total = taps_ref[3:4, at] * du
        taps_grad_ref[3:4, at] += jnp.sum(ip * du, axis=0, keepdims=True)
        for lag in range(1, 4):
            later = ext_ref[lag : lag + LEN, at]
            total = total + taps_ref[3 - lag : 4 - lag, at] * later
            taps_grad_ref[3 - lag : 4 - lag, at] += jnp.sum(ip * later, axis=0, keepdims=True)
        ig_ref[:, at] = total.astype(BF16)
        return carry

    lax.fori_loop(0, width // WIDE, conv, 0)

    @pl.when(c == 0)
    def _():
        head_ref[...] = ext_ref[0:8, :] * keep
        for lag in range(1, 4):
            part = keep * ext_ref[0:lag, :] * halo_ref[HALO - lag : HALO, :]
            taps_grad_ref[3 - lag : 4 - lag, :] += jnp.sum(part, axis=0, keepdims=True)


def place_kernel(copies, count, where_ref, *refs):
    pieces, out_ref = refs[:count], refs[count]
    stages, sems = refs[count + 1 : -1], refs[-1]
    loads = []
    for i, piece in enumerate(pieces):
        for t in range(piece.shape[0]):
            load = pltpu.make_async_copy(piece.at[t], stages[i].at[t], sems.at[0, i, t])
            load.start()
            loads.append((i, t, load))
    stores = []
    for i, t, load in loads:
        load.wait()
        rows, cols = pieces[i].shape[1:]
        row_slot, col_slot = copies[i][t]
        row = pl.multiple_of(where_ref[row_slot], 16)
        if col_slot is None:
            target = out_ref.at[pl.ds(row, rows)]
        else:
            col = pl.multiple_of(where_ref[col_slot], 128)
            target = out_ref.at[pl.ds(row, rows), pl.ds(col, cols)]
        store = pltpu.make_async_copy(stages[i].at[t], target, sems.at[1, i, t])
        store.start()
        stores.append(store)
    for store in stores:
        store.wait()


def place(pieces, rows_of, cols_of, shape):
    slots, copies = [], []
    whole = pieces[0].shape[2] == shape[1]
    for i, piece in enumerate(pieces):
        row = []
        for t in range(piece.shape[0]):
            slots.append(jnp.asarray(rows_of[i][t], jnp.int32))
            row_slot = len(slots) - 1
            col_slot = None
            if not whole:
                slots.append(jnp.asarray(cols_of[i][t], jnp.int32))
                col_slot = len(slots) - 1
            row.append((row_slot, col_slot))
        copies.append(row)
    anywhere = pl.BlockSpec(memory_space=pl.ANY)
    nbytes = 2 * shape[0] * shape[1] * 2
    return pl.pallas_call(
        functools.partial(place_kernel, copies, len(pieces)),
        in_specs=[pl.BlockSpec(memory_space=pltpu.SMEM)] + [anywhere] * len(pieces),
        out_specs=anywhere,
        out_shape=jax.ShapeDtypeStruct(shape, pieces[0].dtype),
        scratch_shapes=[pltpu.VMEM(piece.shape, piece.dtype) for piece in pieces]
        + [pltpu.SemaphoreType.DMA((2, len(pieces), pieces[0].shape[0]))],
        compiler_params=pltpu.CompilerParams(vmem_limit_bytes=VMEM),
        cost_estimate=pl.CostEstimate(flops=0, bytes_accessed=nbytes, transcendentals=0),
        name="place",
    )(jnp.stack(slots), *pieces)


def norm_kernel(rot_ref, gain_ref, *refs):
    pieces, (hid_ref, normed_ref) = refs[:-2], refs[-2:]
    width = pieces[0].shape[1]
    squares = jnp.zeros((pieces[0].shape[0], 128), F32)
    for piece in pieces:
        v = piece[...].astype(F32)
        squares = squares + fold(v * v)
    mean = jnp.sum(squares, axis=1, keepdims=True) / (width * len(pieces))
    factor = lax.rsqrt(mean + EPSILON)
    for d, piece in enumerate(pieces):
        at = pl.ds(pl.multiple_of(rot_ref[d] * width, 128), width)
        v = piece[...]
        hid_ref[:, at] = v
        normed_ref[:, at] = (v.astype(F32) * factor * gain_ref[:, at]).astype(BF16)


def join_kernel(rot_ref, live_ref, *refs):
    pieces, out_ref = refs[:-1], refs[-1]
    width = pieces[0].shape[1]
    for d, piece in enumerate(pieces):
        at = pl.ds(pl.multiple_of(rot_ref[d] * width, 128), width)
        out_ref[:, at] = (piece[...].astype(F32) * live_ref[...]).astype(BF16)


def land_kernel(rot_ref, base_ref, live_ref, *refs):
    pieces, out_ref = refs[:-1], refs[-1]
    for d, piece in enumerate(pieces):

        @pl.when(pl.program_id(0) == d)
        def _(piece=piece):
            total = base_ref[...].astype(F32) + live_ref[...] * piece[...].astype(F32)
            out_ref[...] = total.astype(out_ref.dtype)


def swap(v, bit, count):
    return lax.ppermute(v, "dp", [(i, i ^ (1 << bit)) for i in range(count)])


def rotate(v, by, count):
    return lax.ppermute(v, "tensor", [(i, (i + by) % count) for i in range(count)])


def in_order(pieces, column):
    return jnp.roll(jnp.stack([pieces[0]] + pieces[:0:-1]), column, axis=0)


def gather_pieces(v, count):
    bits = count.bit_length() - 1
    if bits == 3:
        near, far = swap(v, 1, count), swap(v, 2, count)
        half = v.shape[1] // 2
        first = swap(near[:, :half], 2, count)
        second = swap(far[:, half:], 1, count)
        mine = [(v, 0, 0), (near, 2, 0), (far, 4, 0), (first, 6, 0), (second, 6, half)]
    else:
        mine = [(v, 0, 0)]
        for bit in range(1, bits):
            mine += [(swap(a, bit, count), m ^ (1 << bit), o) for a, m, o in mine]
    return mine + [(swap(a, 0, count), m ^ 1, o) for a, m, o in mine]


def reduce_core(keep, received):
    return keep + received.astype(F32)


def scatter_rows(total, count, index):
    bits = count.bit_length() - 1
    q = index >> 1
    def run(v, order):
        left = list(range(1, bits))
        for bit in order:
            place_of = left.index(bit)
            low = 1 << place_of
            shaped = v.reshape((v.shape[0] // (2 * low), 2, low) + v.shape[1:])
            mine = (q >> (bit - 1)) & 1
            sent = lax.dynamic_index_in_dim(shaped, 1 - mine, 1, keepdims=False).astype(BF16)
            kept = lax.dynamic_index_in_dim(shaped, mine, 1, keepdims=False).astype(F32)
            v = (kept + swap(sent, bit, count).astype(F32)).reshape(
                (v.shape[0] // 2,) + v.shape[1:]
            )
            left.remove(bit)
        return v[0]

    order = list(range(1, bits))
    half = total.shape[2] // 2
    half = half - half % 128
    return jnp.concatenate(
        [run(total[:, :, :half], order), run(total[:, :, half:], order[::-1])], axis=1
    )


def pair_lanes(v):
    wide = jnp.pad(v, ((0, 0), (0, 64 - v.shape[1])))
    return jnp.concatenate([wide, wide], axis=1)


def local(
    dp_count, tensor_count,
    hidden_in, out_grad, seq_lengths, seq_device, seq_offset, norm_gain, w_gate, w_input, w_shared,
    w_step, conv_inner, conv_shared, conv_inner_bias, conv_shared_bias, step_bias, decay_log,
    skip_gain, gate_norm_gain, w_output,
):
    parts = tensor_count
    dp = lax.axis_index("dp")
    column = lax.axis_index("tensor")
    core, q = dp & 1, dp >> 1
    rows_dev, piece = hidden_in.shape
    rows = rows_dev // parts
    blocks = rows // LEN
    model = norm_gain.shape[0]
    shard = w_input.shape[1]
    inner = shard * parts
    heads_shard = w_step.shape[1]
    heads = heads_shard * parts
    width = inner // heads
    nstate = w_shared.shape[1] // 2
    groups = dp_count // 2

    aligned = piece % 128 == 0
    turn = jnp.stack([(column - d) % parts for d in range(parts)]).astype(jnp.int32)

    def send_rows(v, halo):
        pieces = []
        for d in range(parts):
            start = (column + d) % parts * rows
            mine = lax.dynamic_slice_in_dim(v, start, rows, 0)
            if halo:
                before = lax.dynamic_slice_in_dim(v, jnp.maximum(start - HALO, 0), HALO, 0)
                mine = jnp.concatenate([mine, before], axis=0)
            pieces.append(rotate(mine, d, parts) if d else mine)
        return pieces

    def send_back(v):
        pieces = []
        for d in range(parts):
            mine = lax.dynamic_slice_in_dim(v, (column + d) % parts * piece, piece, 1)
            pieces.append(rotate(mine, d, parts) if d else mine)
        return pieces

    def land(pieces, base, live_rows, dtype):
        if not aligned:
            total = in_order(pieces, column).reshape(rows_dev, piece).astype(F32)
            return (base.astype(F32) + live_rows * total).astype(dtype)
        return pl.pallas_call(
            land_kernel,
            grid_spec=pltpu.PrefetchScalarGridSpec(
                num_scalar_prefetch=1,
                grid=(parts,),
                in_specs=[
                    pl.BlockSpec((rows, piece), lambda d, rot: (rot[d], 0)),
                    pl.BlockSpec((rows, 1), lambda d, rot: (rot[d], 0)),
                ]
                + [pl.BlockSpec((rows, piece), lambda d, rot: (0, 0))] * parts,
                out_specs=pl.BlockSpec((rows, piece), lambda d, rot: (rot[d], 0)),
            ),
            out_shape=jax.ShapeDtypeStruct((rows_dev, piece), dtype),
            compiler_params=pltpu.CompilerParams(vmem_limit_bytes=VMEM),
            cost_estimate=pl.CostEstimate(
                flops=0, bytes_accessed=rows_dev * piece * 10, transcendentals=0
            ),
            name="land",
        )(turn, base, live_rows, *pieces)

    def row_block(size):
        return max(n for n in range(16, 129, 16) if size % n == 0)

    def join(kernel, pieces, extra, extra_rows, outs):
        size = pieces[0].shape[0]
        block = row_block(size)
        extra_spec = (
            pl.BlockSpec((block, 1), lambda g, rot: (g, 0))
            if extra_rows
            else pl.BlockSpec(extra.shape, lambda g, rot: (0, 0))
        )
        wide = pl.BlockSpec((block, model), lambda g, rot: (g, 0))
        return pl.pallas_call(
            kernel,
            grid_spec=pltpu.PrefetchScalarGridSpec(
                num_scalar_prefetch=1,
                grid=(size // block,),
                in_specs=[extra_spec]
                + [pl.BlockSpec((block, piece), lambda g, rot: (g, 0))] * parts,
                out_specs=[wide] * outs,
            ),
            out_shape=[jax.ShapeDtypeStruct((size, model), BF16)] * outs,
            compiler_params=pltpu.CompilerParams(vmem_limit_bytes=VMEM),
            cost_estimate=pl.CostEstimate(
                flops=0, bytes_accessed=size * model * 2 * (1 + outs), transcendentals=0
            ),
            name="join",
        )(turn, extra, *pieces)

    def join_plain(pieces):
        ordered = in_order(pieces, column)
        return jnp.concatenate([ordered[t] for t in range(parts)], axis=1)

    k_rows = model // dp_count
    place_dp = core * (model // 2) + q * k_rows

    def spread_out(v):
        return jnp.stack([v] + [rotate(v, d, parts) for d in range(1, parts)])

    def slices_of(index):
        other_core, other_q = index & 1, index >> 1
        return other_core, other_q

    def gather_columns(w):
        mine = lax.dynamic_slice_in_dim(w, place_dp, k_rows, 0)
        pieces = gather_pieces(spread_out(mine), dp_count)
        rows_of, cols_of = [], []
        for _, mask, offset in pieces:
            c2, q2 = slices_of(dp ^ mask)
            rows_of.append([c2 * (model // 2) + q2 * k_rows + offset] * parts)
            cols_of.append([turn[d] * shard for d in range(parts)])
        return place([a for a, _, _ in pieces], rows_of, cols_of, (model, inner))

    out_rows = shard // dp_count

    def gather_output(w):
        if out_rows % 16:
            return lax.all_gather(w, "tensor", axis=0, tiled=True)
        mine = lax.dynamic_slice_in_dim(w, core * (shard // 2) + q * out_rows, out_rows, 0)
        pieces = gather_pieces(spread_out(mine), dp_count)
        rows_of = []
        for _, mask, offset in pieces:
            c2, q2 = slices_of(dp ^ mask)
            start = c2 * (shard // 2) + q2 * out_rows + offset
            rows_of.append([turn[d] * shard + start for d in range(parts)])
        return place([a for a, _, _ in pieces], rows_of, None, (inner, model))

    hid_pieces = send_rows(hidden_in, True)
    w_in = gather_columns(w_input)

    small = jnp.concatenate(
        [
            conv_inner.reshape(-1),
            conv_inner_bias,
            gate_norm_gain,
            step_bias,
            decay_log,
            skip_gain,
            w_step.astype(F32).reshape(-1),
        ]
    )
    small = in_order([small] + [rotate(small, d, parts) for d in range(1, parts)], column)
    bounds = [0]
    for size in (4 * shard, shard, shard, heads_shard, heads_shard, heads_shard, model * heads_shard):
        bounds.append(bounds[-1] + size)
    take = lambda i: small[:, bounds[i] : bounds[i + 1]]
    taps = jnp.swapaxes(take(0).reshape(parts, 4, shard), 0, 1).reshape(4, inner)
    inner_bias = take(1).reshape(1, inner)
    gain_out = take(2).reshape(1, inner)
    steps_bias = take(3).reshape(1, heads)
    logs = take(4).reshape(1, heads)
    skips = take(5).reshape(1, heads)
    w_steps = (
        jnp.swapaxes(take(6).reshape(parts, model, heads_shard), 0, 1)
        .reshape(model, heads)
        .astype(BF16)
    )
    skip_wide = jnp.repeat(skips, width, axis=1)

    block_start = column * rows + jnp.arange(blocks + 1, dtype=jnp.int32) * LEN
    inside = (
        (seq_device[None, :] == dp)
        & (block_start[:, None] >= seq_offset[None, :])
        & (block_start[:, None] < seq_offset[None, :] + seq_lengths[None, :])
    )
    offset = jnp.sum(jnp.where(inside, block_start[:, None] - seq_offset[None, :], 0), axis=1)
    keep = (offset > 0).astype(jnp.int32)
    keep_f = keep.astype(F32)
    live_blocks = jnp.sum(inside.astype(F32), axis=1)[:blocks]
    live = jnp.repeat(live_blocks, LEN)[:, None]
    dev_start = jnp.arange(rows_dev // LEN, dtype=jnp.int32) * LEN
    dev_inside = (
        (seq_device[None, :] == dp)
        & (dev_start[:, None] >= seq_offset[None, :])
        & (dev_start[:, None] < seq_offset[None, :] + seq_lengths[None, :])
    )
    live_dev = jnp.repeat(jnp.sum(dev_inside.astype(F32), axis=1), LEN)[:, None]

    lane_head = jnp.arange(inner, dtype=jnp.int32) // width
    half_index = jnp.arange(128, dtype=jnp.int32) % 64
    spread = (half_index[:, None] == lane_head[None, :]).astype(BF16)
    select = (lane_head[:, None] == jnp.arange(128, dtype=jnp.int32)[None, :]).astype(BF16)
    columns = (
        (jnp.arange(192, dtype=jnp.int32) % 64)[:, None]
        == (jnp.arange(heads * LEN, dtype=jnp.int32) // LEN)[None, :]
    ).astype(BF16)

    if aligned:
        hid, normed_all = join(norm_kernel, hid_pieces, norm_gain[None, :], False, 2)
    else:
        hid = join_plain(hid_pieces)
        wide_in = hid.astype(F32)
        mean = jnp.mean(wide_in * wide_in, axis=1, keepdims=True)
        normed_all = (wide_in * lax.rsqrt(mean + EPSILON) * norm_gain[None, :]).astype(BF16)
    normed = normed_all[:rows]
    w_misc = jnp.concatenate(
        [w_shared, w_steps, jnp.zeros((model, 128 - heads), BF16)], axis=1
    )
    misc = dot_nn(normed_all, w_misc)
    inner_proj = dot_nn(normed_all, w_in)

    shared_all = misc[:, : 2 * nstate]
    shared_ext = jnp.concatenate([shared_all[rows + 8 :], shared_all[:rows]], axis=0)
    row_in_block = jnp.arange(rows + 8, dtype=jnp.int32) % LEN
    starts = jnp.repeat(1.0 - keep_f, LEN)[: rows + 8]

    def allowed(lag):
        return (1.0 - starts * (row_in_block < lag).astype(F32))[:, None]

    shared_u = conv_shared_bias[None, :] + conv_shared[3][None, :] * shared_ext[8:]
    for lag in range(1, 4):
        shared_u = shared_u + conv_shared[3 - lag][None, :] * (
            shared_ext[8 - lag : 8 - lag + rows] * allowed(lag)[:rows]
        )
    shared_open = jax.nn.sigmoid(shared_u)
    shared_conv = shared_u * shared_open
    b_map, c_map = shared_conv[:, :nstate], shared_conv[:, nstate:]

    raw = misc[:rows, 2 * nstate : 2 * nstate + heads] + steps_bias
    delta = jax.nn.softplus(raw)
    rates = jnp.exp(logs)
    decays = -delta * rates
    triangle = (jnp.arange(LEN)[:, None] >= jnp.arange(LEN)[None, :]).astype(F32)
    cum = jnp.einsum(
        "ts,csh->cth", triangle, decays.reshape(blocks, LEN, heads), precision=PRECISE
    )
    last = cum[:, -1, :]
    fall = jnp.exp(last[:, None, :] - cum).reshape(rows, heads)
    dec = jnp.exp(last)
    cum = cum.reshape(rows, heads)
    cum_t = cum.T
    padded = jnp.pad(cum, ((0, 0), (0, 64 - heads)))
    cum3 = jnp.concatenate([padded] * 3, axis=1)
    delta2 = pair_lanes(delta)
    grow2 = pair_lanes(jnp.exp(cum))
    fall2 = pair_lanes(fall)
    coef2 = pair_lanes(fall * delta)
    pref = [jnp.ones((heads,), F32) * keep_f[0]]
    for c in range(1, blocks):
        pref.append(keep_f[c] * dec[c - 1] * pref[-1])
    through = jnp.repeat(dec[blocks - 1] * pref[-1], width)[None, :]
    pref_wide = jnp.repeat(jnp.stack(pref), width, axis=1)[:, None, :]
    dec_wide = jnp.repeat(dec, width, axis=1)[:, None, :]

    params = pltpu.CompilerParams(vmem_limit_bytes=VMEM)
    smem = pl.BlockSpec(memory_space=pltpu.SMEM)
    full = lambda *shape: pl.BlockSpec(shape, lambda g: (0,) * len(shape))
    up = lambda *shape: pl.BlockSpec(shape, lambda g: (g,) + (0,) * (len(shape) - 1))
    down = lambda *shape: pl.BlockSpec(
        shape, lambda g: (blocks - 1 - g,) + (0,) * (len(shape) - 1)
    )
    out = jax.ShapeDtypeStruct
    cost = lambda flops, size: pl.CostEstimate(
        flops=flops, bytes_accessed=size, transcendentals=rows * inner
    )
    halo_block = pl.BlockSpec((HALO, inner), lambda g: (rows // HALO, 0))
    wide_map = 2 * rows * inner * nstate

    u, local_states, chunk_state = pl.pallas_call(
        conv_states_kernel,
        grid=(blocks,),
        in_specs=[
            smem, up(LEN, inner), halo_block, full(4, inner), full(1, inner), up(LEN, nstate),
            up(LEN, 128), up(1, 1, inner), full(128, inner),
        ],
        out_specs=[up(LEN, inner), up(1, nstate, inner), full(nstate, inner)],
        out_shape=[
            out((rows, inner), F32), out((blocks, nstate, inner), BF16), out((nstate, inner), F32),
        ],
        scratch_shapes=[pltpu.VMEM((LEN + 8, inner), F32), pltpu.VMEM((nstate, inner), F32)],
        compiler_params=params,
        cost_estimate=cost(2 * wide_map, rows * inner * 12),
        name="conv_states",
    )(keep, inner_proj, inner_proj, taps, inner_bias, b_map, coef2, dec_wide, spread)

    to_right = [(i, i + 1) for i in range(parts - 1)]
    to_left = [(i + 1, i) for i in range(parts - 1)]
    entering = lax.ppermute(chunk_state.astype(BF16), "tensor", to_right)
    for _ in range(parts - 2):
        entering = lax.ppermute(
            (chunk_state + through * entering.astype(F32)).astype(BF16), "tensor", to_right
        )

    y_within = pl.pallas_call(
        within_kernel,
        grid=(blocks,),
        in_specs=[
            up(LEN, inner), up(LEN, 192), pl.BlockSpec((heads, LEN), lambda g: (0, g)),
            up(LEN, 128), up(LEN, nstate), up(LEN, nstate), full(192, heads * LEN),
            full(128, inner),
        ],
        out_specs=up(LEN, inner),
        out_shape=out((rows, inner), F32),
        compiler_params=params,
        cost_estimate=cost(8 * wide_map, rows * inner * 8),
        name="within",
    )(u, cum3, cum_t, delta2, b_map, c_map, columns, spread)

    w_gates = gather_columns(w_gate)
    w_out = gather_output(w_output)
    grad_pieces = send_rows(out_grad, False)
    if aligned:
        (masked,) = join(join_kernel, grad_pieces, live, True, 1)
    else:
        masked = join_plain(grad_pieces) * live.astype(BF16)
    gate_proj = dot_nn(normed, w_gates)
    normed_y_grad = dot_nt(masked, w_out)

    normed_y, scan_grad, gate_grad, q_plus, dc_across, gain_out_grad, skip_lanes, chunk_grad = (
        pl.pallas_call(
            gate_kernel,
            grid=(blocks,),
            in_specs=[
                smem, down(LEN, inner), down(LEN, inner), down(LEN, inner), down(LEN, inner),
                down(1, nstate, inner), full(nstate, inner), down(1, 1, inner), down(LEN, nstate),
                down(LEN, 128), full(1, inner), full(1, inner), down(1, 1, inner),
                full(128, inner), full(inner, 128),
            ],
            out_specs=[
                down(LEN, inner), down(LEN, inner), down(LEN, inner), down(LEN, 128),
                down(LEN, nstate), full(1, inner), full(1, inner), full(nstate, inner),
            ],
            out_shape=[
                out((rows, inner), BF16), out((rows, inner), BF16), out((rows, inner), BF16),
                out((rows, 128), F32), out((rows, nstate), F32), out((1, inner), F32),
                out((1, inner), F32), out((nstate, inner), F32),
            ],
            scratch_shapes=[
                pltpu.VMEM((LEN, inner), F32), pltpu.VMEM((nstate, inner), BF16),
                pltpu.VMEM((nstate, inner), F32),
            ],
            compiler_params=params,
            cost_estimate=cost(6 * wide_map, rows * inner * 24),
            name="gate",
        )(
            keep, y_within, u, gate_proj, normed_y_grad, local_states, entering, pref_wide, c_map,
            grow2, skip_wide, gain_out, dec_wide, spread, select,
        )
    )

    leaving = lax.ppermute(chunk_grad.astype(BF16), "tensor", to_left)
    for _ in range(parts - 2):
        leaving = lax.ppermute(
            (chunk_grad + through * leaving.astype(F32)).astype(BF16), "tensor", to_left
        )

    mixed_rows = dot_nn(normed_y, w_out).astype(BF16)

    mixed_out = land(send_back(mixed_rows), hidden_in, live_dev, BF16)

    def half_of(v, which):
        size = v.shape[1] // 2
        return lax.dynamic_slice_in_dim(v, which * size, size, 1)

    def finish(part_of, extra):
        pieces = []
        for d in range(parts):
            mine = part_of((column + d) % parts)
            if extra is not None:
                mine = jnp.concatenate([mine, extra], axis=1)
            mine = mine.astype(BF16)
            pieces.append(rotate(mine, d, parts) if d else mine)
        total = jnp.sum(in_order(pieces, column).astype(F32), axis=0).astype(BF16)
        return gather_pieces(total[None], dp_count)

    def column_grads(grads, extra_width):
        sent = swap(dot_tn(half_of(normed, 1 - core), grads).astype(BF16), 0, dp_count)
        total = reduce_core(dot_tn(half_of(normed, core), grads), sent)
        total = scatter_rows(total.reshape(groups, k_rows, -1), dp_count, dp)
        pieces = finish(
            lambda t: lax.dynamic_slice_in_dim(total, t * shard, shard, 1),
            total[:, inner:] if extra_width else None,
        )
        rows_of = []
        for _, mask, at in pieces:
            c2, q2 = slices_of(dp ^ mask)
            rows_of.append([c2 * (model // 2) + q2 * k_rows + at])
        return place(
            [a for a, _, _ in pieces], rows_of, None, (model, shard + extra_width)
        ).astype(F32)

    def output_grads():
        sent = swap(dot_tn(normed_y, half_of(masked, 1 - core)).astype(BF16), 0, dp_count)
        total = reduce_core(dot_tn(normed_y, half_of(masked, core)), sent)
        cols = model // 2
        size = shard // groups
        total = total.reshape(parts, groups, size, cols)
        total = jnp.swapaxes(total, 0, 1).reshape(groups, parts * size, cols)
        total = scatter_rows(total, dp_count, dp).reshape(parts, size, cols)
        pieces = finish(lambda t: lax.dynamic_index_in_dim(total, t, 0, keepdims=False), None)
        rows_of, cols_of = [], []
        for _, mask, at in pieces:
            c2, q2 = slices_of(dp ^ mask)
            rows_of.append([q2 * size + at])
            cols_of.append([c2 * cols])
        return place([a for a, _, _ in pieces], rows_of, cols_of, (shard, model)).astype(F32)

    w_gate_grad = column_grads(gate_grad, 0)
    w_output_grad = output_grads()
    gate_part = dot_nt(gate_grad, w_gates)

    dv_within, db_within, dc_within = pl.pallas_call(
        within_back_kernel,
        grid=(blocks,),
        in_specs=[
            up(LEN, inner), up(LEN, inner), up(LEN, 192),
            pl.BlockSpec((heads, LEN), lambda g: (0, g)), up(LEN, 128), up(LEN, nstate),
            up(LEN, nstate), full(192, heads * LEN), full(128, inner),
        ],
        out_specs=[up(LEN, inner), up(LEN, nstate), up(LEN, nstate)],
        out_shape=[out((rows, inner), F32), out((rows, nstate), F32), out((rows, nstate), F32)],
        compiler_params=params,
        cost_estimate=cost(16 * wide_map, rows * inner * 10),
        name="within_back",
    )(u, scan_grad, cum3, cum_t, delta2, b_map, c_map, columns, spread)

    inner_grad, db_across, q_minus, step_sums, end_lanes, taps_grad, bias_grad, head_rows = (
        pl.pallas_call(
            across_back_kernel,
            grid=(blocks,),
            in_specs=[
                smem, down(LEN, inner), down(LEN, inner), down(LEN, inner), down(LEN, inner),
                halo_block, down(1, nstate, inner), full(nstate, inner), down(1, 1, inner),
                full(nstate, inner), down(LEN, nstate), down(LEN, nstate), down(LEN, 128),
                down(LEN, 128), down(LEN, 128), full(1, inner), down(1, 1, inner), full(4, inner),
                full(128, inner), full(inner, 128),
            ],
            out_specs=[
                down(LEN, inner), down(LEN, nstate), down(LEN, 128), down(LEN, 128),
                down(1, 1, inner), full(4, inner), full(1, inner), full(8, inner),
            ],
            out_shape=[
                out((rows, inner), BF16), out((rows, nstate), F32), out((rows, 128), F32),
                out((rows, 128), F32), out((blocks, 1, inner), F32), out((4, inner), F32),
                out((1, inner), F32), out((8, inner), F32),
            ],
            scratch_shapes=[
                pltpu.VMEM((nstate, inner), F32), pltpu.VMEM((LEN + 8, inner), F32),
            ],
            compiler_params=params,
            cost_estimate=cost(6 * wide_map, rows * inner * 20),
            name="across_back",
        )(
            keep, u, scan_grad, dv_within, inner_proj, inner_proj, local_states, entering,
            pref_wide, leaving, b_map, c_map, grow2, fall2, delta2, skip_wide, dec_wide, taps,
            spread, select,
        )
    )

    shared_du = jnp.concatenate([db_within + db_across, dc_within + dc_across], axis=1) * (
        shared_open * (1.0 + shared_u * (1.0 - shared_open))
    )
    heads_of_chunk = lax.ppermute(
        jnp.concatenate([head_rows, shared_du[:8] * keep_f[0]], axis=1), "tensor", to_left
    )
    tail = inner_grad[rows - 16 :].astype(F32)
    later = jnp.concatenate([jnp.zeros((8, inner), F32), heads_of_chunk[:, :inner]], axis=0)
    for lag in range(1, 4):
        moved = jnp.concatenate(
            [jnp.zeros((16 - lag, inner), F32), heads_of_chunk[:lag, :inner]], axis=0
        )
        tail = tail + taps[3 - lag][None, :] * moved
    inner_grad = lax.dynamic_update_slice(inner_grad, tail.astype(BF16), (rows - 16, 0))

    shared_later = jnp.concatenate([shared_du, heads_of_chunk[:, inner:]], axis=0)
    shared_grad = conv_shared[3][None, :] * shared_du
    conv_shared_grad = [None] * 4
    conv_shared_grad[3] = jnp.sum(shared_du * shared_ext[8:], axis=0)
    for lag in range(1, 4):
        blocked = (shared_later * allowed(lag))[lag : lag + rows]
        shared_grad = shared_grad + conv_shared[3 - lag][None, :] * blocked
        conv_shared_grad[3 - lag] = jnp.sum(
            shared_du * shared_ext[8 - lag : 8 - lag + rows] * allowed(lag)[:rows], axis=0
        )
    shared_grad = shared_grad.astype(BF16)
    conv_shared_grad = jnp.stack(conv_shared_grad)
    conv_shared_bias_grad = jnp.sum(shared_du, axis=0)

    ends = jnp.sum(end_lanes.reshape(blocks, heads, width), axis=2)
    dcum = (q_plus - q_minus)[:, :heads].reshape(blocks, LEN, heads)
    da = (
        jnp.einsum("ts,cth->csh", triangle, dcum, precision=PRECISE) + ends[:, None, :]
    ).reshape(rows, heads)
    raw_grad = (step_sums[:, :heads] - da * rates) * jax.nn.sigmoid(raw)
    step_grad = raw_grad.astype(BF16)
    decay_log_grad = jnp.sum(da * decays, axis=0)
    step_bias_grad = jnp.sum(raw_grad, axis=0)
    skip_gain_grad = jnp.sum(skip_lanes.reshape(heads, width), axis=1)

    misc_grad = jnp.concatenate(
        [shared_grad, step_grad, jnp.zeros((rows, 128 - heads), BF16)], axis=1
    )
    w_in_grad = column_grads(
        jnp.concatenate([inner_grad, misc_grad], axis=1), 2 * nstate + 128
    )
    normed_grad = gate_part + dot_nt(inner_grad, w_in) + dot_nt(misc_grad, w_misc)
    own = hid[:rows].astype(F32)
    own_factor = lax.rsqrt(jnp.mean(own * own, axis=1, keepdims=True) + EPSILON)
    weighted = normed_grad * norm_gain[None, :]
    row_stat = jnp.sum(weighted * own, axis=1, keepdims=True)
    input_grad = (
        own_factor * weighted
        - own * (own_factor * own_factor * own_factor * row_stat / model)
    ).astype(BF16)
    norm_gain_grad = jnp.sum(normed_grad * own * own_factor, axis=0)
    hidden_grad = land(send_back(input_grad), out_grad, live_dev, F32)

    tiny = jnp.concatenate(
        [
            taps_grad.reshape(-1), bias_grad.reshape(-1), gain_out_grad.reshape(-1),
            step_bias_grad, decay_log_grad, skip_gain_grad, conv_shared_grad.reshape(-1),
            conv_shared_bias_grad, norm_gain_grad,
        ]
    )
    for bit in range(dp_count.bit_length() - 1):
        tiny = tiny + swap(tiny, bit, dp_count)
    tiny = jnp.sum(
        in_order([tiny] + [rotate(tiny, d, parts) for d in range(1, parts)], column), axis=0
    )
    ends_at = [0]
    for size in (4 * inner, inner, inner, heads, heads, heads, 8 * nstate, 2 * nstate, model):
        ends_at.append(ends_at[-1] + size)
    part = lambda i: tiny[ends_at[i] : ends_at[i + 1]]
    own_part = lambda v, size: lax.dynamic_slice_in_dim(v, column * size, size, 0)
    conv_inner_grad = lax.dynamic_slice_in_dim(part(0).reshape(4, inner), column * shard, shard, 1)
    w_step_grad = lax.dynamic_slice_in_dim(
        w_in_grad, shard + 2 * nstate + column * heads_shard, heads_shard, 1
    )
    return (
        mixed_out,
        hidden_grad,
        part(8),
        w_gate_grad,
        w_in_grad[:, :shard],
        w_in_grad[:, shard : shard + 2 * nstate],
        w_step_grad,
        conv_inner_grad,
        part(6).reshape(4, 2 * nstate),
        own_part(part(1), shard),
        part(7),
        own_part(part(3), heads_shard),
        own_part(part(4), heads_shard),
        own_part(part(5), heads_shard),
        own_part(part(2), shard),
        w_output_grad,
    )


def solution(mesh):
    split = P("tensor")
    in_specs = (
        P("dp", "tensor"), P("dp", "tensor"), P(), P(), P(), P(), P(None, "tensor"),
        P(None, "tensor"), P(), P(None, "tensor"), P(None, "tensor"), P(), split, P(), split,
        split, split, split, P("tensor", None),
    )
    out_specs = (
        P("dp", "tensor"), P("dp", "tensor"), P(), P(None, "tensor"), P(None, "tensor"), P(),
        P(None, "tensor"), P(None, "tensor"), P(), split, P(), split, split, split, split,
        P("tensor", None),
    )
    body = functools.partial(local, mesh.shape["dp"], mesh.shape["tensor"])
    return jax.shard_map(body, mesh=mesh, in_specs=in_specs, out_specs=out_specs, check_vma=False)
```

time: 2050 us -> 1140 us (0.56)
  waiting for transfers between devices: 790 us -> 251 us
  matrix products: 516 us -> 128 us
  Pallas kernels: 0 us -> 290 us
  other arithmetic: 331 us -> 82.3 us
  starting transfers between devices: 0.28 us -> 234 us
  local copies, waits for them, and re-layouts: 282 us -> 143 us
  blocking collectives: 101 us -> 0 us
    psum x3 -> x0, waiting for transfers between devices: 538 us -> none  [the longest x1 212 us: local(): lax.psum(normed_grad.astype(jnp.bfloat16), 'tensor').astype(jnp.float32)]
    dot_general x27 -> x16, matrix products: 516 us -> 128 us  [the longest x6 45.5 us: dot_tn(): lax.dot_general(a, b, (((0,), (0,)), ((), ())), preferred_element_type=F32)]
    pallas_call x0 -> x15, Pallas kernels: none -> 290 us  [the longest x1 64.9 us: local(): pl.pallas_call(across_back_kernel, grid=(blocks,), in_specs=[smem, down(L...]
    ppermute x0 -> x115, waiting for transfers between devices: none -> 251 us  [the longest x36 141 us: rotate(): lax.ppermute(v, 'tensor', [(i, (i + by) % count) for i in range(count)])]
    ppermute x0 -> x115, starting transfers between devices: none -> 234 us  [the longest x36 162 us: rotate(): lax.ppermute(v, 'tensor', [(i, (i + by) % count) for i in range(count)])]
    all_gather x2 -> x0, waiting for transfers between devices: 160 us -> none  [the longest x1 160 us: local(): lax.all_gather(hidden_in, 'tensor', axis=1, tiled=True)]
    reduce_sum x22 -> x12, other arithmetic: 124 us -> 10.1 us  [the longest x3 4.68 us: finish(): total = jnp.sum(in_order(pieces, column).astype(F32), axis=0).astype(BF16)]
    psum x4 -> x0, blocking collectives: 101 us -> none  [the longest x1 43.8 us: local(): lax.psum((norm_gain_part, w_shared_part, conv_shared_part, conv_shared_bi...]
  transfers between devices with their start and end apart: 7 -> 115, of which waited for: 5 -> 30; matrix products, arithmetic and copies ran while one was open for 30% -> 29% of each run, Pallas kernels for 0% -> 20%
where the time goes in v1:
time: 1140 us; the launch traced here: 1130 us
  Pallas kernels  290 us (25%)
  waiting for transfers between devices  251 us (22%)
  starting transfers between devices  234 us (21%)
  local copies, waits for them, and re-layouts  143 us (13%)
  matrix products  128 us (11%)
  other arithmetic  82.3 us (7%)
    ppermute x36, starting transfers between devices, rotate(): lax.ppermute(v, 'tensor', [(i, (i + by) % count) for i in range(count)])  162 us
    ppermute x36, waiting for transfers between devices, rotate(): lax.ppermute(v, 'tensor', [(i, (i + by) % count) for i in range(count)])  141 us
    ppermute x72, waiting for transfers between devices, swap(): return lax.ppermute(v, 'dp', [(i, i ^ 1 << bit) for i in range(count)])  91.1 us
    pallas_call x1, Pallas kernels, local(): pl.pallas_call(across_back_kernel, grid=(blocks,), in_specs=[smem, down(L...  64.9 us
    pallas_call x1, Pallas kernels, local(): pl.pallas_call(gate_kernel, grid=(blocks,), in_specs=[smem, down(LEN, inn...  55.2 us
    ppermute x72, starting transfers between devices, swap(): return lax.ppermute(v, 'dp', [(i, i ^ 1 << bit) for i in range(count)])  52 us
    dot_general x6, matrix products, dot_tn(): lax.dot_general(a, b, (((0,), (0,)), ((), ())), preferred_element_type=F32)  45.5 us
    pallas_call x1, Pallas kernels, local(): pl.pallas_call(within_back_kernel, grid=(blocks,), in_specs=[up(LEN, inne...  44.4 us
  transfers between devices with their start and end apart: 115, of which 30 were waited for; matrix products, arithmetic and copies ran while one was open for 29% of the time, Pallas kernels for 20%

profile of v1, /device:TPU:0, one launch (start us, length us, event | category | flops | bytes accessed | tf_op | source)
XLA Modules:
  0.0 1132.1 jit_solution(7624703205635503106)
XLA Ops:
  67.2 13.7 %collective-permute-start = (bf16[784,384]{1,0:T(8,128)(2,1)}, bf16[784,384]{1,0:T(8,128)(2,1)S(1)}, u32[]{:S(2)}, u32[]{:S(2)}) collective-permute-start(bf16[784,384]{1,0:T(8,128)(2,1)} %pad_maximum_fusion.10), channel_id=1, source_target_pairs={{0,1},{1,2},{2,3},{3,0},{4,5},{5,6},{6,7},{7,4},{8,9},{9,10},{10,1... | collective-permute-start | bytes 1806344 | tf_op jit(solution)/shard_map/ppermute | solution.py:455
  90.5 37.5 %collective-permute-done.19 = bf16[192,768]{1,0:T(8,128)(2,1)} collective-permute-done((bf16[192,768]{1,0:T(8,128)(2,1)}, bf16[192,768]{1,0:T(8,128)(2,1)}, u32[]{:S(2)}, u32[]{:S(2)}) %collective-permute-start.19) | collective-permute-done | bytes 294944 | tf_op jit(solution)/shard_map/ppermute | solution.py:455
  147.7 26.9 %collective-permute-start.2 = (bf16[784,384]{1,0:T(8,128)(2,1)}, bf16[784,384]{1,0:T(8,128)(2,1)}, u32[]{:S(2)}, u32[]{:S(2)}) collective-permute-start(bf16[784,384]{1,0:T(8,128)(2,1)} %pad_maximum_fusion.12), channel_id=1, source_target_pairs={{0,3},{1,0},{2,1},{3,2},{4,7},{5,4},{6,5},{7,6},{8,11},{9,8},{10,9... | collective-permute-start | bytes 1806344 | tf_op jit(solution)/shard_map/ppermute | solution.py:455
  229.6 11.0 collective-permute-done.8.refs_3_
  287.3 12.4 %fusion.138.ip_ref.halo_ref = f32[784,3072]{1,0:T(8,128)} fusion(bf16[784,1536]{1,0:T(8,128)(2,1)S(1)} %copy-done.58, bf16[1536,3072]{1,0:T(8,128)(2,1)} %place.6), kind=kOutput, calls=%fused_computation.341 | convolution fusion | flops 7398752256 | bytes 21479424 | tf_op jit(solution)/shard_map/dot_general | solution.py:21
  299.7 30.0 %conv_states.1 = (f32[768,3072]{1,0:T(8,128)}, bf16[6,128,3072]{2,1,0:T(8,128)(2,1)}, f32[128,3072]{1,0:T(8,128)}) custom-call(s32[7]{0:T(128)S(1)} %get-tuple-element.211.keep_ref, f32[784,3072]{1,0:T(8,128)} %fusion.138.ip_ref.halo_ref, f32[784,3072]{1,0:T(8,128)} %fusion.138.ip_ref.halo_ref, f32[4,3072]{1,0:T(4,128)S(1)} %bitcast.288, ...), custom_call_target="tpu_custom_call" | custom-call | flops 1207959552 | bytes 28311552 | tf_op jit(solution)/shard_map/conv_states/pallas_call | solution.py:777
  363.6 12.2 %fusion.121.gate_ref = f32[768,3072]{1,0:T(8,128)} fusion(bf16[1536,3072]{1,0:T(8,128)(2,1)} %place.7, bf16[784,1536]{1,0:T(8,128)(2,1)S(1)} %copy-done.58), kind=kOutput, calls=%fused_computation.324 | convolution fusion | flops 7247757312 | bytes 21233664 | tf_op jit(solution)/shard_map/dot_general | solution.py:21
  390.1 12.3 %fusion.139.ng_ref = f32[768,3072]{1,0:T(8,128)} fusion(bf16[768,1536]{1,0:T(8,128)(2,1)S(1)} %copy-done.54, bf16[3072,1536]{1,0:T(8,128)(2,1)} %place.8), kind=kOutput, calls=%fused_computation.342 | convolution fusion | flops 7247757312 | bytes 21233664 | tf_op jit(solution)/shard_map/dot_general | solution.py:25
  402.5 39.9 %within.1.y_ref = f32[768,3072]{1,0:T(8,128)} custom-call(f32[768,3072]{1,0:T(8,128)} %get-tuple-element.42.u_ref, f32[768,192]{1,0:T(8,128)} %pad_maximum_fusion.5.cum_ref, f32[48,768]{1,0:T(8,128)S(1)} %copy.72.cum_t_ref, f32[768,128]{1,0:T(8,128)S(1)} %get-tuple-element.215.step_ref, f32[768,128]{1,0:T(8,128)S(1)} %get-tuple-element.173.b_ref, ...), custom_call_target="tpu_custom_call" | custom-call | flops 4831838208 | bytes 18874368 | tf_op jit(solution)/shard_map/within/pallas_call | solution.py:802
  443.3 55.2 %gate.1 = (bf16[768,3072]{1,0:T(8,128)(2,1)}, bf16[768,3072]{1,0:T(8,128)(2,1)}, bf16[768,3072]{1,0:T(8,128)(2,1)}, f32[768,128]{1,0:T(8,128)S(1)}, f32[768,128]...) custom-call(s32[7]{0:T(128)S(1)} %get-tuple-element.211.keep_ref, ...), custom_call_target="tpu_custom_call" | custom-call | flops 3623878656 | bytes 56623104 | tf_op jit(solution)/shard_map/gate/pallas_call | solution.py:828
  502.0 12.6 %convolution_convert_fusion.3 = bf16[768,1536]{1,0:T(8,128)(2,1)} fusion(bf16[768,3072]{1,0:T(8,128)(2,1)} %get-tuple-element.45, bf16[3072,1536]{1,0:T(8,128)(2,1)} %place.8), kind=kOutput, calls=%fused_computation.42 | convolution fusion | flops 7248936960 | bytes 16515072 | tf_op jit(solution)/shard_map/dot_general | solution.py:21
  531.3 13.2 %collective-permute-done.52 = bf16[128,3072]{1,0:T(8,128)(2,1)} collective-permute-done((bf16[128,3072]{1,0:T(8,128)(2,1)}, bf16[128,3072]{1,0:T(8,128)(2,1)}, u32[]{:S(2)}, u32[]{:S(2)}) %collective-permute-start.52) | collective-permute-done | bytes 786464 | tf_op jit(solution)/shard_map/ppermute | solution.py:861
  547.6 44.4 %within_back.1 = (f32[768,3072]{1,0:T(8,128)}, f32[768,128]{1,0:T(8,128)S(1)}, f32[768,128]{1,0:T(8,128)S(1)}) custom-call(f32[768,3072]{1,0:T(8,128)} %get-tuple-element.42.u_ref, bf16[768,3072]{1,0:T(8,128)(2,1)} %get-tuple-element.48.dy_ref, f32[768,192]{1,0:T(8,128)} %pad_maximum_fusion.5.cum_ref, f32[48,768]{1,0:T(8,128)S(1)} %copy.72.cum_t_ref, ...), custom_call_target="tpu_custom_call" | custom-call | flops 9663676416 | bytes 23592960 | tf_op jit(solution)/shard_map/within_back/pallas_call | solution.py:920
  594.2 64.9 %across_back.1 = (bf16[768,3072]{1,0:T(8,128)(2,1)}, f32[768,128]{1,0:T(8,128)S(1)}, f32[768,128]{1,0:T(8,128)S(1)}, f32[768,128]{1,0:T(8,128)S(1)}, f32[6,1,307...) custom-call(s32[7]{0:T(128)S(1)} %get-tuple-element.211.keep_ref, ...), custom_call_target="tpu_custom_call" | custom-call | flops 3623878656 | bytes 47185920 | tf_op jit(solution)/shard_map/across_back/pallas_call | solution.py:936
  673.0 8.9 concatenate.146
  681.9 9.9 convolution_convert_fusion
  695.5 10.9 fusion.140
  706.5 14.7 %fusion.5 = (f32[1536]{0:T(1024)S(1)}, f32[768]{0:T(1024)S(1)}, f32[768,1536]{1,0:T(8,128)}) fusion(f32[768]{0:T(1024)S(1)} %add_rsqrt_fusion, bf16[784,1536]{1,0:T(8,128)(2,1)} %get-tuple-element.46, f32[1536]{0:T(1024)S(1)} %copy-done.100, f32[768,1536]{1,0:T(8,128)} %fusion.51, f32[768,1536]{1,0:T(8,128)} %fusion.140, ...), kind=kOutput, calls=%fused_computation.15 | convolution fusion | flops 7258372096 | bytes 30689280 | tf_op jit(solution)/shard_map/dot_general | solution.py:25
  730.3 10.1 convert_add_fusion.1
  771.3 10.3 collective-permute-done.101
  787.6 19.6 %collective-permute-done.65 = bf16[2,1,192,1536]{3,2,1,0:T(8,128)(2,1)S(1)} collective-permute-done((bf16[2,1,192,1536]{3,2,1,0:T(8,128)(2,1)S(1)}, bf16[2,1,192,1536]{3,2,1,0:T(8,128)(2,1)S(1)}, u32[]{:S(2)}, u32[]{:S(2)}) %collective-permute-start.65) | collective-permute-done | bytes 1179680 | tf_op jit(solution)/shard_map/ppermute | solution.py:451
  811.3 8.6 collective-permute-done.102
  840.1 17.9 %collective-permute-start.48 = (bf16[768,384]{1,0:T(8,128)(2,1)S(1)}, bf16[768,384]{1,0:T(8,128)(2,1)S(1)}, u32[]{:S(2)}, u32[]{:S(2)}) collective-permute-start(bf16[768,384]{1,0:T(8,128)(2,1)S(1)} %copy-done.79), channel_id=1, source_target_pairs={{0,1},{1,2},{2,3},{3,0},{4,5},{5,6},{6,7},{7,4},{8,9},{9,10},{10,1... | collective-permute-start | bytes 1769480 | tf_op jit(solution)/shard_map/ppermute | solution.py:455
  858.0 12.1 %collective-permute-done.104 = bf16[192,768]{1,0:T(8,128)(2,1)} collective-permute-done((bf16[192,768]{1,0:T(8,128)(2,1)}, bf16[192,768]{1,0:T(8,128)(2,1)}, u32[]{:S(2)}, u32[]{:S(2)}) %collective-permute-start.104) | collective-permute-done | bytes 294944 | tf_op jit(solution)/shard_map/ppermute | solution.py:455
  890.3 21.1 %collective-permute-start.49 = (bf16[768,384]{1,0:T(8,128)(2,1)S(1)}, bf16[768,384]{1,0:T(8,128)(2,1)S(1)}, u32[]{:S(2)}, u32[]{:S(2)}) collective-permute-start(bf16[768,384]{1,0:T(8,128)(2,1)S(1)} %copy-done.78), channel_id=1, source_target_pairs={{0,2},{1,3},{2,0},{3,1},{4,6},{5,7},{6,4},{7,5},{8,10},{9,11},{10,... | collective-permute-start | bytes 1769480 | tf_op jit(solution)/shard_map/ppermute | solution.py:455
  916.9 21.6 %collective-permute-done.86 = bf16[192,1152]{1,0:T(8,128)(2,1)S(1)} collective-permute-done((bf16[192,1152]{1,0:T(8,128)(2,1)S(1)}, bf16[192,1152]{1,0:T(8,128)(2,1)S(1)}, u32[]{:S(2)}, u32[]{:S(2)}) %collective-permute-start.86) | collective-permute-done | bytes 442400 | tf_op jit(solution)/shard_map/ppermute | solution.py:455
  938.5 19.8 %collective-permute-start.87 = (bf16[192,1152]{1,0:T(8,128)(2,1)S(1)}, bf16[192,1152]{1,0:T(8,128)(2,1)S(1)}, u32[]{:S(2)}, u32[]{:S(2)}) collective-permute-start(bf16[192,1152]{1,0:T(8,128)(2,1)S(1)} %get-tuple-element.181), channel_id=1, source_target_pairs={{0,2},{1,3},{2,0},{3,1},{4,6},{5,7},{6,4},{7,5},{8,10},{9,11},{10,... | collective-permute-start | bytes 1327112 | tf_op jit(solution)/shard_map/ppermute | solution.py:455
  958.3 15.7 %collective-permute-done.87 = bf16[192,1152]{1,0:T(8,128)(2,1)S(1)} collective-permute-done((bf16[192,1152]{1,0:T(8,128)(2,1)S(1)}, bf16[192,1152]{1,0:T(8,128)(2,1)S(1)}, u32[]{:S(2)}, u32[]{:S(2)}) %collective-permute-start.87) | collective-permute-done | bytes 442400 | tf_op jit(solution)/shard_map/ppermute | solution.py:455
  974.3 14.7 %collective-permute-done.88 = bf16[192,1152]{1,0:T(8,128)(2,1)S(1)} collective-permute-done((bf16[192,1152]{1,0:T(8,128)(2,1)S(1)}, bf16[192,1152]{1,0:T(8,128)(2,1)S(1)}, u32[]{:S(2)}, u32[]{:S(2)}) %collective-permute-start.88) | collective-permute-done | bytes 442400 | tf_op jit(solution)/shard_map/ppermute | solution.py:455
  989.0 12.3 %collective-permute-start.56 = (bf16[768,384]{1,0:T(8,128)(2,1)S(1)}, bf16[768,384]{1,0:T(8,128)(2,1)S(1)}, u32[]{:S(2)}, u32[]{:S(2)}) collective-permute-start(bf16[768,384]{1,0:T(8,128)(2,1)S(1)} %copy-done.81), channel_id=1, source_target_pairs={{0,2},{1,3},{2,0},{3,1},{4,6},{5,7},{6,4},{7,5},{8,10},{9,11},{10,... | collective-permute-start | bytes 1769480 | tf_op jit(solution)/shard_map/ppermute | solution.py:455
  1005.1 13.0 %collective-permute-done.61 = f32[21392]{0:T(1024)S(1)} collective-permute-done((f32[21392]{0:T(1024)S(1)}, f32[21392]{0:T(1024)S(1)}, u32[]{:S(2)}, u32[]{:S(2)}) %collective-permute-start.61) | collective-permute-done | bytes 85600 | tf_op jit(solution)/shard_map/ppermute | solution.py:455
  1042.6 10.7 collective-permute-done.74.refs_3_
  (749 shorter events, 490.7 us)
Async XLA Ops:
  50.1 77.9 %collective-permute-start.19 = (bf16[192,768]{1,0:T(8,128)(2,1)}, bf16[192,768]{1,0:T(8,128)(2,1)}, u32[]{:S(2)}, u32[]{:S(2)}) collective-permute-start(bf16[192,768]{1,0:T(8,128)(2,1)} %constant_dynamic-slice_fusion.16), channel_id=1, source_target_pairs={{0,2},{1,3},{2,0},{3,1},{4,6},{5,7},{6,4},{7,5},{8,10},{9,11},{10,... | collective-permute-start | bytes 884744 | tf_op jit(solution)/shard_map/ppermute | solution.py:455
  60.0 80.1 %collective-permute-start.20 = (bf16[192,768]{1,0:T(8,128)(2,1)}, bf16[192,768]{1,0:T(8,128)(2,1)}, u32[]{:S(2)}, u32[]{:S(2)}) collective-permute-start(bf16[192,768]{1,0:T(8,128)(2,1)} %constant_dynamic-slice_fusion.16), channel_id=1, source_target_pairs={{0,3},{1,0},{2,1},{3,2},{4,7},{5,4},{6,5},{7,6},{8,11},{9,8},{10,9... | collective-permute-start | bytes 884744 | tf_op jit(solution)/shard_map/ppermute | solution.py:455
  67.2 109.0 %collective-permute-start = (bf16[784,384]{1,0:T(8,128)(2,1)}, bf16[784,384]{1,0:T(8,128)(2,1)S(1)}, u32[]{:S(2)}, u32[]{:S(2)}) collective-permute-start(bf16[784,384]{1,0:T(8,128)(2,1)} %pad_maximum_fusion.10), channel_id=1, source_target_pairs={{0,1},{1,2},{2,3},{3,0},{4,5},{5,6},{6,7},{7,4},{8,9},{9,10},{10,1... | collective-permute-start | bytes 1806344 | tf_op jit(solution)/shard_map/ppermute | solution.py:455
  80.9 65.3 %collective-permute-start.30 = (bf16[768,384]{1,0:T(8,128)(2,1)}, bf16[768,384]{1,0:T(8,128)(2,1)}, u32[]{:S(2)}, u32[]{:S(2)}) collective-permute-start(bf16[768,384]{1,0:T(8,128)(2,1)} %get-tuple-element.150), channel_id=1, source_target_pairs={{0,1},{1,2},{2,3},{3,0},{4,5},{5,6},{6,7},{7,4},{8,9},{9,10},{10,1... | collective-permute-start | bytes 1769480 | tf_op jit(solution)/shard_map/ppermute | solution.py:455
  86.7 61.0 %collective-permute-start.31 = (bf16[768,384]{1,0:T(8,128)(2,1)}, bf16[768,384]{1,0:T(8,128)(2,1)}, u32[]{:S(2)}, u32[]{:S(2)}) collective-permute-start(bf16[768,384]{1,0:T(8,128)(2,1)} %get-tuple-element.149), channel_id=1, source_target_pairs={{0,2},{1,3},{2,0},{3,1},{4,6},{5,7},{6,4},{7,5},{8,10},{9,11},{10,... | collective-permute-start | bytes 1769480 | tf_op jit(solution)/shard_map/ppermute | solution.py:455
  128.0 46.6 %collective-permute-start.32 = (bf16[768,384]{1,0:T(8,128)(2,1)}, bf16[768,384]{1,0:T(8,128)(2,1)}, u32[]{:S(2)}, u32[]{:S(2)}) collective-permute-start(bf16[768,384]{1,0:T(8,128)(2,1)} %get-tuple-element.148), channel_id=1, source_target_pairs={{0,3},{1,0},{2,1},{3,2},{4,7},{5,4},{6,5},{7,6},{8,11},{9,8},{10,9... | collective-permute-start | bytes 1769480 | tf_op jit(solution)/shard_map/ppermute | solution.py:455
  140.1 67.8 %collective-permute-start.6 = (bf16[4,192,768]{2,1,0:T(8,128)(2,1)}, bf16[4,192,768]{2,1,0:T(8,128)(2,1)}, u32[]{:S(2)}, u32[]{:S(2)}) collective-permute-start(bf16[4,192,768]{2,1,0:T(8,128)(2,1)} %pad_maximum_fusion.refs_0_), channel_id=1, source_target_pairs={{0,8},{4,12},{8,0},{12,4},{16,24},{20,28},{24,16},{28,20},{1,9},{5... | collective-permute-start | bytes 3538952 | tf_op jit(solution)/shard_map/ppermute | solution.py:451
  146.2 43.5 %collective-permute-start.1 = (bf16[784,384]{1,0:T(8,128)(2,1)}, bf16[784,384]{1,0:T(8,128)(2,1)}, u32[]{:S(2)}, u32[]{:S(2)}) collective-permute-start(bf16[784,384]{1,0:T(8,128)(2,1)} %pad_maximum_fusion.11), channel_id=1, source_target_pairs={{0,2},{1,3},{2,0},{3,1},{4,6},{5,7},{6,4},{7,5},{8,10},{9,11},{10,... | collective-permute-start | bytes 1806344 | tf_op jit(solution)/shard_map/ppermute | solution.py:455
  147.7 49.1 %collective-permute-start.2 = (bf16[784,384]{1,0:T(8,128)(2,1)}, bf16[784,384]{1,0:T(8,128)(2,1)}, u32[]{:S(2)}, u32[]{:S(2)}) collective-permute-start(bf16[784,384]{1,0:T(8,128)(2,1)} %pad_maximum_fusion.12), channel_id=1, source_target_pairs={{0,3},{1,0},{2,1},{3,2},{4,7},{5,4},{6,5},{7,6},{8,11},{9,8},{10,9... | collective-permute-start | bytes 1806344 | tf_op jit(solution)/shard_map/ppermute | solution.py:455
  211.8 48.0 %collective-permute-start.11 = (bf16[4,192,768]{2,1,0:T(8,128)(2,1)}, bf16[4,192,768]{2,1,0:T(8,128)(2,1)}, u32[]{:S(2)}, u32[]{:S(2)}) collective-permute-start(bf16[4,192,768]{2,1,0:T(8,128)(2,1)} %collective-permute-done.6.refs_1_), channel_id=1, source_target_pairs={{0,4},{4,0},{8,12},{12,8},{16,20},{20,16},{24,28},{28,24},{1,5},{5... | collective-permute-start | bytes 3538952 | tf_op jit(solution)/shard_map/ppermute | solution.py:451
  211.9 48.0 %collective-permute-start.12 = (bf16[4,192,768]{2,1,0:T(8,128)(2,1)}, bf16[4,192,768]{2,1,0:T(8,128)(2,1)}, u32[]{:S(2)}, u32[]{:S(2)}) collective-permute-start(bf16[4,192,768]{2,1,0:T(8,128)(2,1)} %collective-permute-done.7.refs_2_), channel_id=1, source_target_pairs={{0,4},{4,0},{8,12},{12,8},{16,20},{20,16},{24,28},{28,24},{1,5},{5... | collective-permute-start | bytes 3538952 | tf_op jit(solution)/shard_map/ppermute | solution.py:451
  218.5 68.1 %collective-permute-start.36 = (bf16[4,96,1536]{2,1,0:T(8,128)(2,1)}, bf16[4,96,1536]{2,1,0:T(8,128)(2,1)}, u32[]{:S(2)}, u32[]{:S(2)}) collective-permute-start(bf16[4,96,1536]{2,1,0:T(8,128)(2,1)} %pad_maximum_fusion.2.refs_0_), channel_id=1, source_target_pairs={{0,8},{4,12},{8,0},{12,4},{16,24},{20,28},{24,16},{28,20},{1,9},{5... | collective-permute-start | bytes 3538952 | tf_op jit(solution)/shard_map/ppermute | solution.py:451
  228.1 58.7 %collective-permute-start.37 = (bf16[4,96,1536]{2,1,0:T(8,128)(2,1)}, bf16[4,96,1536]{2,1,0:T(8,128)(2,1)}, u32[]{:S(2)}, u32[]{:S(2)}) collective-permute-start(bf16[4,96,1536]{2,1,0:T(8,128)(2,1)} %pad_maximum_fusion.2.refs_0_), channel_id=1, source_target_pairs={{0,16},{4,20},{8,24},{12,28},{16,0},{20,4},{24,8},{28,12},{1,17},{... | collective-permute-start | bytes 3538952 | tf_op jit(solution)/shard_map/ppermute | solution.py:451
  276.9 55.2 %collective-permute-start.25 = (bf16[4,192,768]{2,1,0:T(8,128)(2,1)}, bf16[4,192,768]{2,1,0:T(8,128)(2,1)S(1)}, u32[]{:S(2)}, u32[]{:S(2)}) collective-permute-start(bf16[4,192,768]{2,1,0:T(8,128)(2,1)} %pad_maximum_fusion.1.refs_0_), channel_id=1, source_target_pairs={{0,4},{4,0},{8,12},{12,8},{16,20},{20,16},{24,28},{28,24},{1,5},{5... | collective-permute-start | bytes 3538952 | tf_op jit(solution)/shard_map/ppermute | solution.py:451
  277.0 66.7 %collective-permute-start.24 = (bf16[4,96,768]{2,1,0:T(8,128)(2,1)S(1)}, bf16[4,96,768]{2,1,0:T(8,128)(2,1)S(1)}, u32[]{:S(2)}, u32[]{:S(2)}) collective-permute-start(bf16[4,96,768]{2,1,0:T(8,128)(2,1)S(1)} %slice.366), channel_id=1, source_target_pairs={{0,8},{4,12},{8,0},{12,4},{16,24},{20,28},{24,16},{28,20},{1,9},{5... | collective-permute-start | bytes 1769480 | tf_op jit(solution)/shard_map/ppermute | solution.py:451
  286.6 57.6 %collective-permute-start.26 = (bf16[4,192,768]{2,1,0:T(8,128)(2,1)}, bf16[4,192,768]{2,1,0:T(8,128)(2,1)}, u32[]{:S(2)}, u32[]{:S(2)}) collective-permute-start(bf16[4,192,768]{2,1,0:T(8,128)(2,1)} %collective-permute-done.21.refs_1_), channel_id=1, source_target_pairs={{0,4},{4,0},{8,12},{12,8},{16,20},{20,16},{24,28},{28,24},{1,5},{5... | collective-permute-start | bytes 3538952 | tf_op jit(solution)/shard_map/ppermute | solution.py:451
  286.8 57.9 %collective-permute-start.27 = (bf16[4,192,768]{2,1,0:T(8,128)(2,1)}, bf16[4,192,768]{2,1,0:T(8,128)(2,1)}, u32[]{:S(2)}, u32[]{:S(2)}) collective-permute-start(bf16[4,192,768]{2,1,0:T(8,128)(2,1)} %collective-permute-done.22.refs_2_), channel_id=1, source_target_pairs={{0,4},{4,0},{8,12},{12,8},{16,20},{20,16},{24,28},{28,24},{1,5},{5... | collective-permute-start | bytes 3538952 | tf_op jit(solution)/shard_map/ppermute | solution.py:451
  287.1 58.8 %collective-permute-start.28 = (bf16[4,96,768]{2,1,0:T(8,128)(2,1)S(1)}, bf16[4,96,768]{2,1,0:T(8,128)(2,1)S(1)}, u32[]{:S(2)}, u32[]{:S(2)}) collective-permute-start(bf16[4,96,768]{2,1,0:T(8,128)(2,1)S(1)} %collective-permute-done.23.refs_3_), channel_id=1, source_target_pairs={{0,4},{4,0},{8,12},{12,8},{16,20},{20,16},{24,28},{28,24},{1,5},{5... | collective-permute-start | bytes 1769480 | tf_op jit(solution)/shard_map/ppermute | solution.py:451
  385.4 57.0 %collective-permute-start.47 = (bf16[128,3072]{1,0:T(8,128)(2,1)S(1)}, bf16[128,3072]{1,0:T(8,128)(2,1)S(1)}, u32[]{:S(2)}, u32[]{:S(2)}) collective-permute-start(bf16[128,3072]{1,0:T(8,128)(2,1)S(1)} %add_convert_fusion.2), channel_id=1, source_target_pairs={{0,1},{1,2},{2,3},{4,5},{5,6},{6,7},{8,9},{9,10},{10,11},{12,13},{... | collective-permute-start | bytes 2359304 | tf_op jit(solution)/shard_map/ppermute | solution.py:798
  520.2 210.1 %collective-permute-start.98 = (bf16[3072,768]{1,0:T(8,128)(2,1)}, bf16[3072,768]{1,0:T(8,128)(2,1)}, u32[]{:S(2)}, u32[]{:S(2)}) collective-permute-start(bf16[3072,768]{1,0:T(8,128)(2,1)} %convolution_convert_fusion.1), channel_id=1, source_target_pairs={{0,4},{4,0},{8,12},{12,8},{16,20},{20,16},{24,28},{28,24},{1,5},{5... | collective-permute-start | bytes 14155784 | tf_op jit(solution)/shard_map/ppermute | solution.py:451
  529.8 224.7 %collective-permute-start.64 = (bf16[768,3072]{1,0:T(8,128)(2,1)}, bf16[768,3072]{1,0:T(8,128)(2,1)}, u32[]{:S(2)}, u32[]{:S(2)}) collective-permute-start(bf16[768,3072]{1,0:T(8,128)(2,1)} %convolution_convert_fusion.2), channel_id=1, source_target_pairs={{0,4},{4,0},{8,12},{12,8},{16,20},{20,16},{24,28},{28,24},{1,5},{5... | collective-permute-start | bytes 14155784 | tf_op jit(solution)/shard_map/ppermute | solution.py:451
  546.3 47.0 %collective-permute-start.53 = (bf16[128,3072]{1,0:T(8,128)(2,1)S(1)}, bf16[128,3072]{1,0:T(8,128)(2,1)S(1)}, u32[]{:S(2)}, u32[]{:S(2)}) collective-permute-start(bf16[128,3072]{1,0:T(8,128)(2,1)S(1)} %add_convert_fusion), channel_id=1, source_target_pairs={{1,0},{2,1},{3,2},{5,4},{6,5},{7,6},{9,8},{10,9},{11,10},{13,12},{... | collective-permute-start | bytes 2359304 | tf_op jit(solution)/shard_map/ppermute | solution.py:861
  695.5 129.2 %collective-permute-start.81 = (bf16[768,3456]{1,0:T(8,128)(2,1)}, bf16[768,3456]{1,0:T(8,128)(2,1)}, u32[]{:S(2)}, u32[]{:S(2)}) collective-permute-start(bf16[768,3456]{1,0:T(8,128)(2,1)} %convolution_convert_fusion), channel_id=1, source_target_pairs={{0,4},{4,0},{8,12},{12,8},{16,20},{20,16},{24,28},{28,24},{1,5},{5... | collective-permute-start | bytes 15925256 | tf_op jit(solution)/shard_map/ppermute | solution.py:451
  823.8 46.3 %collective-permute-start.104 = (bf16[192,768]{1,0:T(8,128)(2,1)}, bf16[192,768]{1,0:T(8,128)(2,1)}, u32[]{:S(2)}, u32[]{:S(2)}) collective-permute-start(bf16[192,768]{1,0:T(8,128)(2,1)} %get-tuple-element.166), channel_id=1, source_target_pairs={{0,2},{1,3},{2,0},{3,1},{4,6},{5,7},{6,4},{7,5},{8,10},{9,11},{10,... | collective-permute-start | bytes 884744 | tf_op jit(solution)/shard_map/ppermute | solution.py:455
  824.6 45.5 %collective-permute-start.105 = (bf16[192,768]{1,0:T(8,128)(2,1)}, bf16[192,768]{1,0:T(8,128)(2,1)}, u32[]{:S(2)}, u32[]{:S(2)}) collective-permute-start(bf16[192,768]{1,0:T(8,128)(2,1)} %get-tuple-element.167), channel_id=1, source_target_pairs={{0,1},{1,2},{2,3},{3,0},{4,5},{5,6},{6,7},{7,4},{8,9},{9,10},{10,1... | collective-permute-start | bytes 884744 | tf_op jit(solution)/shard_map/ppermute | solution.py:455
  840.1 161.2 %collective-permute-start.48 = (bf16[768,384]{1,0:T(8,128)(2,1)S(1)}, bf16[768,384]{1,0:T(8,128)(2,1)S(1)}, u32[]{:S(2)}, u32[]{:S(2)}) collective-permute-start(bf16[768,384]{1,0:T(8,128)(2,1)S(1)} %copy-done.79), channel_id=1, source_target_pairs={{0,1},{1,2},{2,3},{3,0},{4,5},{5,6},{6,7},{7,4},{8,9},{9,10},{10,1... | collective-permute-start | bytes 1769480 | tf_op jit(solution)/shard_map/ppermute | solution.py:455
  890.3 111.6 %collective-permute-start.49 = (bf16[768,384]{1,0:T(8,128)(2,1)S(1)}, bf16[768,384]{1,0:T(8,128)(2,1)S(1)}, u32[]{:S(2)}, u32[]{:S(2)}) collective-permute-start(bf16[768,384]{1,0:T(8,128)(2,1)S(1)} %copy-done.78), channel_id=1, source_target_pairs={{0,2},{1,3},{2,0},{3,1},{4,6},{5,7},{6,4},{7,5},{8,10},{9,11},{10,... | collective-permute-start | bytes 1769480 | tf_op jit(solution)/shard_map/ppermute | solution.py:455
  911.4 91.6 %collective-permute-start.50 = (bf16[768,384]{1,0:T(8,128)(2,1)S(1)}, bf16[768,384]{1,0:T(8,128)(2,1)S(1)}, u32[]{:S(2)}, u32[]{:S(2)}) collective-permute-start(bf16[768,384]{1,0:T(8,128)(2,1)S(1)} %copy-done.77), channel_id=1, source_target_pairs={{0,3},{1,0},{2,1},{3,2},{4,7},{5,4},{6,5},{7,6},{8,11},{9,8},{10,9... | collective-permute-start | bytes 1769480 | tf_op jit(solution)/shard_map/ppermute | solution.py:455
  911.9 116.5 %collective-permute-start.55 = (bf16[768,384]{1,0:T(8,128)(2,1)S(1)}, bf16[768,384]{1,0:T(8,128)(2,1)S(1)}, u32[]{:S(2)}, u32[]{:S(2)}) collective-permute-start(bf16[768,384]{1,0:T(8,128)(2,1)S(1)} %copy-done.82), channel_id=1, source_target_pairs={{0,1},{1,2},{2,3},{3,0},{4,5},{5,6},{6,7},{7,4},{8,9},{9,10},{10,1... | collective-permute-start | bytes 1769480 | tf_op jit(solution)/shard_map/ppermute | solution.py:455
  1075.8 43.8 %collective-permute-start.93 = (bf16[1,192,1152]{2,1,0:T(8,128)(2,1)S(1)}, bf16[1,192,1152]{2,1,0:T(8,128)(2,1)}, u32[]{:S(2)}, u32[]{:S(2)}) collective-permute-start(bf16[1,192,1152]{2,1,0:T(8,128)(2,1)S(1)} %bitcast.277), channel_id=1, source_target_pairs={{0,4},{4,0},{8,12},{12,8},{16,20},{20,16},{24,28},{28,24},{1,5},{5... | collective-permute-start | bytes 1327112 | tf_op jit(solution)/shard_map/ppermute | solution.py:451
  1077.8 41.8 %collective-permute-start.94 = (bf16[1,192,1152]{2,1,0:T(8,128)(2,1)S(1)}, bf16[1,192,1152]{2,1,0:T(8,128)(2,1)}, u32[]{:S(2)}, u32[]{:S(2)}) collective-permute-start(bf16[1,192,1152]{2,1,0:T(8,128)(2,1)S(1)} %collective-permute-done.89.refs_1_), channel_id=1, source_target_pairs={{0,4},{4,0},{8,12},{12,8},{16,20},{20,16},{24,28},{28,24},{1,5},{5... | collective-permute-start | bytes 1327112 | tf_op jit(solution)/shard_map/ppermute | solution.py:451
  1077.8 41.8 %collective-permute-start.95 = (bf16[1,192,1152]{2,1,0:T(8,128)(2,1)}, bf16[1,192,1152]{2,1,0:T(8,128)(2,1)}, u32[]{:S(2)}, u32[]{:S(2)}) collective-permute-start(bf16[1,192,1152]{2,1,0:T(8,128)(2,1)} %copy-done.68), channel_id=1, source_target_pairs={{0,4},{4,0},{8,12},{12,8},{16,20},{20,16},{24,28},{28,24},{1,5},{5... | collective-permute-start | bytes 1327112 | tf_op jit(solution)/shard_map/ppermute | solution.py:451
  (222 other events, 4832.1 us)

commit v2 on v1

v2 whole, which is shorter than its diff:
```python
import functools

import jax
import jax.numpy as jnp
from jax import lax
from jax.experimental import pallas as pl
from jax.experimental.pallas import tpu as pltpu
from jax.sharding import PartitionSpec as P

F32 = jnp.float32
BF16 = jnp.bfloat16
PRECISE = lax.Precision.HIGHEST
EPSILON = 1e-05
LEN = 128
HALO = 16
WIDE = 256
VMEM = 52 * 1024 * 1024


def dot_nn(a, b):
    return jnp.dot(a, b, preferred_element_type=F32)


def dot_nt(a, b):
    return lax.dot_general(a, b, (((1,), (1,)), ((), ())), preferred_element_type=F32)


def dot_tn(a, b):
    return lax.dot_general(a, b, (((0,), (0,)), ((), ())), preferred_element_type=F32)


def sigmoid(v):
    return 0.5 * jnp.tanh(0.5 * v) + 0.5


def split_pair(v):
    lane = lax.broadcasted_iota(jnp.int32, v.shape, 1)
    high = v.astype(BF16).astype(F32)
    return jnp.where(lane < 64, high, v - high).astype(BF16)


def split_triple(v):
    lane = lax.broadcasted_iota(jnp.int32, v.shape, 1)
    high = v.astype(BF16).astype(F32)
    rest = v - high
    middle = rest.astype(BF16).astype(F32)
    return jnp.where(lane < 64, high, jnp.where(lane < 128, middle, rest - middle)).astype(BF16)


def head_sums(v, select):
    high = v.astype(BF16)
    low = (v - high.astype(F32)).astype(BF16)
    return dot_nn(high, select) + dot_nn(low, select)


def halves(v):
    high = v.astype(BF16)
    return high, (v - high.astype(F32)).astype(BF16)


def finer(dot, a, b):
    a_high, a_low = halves(a)
    b_high, b_low = halves(b)
    return dot(a_high, b_high) + (dot(a_high, b_low) + dot(a_low, b_high))


def fold(v):
    total = v[:, :128]
    for i in range(1, v.shape[1] // 128):
        total = total + v[:, i * 128 : (i + 1) * 128]
    return total


def chunk(i, width):
    return pl.ds(pl.multiple_of(i * width, width), width)


def maps_kernel(
    keep_ref, misc_ref, halo_ref, taps_ref, bias_ref, step_bias_ref, logs_ref,
    u_ref, b_ref, c_ref, step_ref, slope_ref, rate_ref, cum_ref, cum_t_ref, grow_ref, fall_ref,
    coef_ref, dec_ref, ext_ref,
):
    c = pl.program_id(0)
    keep = keep_ref[c].astype(F32)
    shared = u_ref.shape[1]

    @pl.when(c == 0)
    def _():
        ext_ref[0:8, :] = halo_ref[8:16, :shared] * keep

    @pl.when(c > 0)
    def _():
        ext_ref[0:8, :] = ext_ref[LEN : LEN + 8, :] * keep

    ext_ref[8 : LEN + 8, :] = misc_ref[:, :shared]
    u = bias_ref[...] + taps_ref[3:4, :] * ext_ref[8 : 8 + LEN, :]
    for lag in range(1, 4):
        u = u + taps_ref[3 - lag : 4 - lag, :] * ext_ref[8 - lag : 8 - lag + LEN, :]
    u_ref[...] = u
    maps = u * sigmoid(u)
    b_ref[...] = maps[:, : shared // 2]
    c_ref[...] = maps[:, shared // 2 :]

    raw = misc_ref[:, shared:] + step_bias_ref[...]
    step = jnp.maximum(raw, 0.0) + jnp.log1p(jnp.exp(-jnp.abs(raw)))
    slope_ref[...] = sigmoid(raw)
    step_ref[...] = step
    rates = -step * jnp.exp(logs_ref[...])
    rate_ref[...] = rates
    cum = running_sum(rates, False)
    cum_ref[...] = jnp.concatenate([cum, cum[:, :64]], axis=1)
    cum_t_ref[...] = cum.T
    last = cum[LEN - 1 : LEN, :]
    fall = jnp.exp(last - cum)
    grow_ref[...] = jnp.exp(cum)
    fall_ref[...] = fall
    coef_ref[...] = fall * step
    dec_ref[0] = jnp.exp(last)


def running_sum(v, backwards):
    row = lax.broadcasted_iota(jnp.int32, (LEN, LEN), 0)
    col = lax.broadcasted_iota(jnp.int32, (LEN, LEN), 1)
    ones = jnp.where((row <= col) if backwards else (row >= col), 1.0, 0.0).astype(BF16)
    total = jnp.zeros(v.shape, F32)
    for _ in range(3):
        term = v.astype(BF16)
        total = total + dot_nn(ones, term)
        v = v - term.astype(F32)
    return total


def maps_back_kernel(
    keep_ref, db1_ref, db2_ref, dc1_ref, dc2_ref, u_ref, misc_ref, halo_ref, taps_ref, plus_ref,
    minus_ref, sums_ref, ends_ref, slope_ref, rate_ref, logs_ref, whole_ref,
    grad_ref, taps_grad_ref, bias_grad_ref, head_ref, vector_ref, ext_ref,
):
    g = pl.program_id(0)
    c = pl.num_programs(0) - 1 - g
    keep = keep_ref[c].astype(F32)
    shared = u_ref.shape[1]

    @pl.when(g == 0)
    def _():
        taps_grad_ref[...] = jnp.zeros_like(taps_grad_ref)
        bias_grad_ref[...] = jnp.zeros_like(bias_grad_ref)
        vector_ref[...] = jnp.zeros_like(vector_ref)
        ext_ref[LEN : LEN + 8, :] = jnp.zeros((8, shared), F32)

    @pl.when(g > 0)
    def _():
        ext_ref[LEN : LEN + 8, :] = ext_ref[0:8, :] * keep_ref[c + 1].astype(F32)

    u = u_ref[...]
    open_ = sigmoid(u)
    dmaps = jnp.concatenate([db1_ref[...] + db2_ref[...], dc1_ref[...] + dc2_ref[...]], axis=1)
    du = dmaps * (open_ * (1.0 + u * (1.0 - open_)))
    ext_ref[0:LEN, :] = du
    proj = misc_ref[:, :shared]
    bias_grad_ref[...] += jnp.sum(du, axis=0, keepdims=True)
    total = taps_ref[3:4, :] * du
    taps_grad_ref[3:4, :] += jnp.sum(proj * du, axis=0, keepdims=True)
    for lag in range(1, 4):
        later = ext_ref[lag : lag + LEN, :]
        total = total + taps_ref[3 - lag : 4 - lag, :] * later
        taps_grad_ref[3 - lag : 4 - lag, :] += jnp.sum(proj * later, axis=0, keepdims=True)
    da = running_sum(plus_ref[...] - minus_ref[...], True) + ends_ref[0, 0:1, :]
    raw_grad = (sums_ref[...] - da * jnp.exp(logs_ref[...])) * slope_ref[...]
    grad_ref[...] = jnp.concatenate([total, raw_grad], axis=1).astype(BF16)
    vector_ref[0:1, :] += jnp.sum(raw_grad, axis=0, keepdims=True)
    vector_ref[1:2, :] += jnp.sum(da * rate_ref[...], axis=0, keepdims=True)

    @pl.when(c == 0)
    def _():
        head_ref[...] = ext_ref[0:8, :] * keep
        for lag in range(1, 4):
            part = keep * ext_ref[0:lag, :] * halo_ref[HALO - lag : HALO, :shared]
            taps_grad_ref[3 - lag : 4 - lag, :] += jnp.sum(part, axis=0, keepdims=True)


def input_grad_kernel(ng_ref, hid_ref, gain_ref, out_ref, gain_grad_ref):
    @pl.when(pl.program_id(0) == 0)
    def _():
        gain_grad_ref[...] = jnp.zeros_like(gain_grad_ref)

    width = ng_ref.shape[1]
    u = hid_ref[...].astype(F32)
    ng = ng_ref[...]
    factor = lax.rsqrt(jnp.sum(fold(u * u), axis=1, keepdims=True) / width + EPSILON)
    gain_grad_ref[...] += jnp.sum(ng * u * factor, axis=0, keepdims=True)
    weighted = ng * gain_ref[...]
    stat = jnp.sum(fold(weighted * u), axis=1, keepdims=True) / width
    out_ref[...] = (factor * weighted - u * (factor * factor * factor * stat)).astype(BF16)


def conv_states_kernel(
    keep_ref, ip_ref, halo_ref, taps_ref, bias_ref, b_ref, coef_ref, dec_ref, spread_ref,
    u_ref, local_ref, out_ref, wide_ref, pref_ref, through_ref, ext_ref, state_ref, run_ref,
):
    c = pl.program_id(0)
    keep = keep_ref[c].astype(F32)

    @pl.when(c == 0)
    def _():
        state_ref[...] = jnp.zeros_like(state_ref)
        run_ref[...] = jnp.ones_like(run_ref)
        ext_ref[0:8, :] = halo_ref[8:16, :] * keep

    @pl.when(c > 0)
    def _():
        ext_ref[0:8, :] = ext_ref[LEN : LEN + 8, :] * keep

    ext_ref[8 : LEN + 8, :] = ip_ref[...]
    coef = split_pair(coef_ref[...])
    dec = split_pair(jnp.broadcast_to(dec_ref[0], (8, 128)))
    b_map, b_low = halves(b_ref[...])

    def step(i, carry):
        at = chunk(i, WIDE)
        u = bias_ref[:, at] + taps_ref[3:4, at] * ext_ref[8 : 8 + LEN, at]
        for lag in range(1, 4):
            u = u + taps_ref[3 - lag : 4 - lag, at] * ext_ref[8 - lag : 8 - lag + LEN, at]
        u_ref[:, at] = u
        spread = spread_ref[:, at]
        w = (u * sigmoid(u) * dot_nn(coef, spread)).astype(BF16)
        state = state_ref[:, at] * keep
        local_ref[0, :, at] = state.astype(BF16)
        decay = dot_nn(dec, spread)[0:1, :]
        wide_ref[0, :, at] = decay
        pref = run_ref[:, at] * keep
        pref_ref[0, :, at] = pref
        run_ref[:, at] = pref * decay
        state_ref[:, at] = decay * state + (dot_tn(b_map, w) + dot_tn(b_low, w))
        return carry

    lax.fori_loop(0, u_ref.shape[1] // WIDE, step, 0, unroll=3)

    @pl.when(c == pl.num_programs(0) - 1)
    def _():
        out_ref[...] = state_ref[...]
        through_ref[...] = run_ref[...]


def within_kernel(
    u_ref, cum_ref, cum_t_ref, step_ref, b_ref, c_ref, columns_ref, spread_ref, y_ref
):
    scores = finer(dot_nt, c_ref[...], b_ref[...])
    row = lax.broadcasted_iota(jnp.int32, (LEN, LEN), 0)
    col = lax.broadcasted_iota(jnp.int32, (LEN, LEN), 1)
    scores = jnp.where(row >= col, scores, 0.0)
    scores = jnp.concatenate([scores, scores], axis=1)
    cum = split_triple(cum_ref[...])
    steps = split_pair(step_ref[...])
    first = col < 64

    def pair(p, carry):
        at = chunk(p, 128)
        left = dot_nn(cum, columns_ref[:, chunk(p, 256)])
        right = jnp.concatenate(
            [cum_t_ref[pl.ds(2 * p, 1), :], cum_t_ref[pl.ds(2 * p + 1, 1), :]], axis=1
        )
        mixing = (jnp.exp(jnp.minimum(left - right, 0.0)) * scores).astype(BF16)
        u = u_ref[:, at]
        v = u * sigmoid(u) * dot_nn(steps, spread_ref[:, at])
        stacked = jnp.concatenate(
            [jnp.where(first, v, 0.0).astype(BF16), jnp.where(first, 0.0, v).astype(BF16)], axis=0
        )
        y_ref[:, at] = dot_nn(mixing, stacked)
        return carry

    lax.fori_loop(0, u_ref.shape[1] // 128, pair, 0, unroll=8)


def gate_kernel(
    keep_ref, y_ref, u_ref, gate_ref, ng_ref, local_ref, enter_ref, pref_ref, c_ref, grow_ref,
    skip_ref, gain_ref, dec_ref, spread_ref, select_ref,
    ny_ref, dy_ref, gg_ref, q_ref, dc_ref, gain_grad_ref, skip_grad_ref, out_ref,
    scan_ref, carried_ref, state_ref, high_ref, low_ref, z_ref,
):
    g = pl.program_id(0)
    c = pl.num_programs(0) - 1 - g
    width = y_ref.shape[1]
    keep = keep_ref[c].astype(F32)

    @pl.when(g == 0)
    def _():
        state_ref[...] = jnp.zeros_like(state_ref)
        gain_grad_ref[...] = jnp.zeros_like(gain_grad_ref)
        skip_grad_ref[...] = jnp.zeros_like(skip_grad_ref)

    c_map, c_low = halves(c_ref[...])
    grow = split_pair(grow_ref[...])

    def forward(i, sums):
        squares, stat = sums
        at = chunk(i, WIDE)
        carried = (
            local_ref[0, :, at].astype(F32) + pref_ref[0, :, at] * enter_ref[:, at].astype(F32)
        ).astype(BF16)
        carried_ref[:, at] = carried
        scanned = y_ref[:, at] + dot_nn(grow, spread_ref[:, at]) * (dot_nn(c_map, carried)+dot_nn(c_low,carried))
        scan_ref[:, at] = scanned
        u = u_ref[:, at]
        y = scanned + skip_ref[:, at] * (u * sigmoid(u))
        gate = gate_ref[:, at]
        gated = y * (gate * sigmoid(gate))
        squares = squares + fold(gated * gated)
        stat = stat + fold(ng_ref[:, at] * gain_ref[:, at] * gated)
        return (squares, stat)

    nothing = jnp.zeros((LEN, 128), F32)
    squares, stat = lax.fori_loop(0, width // WIDE, forward, (nothing, nothing), unroll=3)
    scale = lax.rsqrt(jnp.sum(squares, axis=1, keepdims=True) / width + EPSILON)
    back = scale * scale * scale * (jnp.sum(stat, axis=1, keepdims=True) / width)

    def backward(i, carry):
        at = chunk(i, WIDE)
        scanned = scan_ref[:, at]
        u = u_ref[:, at]
        x = u * sigmoid(u)
        y = scanned + skip_ref[:, at] * x
        gate = gate_ref[:, at]
        open_ = sigmoid(gate)
        act = gate * open_
        gated = y * act
        scaled = gated * scale
        ng = ng_ref[:, at]
        gain = gain_ref[:, at]
        ny_ref[:, at] = (scaled * gain).astype(BF16)
        gain_grad_ref[:, at] += jnp.sum(ng * scaled, axis=0, keepdims=True)
        gated_grad = scale * (ng * gain) - gated * back
        gg_ref[:, at] = (gated_grad * y * open_ * (1.0 + gate * (1.0 - open_))).astype(BF16)
        dy_low = (gated_grad * act).astype(BF16)
        dy_ref[:, at] = dy_low
        dy = dy_low.astype(F32)
        skip_grad_ref[:, at] += jnp.sum(dy * x, axis=0, keepdims=True)
        high_ref[:, at], low_ref[:, at] = halves(dy * scanned)
        z = (dot_nn(grow, spread_ref[:, at]) * dy).astype(BF16)
        z_ref[:, at] = z
        state_ref[:, at] = keep * (dec_ref[0, :, at] * state_ref[:, at] + (dot_tn(c_map, z)+dot_tn(c_low,z)))
        return carry

    lax.fori_loop(0, width // WIDE, backward, 0, unroll=3)
    select = select_ref[...]
    q_ref[...] = dot_nn(high_ref[...], select) + dot_nn(low_ref[...], select)
    dc_ref[...] = dot_nt(z_ref[...], carried_ref[...])

    @pl.when(c == 0)
    def _():
        out_ref[...] = state_ref[...]


def within_back_kernel(
    u_ref, dy_ref, cum_ref, cum_t_ref, step_ref, b_ref, c_ref, columns_ref, spread_ref,
    dv_ref, db_ref, dc_ref,
):
    scores = finer(dot_nt, b_ref[...], c_ref[...])
    row = lax.broadcasted_iota(jnp.int32, (LEN, LEN), 0)
    col = lax.broadcasted_iota(jnp.int32, (LEN, LEN), 1)
    scores = jnp.where(row <= col, scores, 0.0)
    scores = jnp.concatenate([scores, scores], axis=1)
    cum = split_triple(cum_ref[...])
    steps = split_pair(step_ref[...])
    first = col < 64

    def pair(p, total):
        at = chunk(p, 128)
        left = dot_nn(cum, columns_ref[:, chunk(p, 256)])
        right = jnp.concatenate(
            [cum_t_ref[pl.ds(2 * p, 1), :], cum_t_ref[pl.ds(2 * p + 1, 1), :]], axis=1
        )
        decay = jnp.exp(jnp.minimum(right - left, 0.0))
        mixing = (decay * scores).astype(BF16)
        dy_low = dy_ref[:, at]
        dy = dy_low.astype(F32)
        dy_stack = jnp.concatenate(
            [jnp.where(first, dy, 0.0).astype(BF16), jnp.where(first, 0.0, dy).astype(BF16)], axis=0
        )
        dv_ref[:, at] = dot_nn(mixing, dy_stack)
        u = u_ref[:, at]
        v = u * sigmoid(u) * dot_nn(steps, spread_ref[:, at])
        v_stack = jnp.concatenate(
            [jnp.where(first, v, 0.0).astype(BF16), jnp.where(first, 0.0, v).astype(BF16)], axis=0
        )
        dw = dot_nt(v_stack, dy_low)
        return total + decay[:, :LEN] * dw[:LEN] + decay[:, LEN:] * dw[LEN:]

    total = lax.fori_loop(
        0, u_ref.shape[1] // 128, pair, jnp.zeros((LEN, LEN), F32), unroll=8
    )
    total = jnp.where(row <= col, total, 0.0)
    db_ref[...] = finer(dot_nn, total, c_ref[...])
    dc_ref[...] = finer(dot_tn, total, b_ref[...])


def across_back_kernel(
    keep_ref, u_ref, dy_ref, dv_ref, ip_ref, halo_ref, local_ref, enter_ref, pref_ref, leave_ref,
    b_ref, c_ref, grow_ref, fall_ref, step_ref, skip_ref, dec_ref, taps_ref, spread_ref, select_ref,
    ig_ref, db_ref, q_ref, r_ref, end_ref, taps_grad_ref, bias_grad_ref, head_ref,
    state_ref, ext_ref, high_ref, low_ref, x_ref, fall_v_ref, state_low_ref, ends_ref,
):
    g = pl.program_id(0)
    c = pl.num_programs(0) - 1 - g
    width = u_ref.shape[1]
    keep = keep_ref[c].astype(F32)

    @pl.when(g == 0)
    def _():
        state_ref[...] = leave_ref[...].astype(F32)
        taps_grad_ref[...] = jnp.zeros_like(taps_grad_ref)
        bias_grad_ref[...] = jnp.zeros_like(bias_grad_ref)
        ext_ref[LEN : LEN + 8, :] = jnp.zeros((8, width), F32)

    @pl.when(g > 0)
    def _():
        ext_ref[LEN : LEN + 8, :] = ext_ref[0:8, :] * keep_ref[c + 1].astype(F32)

    b_map, b_low = halves(b_ref[...])
    c_map, c_low = halves(c_ref[...])
    grow = split_pair(grow_ref[...])
    fall = split_pair(fall_ref[...])
    steps = split_pair(step_ref[...])

    def step(i, carry):
        at = chunk(i, WIDE)
        spread = spread_ref[:, at]
        state = state_ref[:, at]
        state_low = state.astype(BF16)
        falling = dot_nn(fall, spread)
        across = falling * (dot_nn(b_map, state_low)+dot_nn(b_low, state_low))
        dv = dv_ref[:, at] + across
        u = u_ref[:, at]
        open_ = sigmoid(u)
        x = u * open_
        delta = dot_nn(steps, spread)
        v = x * delta
        v_low = v.astype(BF16).astype(F32)
        dy = dy_ref[:, at].astype(F32)
        dx = delta * dv + skip_ref[:, at] * dy
        ext_ref[0:LEN, at] = dx * (open_ * (1.0 + u * (1.0 - open_)))
        high_ref[:, at], low_ref[:, at] = halves(v_low * dv)
        x_ref[:, at] = (x * dv).astype(BF16)
        carried = (
            local_ref[0, :, at].astype(F32) + pref_ref[0, :, at] * enter_ref[:, at].astype(F32)
        ).astype(BF16)
        decay = dec_ref[0, :, at]
        end = jnp.sum(v_low * across, axis=0, keepdims=True) + decay * jnp.sum(
            state * carried.astype(F32), axis=0, keepdims=True
        )
        ends_ref[:, at] = jnp.broadcast_to(end, (8, WIDE))
        fall_v_ref[:, at] = (falling * v).astype(BF16)
        state_low_ref[:, at] = state_low
        z = (dot_nn(grow, spread) * dy).astype(BF16)
        state_ref[:, at] = keep * (decay * state + (dot_tn(c_map, z)+dot_tn(c_low,z)))
        return carry

    lax.fori_loop(0, width // WIDE, step, 0, unroll=2)
    select = select_ref[...]
    db_ref[...] = dot_nt(fall_v_ref[...], state_low_ref[...])
    q_ref[...] = dot_nn(high_ref[...], select) + dot_nn(low_ref[...], select)
    r_ref[...] = dot_nn(x_ref[...], select)
    end_ref[0] = head_sums(ends_ref[...], select)

    def conv(i, carry):
        at = chunk(i, WIDE)
        ip = ip_ref[:, at]
        du = ext_ref[0:LEN, at]
        bias_grad_ref[:, at] += jnp.sum(du, axis=0, keepdims=True)
        total = taps_ref[3:4, at] * du
        taps_grad_ref[3:4, at] += jnp.sum(ip * du, axis=0, keepdims=True)
        for lag in range(1, 4):
            later = ext_ref[lag : lag + LEN, at]
            total = total + taps_ref[3 - lag : 4 - lag, at] * later
            taps_grad_ref[3 - lag : 4 - lag, at] += jnp.sum(ip * later, axis=0, keepdims=True)
        ig_ref[:, at] = total.astype(BF16)
        return carry

    lax.fori_loop(0, width // WIDE, conv, 0, unroll=3)

    @pl.when(c == 0)
    def _():
        head_ref[...] = ext_ref[0:8, :] * keep
        for lag in range(1, 4):
            part = keep * ext_ref[0:lag, :] * halo_ref[HALO - lag : HALO, :]
            taps_grad_ref[3 - lag : 4 - lag, :] += jnp.sum(part, axis=0, keepdims=True)


def place_kernel(moves, count, outs, where_ref, *refs):
    pieces, out_refs = refs[:count], refs[count : count + outs]
    stages, casts, sems = refs[count + outs : 2 * count + outs], refs[2 * count + outs : -1], refs[-1]
    loads = []
    for i, piece in enumerate(pieces):
        load = pltpu.make_async_copy(piece, stages[i], sems.at[0, i])
        load.start()
        loads.append(load)
    stores, waited = [], set()
    for n, (i, t, window, out, row_slot, col_slot) in enumerate(moves):
        if i not in waited:
            loads[i].wait()
            waited.add(i)
        first, rows, left, width = window
        source = stages[i].at[t, pl.ds(first, rows), pl.ds(left, width)]
        if casts:
            cast = casts[n]
            cast[...] = source[...].astype(cast.dtype)
            source = cast
        row = pl.multiple_of(where_ref[row_slot], 16)
        if width == out_refs[out].shape[1]:
            target = out_refs[out].at[pl.ds(row, rows)]
        else:
            col = pl.multiple_of(where_ref[col_slot], 128)
            target = out_refs[out].at[pl.ds(row, rows), pl.ds(col, width)]
        store = pltpu.make_async_copy(source, target, sems.at[1, n])
        store.start()
        stores.append(store)
    for store in stores:
        store.wait()


def place(pieces, moves, shapes, dtype):
    slots, fixed = [], []
    for i, t, window, which, row, col in moves:
        window = window or (0, pieces[i].shape[1], 0, pieces[i].shape[2])
        fixed.append((i, t, window, which, len(slots), len(slots) + 1))
        slots += [jnp.asarray(row, jnp.int32), jnp.asarray(col, jnp.int32)]
    anywhere = pl.BlockSpec(memory_space=pl.ANY)
    casts = []
    if dtype != pieces[0].dtype:
        casts = [pltpu.VMEM((w[1], w[3]), dtype) for _, _, w, _, _, _ in fixed]
    nbytes = sum(2 * 2 * a * b for a, b in shapes)
    return pl.pallas_call(
        functools.partial(place_kernel, fixed, len(pieces), len(shapes)),
        in_specs=[pl.BlockSpec(memory_space=pltpu.SMEM)] + [anywhere] * len(pieces),
        out_specs=[anywhere] * len(shapes),
        out_shape=[jax.ShapeDtypeStruct(shape, dtype) for shape in shapes],
        scratch_shapes=[pltpu.VMEM(piece.shape, piece.dtype) for piece in pieces]
        + casts
        + [pltpu.SemaphoreType.DMA((2, max(len(pieces), len(moves))))],
        compiler_params=pltpu.CompilerParams(vmem_limit_bytes=VMEM),
        cost_estimate=pl.CostEstimate(flops=0, bytes_accessed=nbytes, transcendentals=0),
        name="place",
    )(jnp.stack(slots), *pieces)


def norm_kernel(pieces_ref, gain_ref, hid_ref, normed_ref):
    parts, rows, width = pieces_ref.shape
    squares = jnp.zeros((rows, 128), F32)
    for t in range(parts):
        v = pieces_ref[t].astype(F32)
        squares = squares + fold(v * v)
    mean = jnp.sum(squares, axis=1, keepdims=True) / (width * parts)
    factor = lax.rsqrt(mean + EPSILON)
    for t in range(parts):
        at = slice(t * width, (t + 1) * width)
        v = pieces_ref[t]
        hid_ref[:, at] = v
        normed_ref[:, at] = (v.astype(F32) * factor * gain_ref[:, at]).astype(BF16)


def join_kernel(pieces_ref, live_ref, out_ref):
    parts, _, width = pieces_ref.shape
    for t in range(parts):
        live = live_ref[...]
        out_ref[:, t * width : (t + 1) * width] = (pieces_ref[t].astype(F32) * live).astype(BF16)


def swap(v, mask, count):
    return lax.ppermute(v, "dp", [(i, i ^ mask) for i in range(count)])


def exchange(v):
    return lax.all_to_all(v, "tensor", 0, 0, tiled=True)


def rotate(v, by, count):
    return lax.ppermute(v, "tensor", [(i, (i + by) % count) for i in range(count)])


def in_order(pieces, column):
    return jnp.roll(jnp.stack([pieces[0]] + pieces[:0:-1]), column, axis=0)


def same_core(count):
    return [list(range(0, count, 2)), list(range(1, count, 2))]


def gather_chips(v, count):
    return [(v, 0)] + [(swap(v, mask, count), mask) for mask in range(2, count, 2)]


def gather_core(mine, count):
    return mine + [(swap(a, 1, count), mask ^ 1) for a, mask in mine]


def gather_pieces(v, count):
    return gather_core(gather_chips(v, count), count)


ANYWHERE = pl.BlockSpec(memory_space=pl.ANY)


def unread(count, extra):
    return lambda kernel: lambda *refs: kernel(*refs[:count], *refs[count + extra :])


def after(v, *first):
    first = jax.tree.leaves(first)
    return pl.pallas_call(
        lambda *refs: None,
        in_specs=[ANYWHERE] * (1 + len(first)),
        out_specs=ANYWHERE,
        out_shape=jax.ShapeDtypeStruct(v.shape, v.dtype),
        input_output_aliases={0: 0},
        cost_estimate=pl.CostEstimate(flops=0, bytes_accessed=0, transcendentals=0),
        name="after",
    )(v, *first)


def pair_lanes(v):
    wide = jnp.pad(v, ((0, 0), (0, 64 - v.shape[1])))
    return jnp.concatenate([wide, wide], axis=1)


def local(
    dp_count, tensor_count,
    hidden_in, out_grad, seq_lengths, seq_device, seq_offset, norm_gain, w_gate, w_input, w_shared,
    w_step, conv_inner, conv_shared, conv_inner_bias, conv_shared_bias, step_bias, decay_log,
    skip_gain, gate_norm_gain, w_output,
):
    parts = tensor_count
    dp = lax.axis_index("dp")
    column = lax.axis_index("tensor")
    core, q = dp & 1, dp >> 1
    rows_dev, piece = hidden_in.shape
    rows = rows_dev // parts
    blocks = rows // LEN
    model = norm_gain.shape[0]
    shard = w_input.shape[1]
    inner = shard * parts
    heads_shard = w_step.shape[1]
    heads = heads_shard * parts
    width = inner // heads
    nstate = w_shared.shape[1] // 2
    groups = dp_count // 2

    aligned = piece % 128 == 0
    turn = jnp.stack([(column - d) % parts for d in range(parts)]).astype(jnp.int32)

    def send_rows(v, halo):
        pieces = []
        for t in range(parts):
            pieces.append(v[t * rows : (t + 1) * rows])
            if halo:
                start = max(t * rows, HALO)
                pieces.append(v[start - HALO : start])
        size = rows + (HALO if halo else 0)
        return exchange(jnp.concatenate(pieces, axis=0).reshape(parts, size, piece))

    def send_back(v):
        pieces = [v[:, t * piece : (t + 1) * piece] for t in range(parts)]
        return jnp.stack(pieces)

    def row_block(size):
        return max(n for n in range(16, 129, 16) if size % n == 0)

    def join(kernel, pieces, extra, extra_rows, outs):
        size = pieces.shape[1]
        block = row_block(size)
        extra_spec = (
            pl.BlockSpec((block, 1), lambda g: (g, 0))
            if extra_rows
            else pl.BlockSpec(extra.shape, lambda g: (0, 0))
        )
        wide = pl.BlockSpec((block, model), lambda g: (g, 0))
        return pl.pallas_call(
            kernel,
            grid=(size // block,),
            in_specs=[pl.BlockSpec((parts, block, piece), lambda g: (0, g, 0)), extra_spec],
            out_specs=[wide] * outs,
            out_shape=[jax.ShapeDtypeStruct((size, model), BF16)] * outs,
            compiler_params=pltpu.CompilerParams(vmem_limit_bytes=VMEM),
            cost_estimate=pl.CostEstimate(
                flops=0, bytes_accessed=size * model * 2 * (1 + outs), transcendentals=0
            ),
            name="join",
        )(pieces, extra)

    def join_plain(pieces):
        return jnp.concatenate([pieces[t] for t in range(parts)], axis=1)

    k_rows = model // dp_count
    out_rows = shard // dp_count

    def slices_of(index):
        return index & 1, index >> 1

    def gather_all(v):
        return lax.all_gather(v, ("dp", "tensor"), axis=0)

    def my_rows(w, size):
        return lax.dynamic_slice_in_dim(w, dp * size, size, 0)

    def place_columns(slices):
        moves = [
            (0, j, None, 0, j // parts * k_rows, j % parts * shard) for j in range(slices.shape[0])
        ]
        return place([slices], moves, [(model, inner)], BF16)[0]

    def place_output(slices):
        moves = [
            (0, j, None, 0, j % parts * shard + j // parts * out_rows, 0)
            for j in range(slices.shape[0])
        ]
        return place([slices], moves, [(inner, model)], BF16)[0]

    place_dp = core * (model // 2) + q * k_rows

    vectors = jnp.concatenate([step_bias, decay_log, skip_gain])
    vectors = jnp.pad(vectors, (0, shard - vectors.shape[0]))[None, :]
    small = jnp.concatenate(
        [conv_inner, conv_inner_bias[None, :], gate_norm_gain[None, :], vectors], axis=0
    )
    terms = []
    for _ in range(3):
        term = lax.reduce_precision(small, 8, 7)
        terms.append(term.astype(BF16))
        small = small - term
    step_rows = model * heads_shard // shard
    small = jnp.concatenate(terms + [w_step.reshape(step_rows, shard)], axis=0)
    small_rows = -(-small.shape[0] // 16) * 16
    small = jnp.pad(small, ((0, small_rows - small.shape[0]), (0, 0)))
    first = lax.dynamic_slice_in_dim(w_input, place_dp, k_rows, 0)
    first = jnp.concatenate([first, small], axis=0)
    first = [first] + [rotate(first, d, parts) for d in range(1, parts)]
    hid_pieces = send_rows(hidden_in, True)
    small = in_order([v[k_rows:] for v in first], column)
    in_pieces = gather_pieces(jnp.stack([v[:k_rows] for v in first]), dp_count)
    terms = small[:, :21].astype(F32).reshape(parts, 3, 7, shard)
    terms = (terms[:, 0] + terms[:, 1]) + terms[:, 2]
    by_shard = lambda v: jnp.swapaxes(v, 0, 1).reshape(v.shape[1], inner)
    taps = by_shard(terms[:, :4])
    inner_bias = by_shard(terms[:, 4:5])
    gain_out = by_shard(terms[:, 5:6])
    by_head = lambda i: terms[:, 6, i * heads_shard : (i + 1) * heads_shard].reshape(1, heads)
    steps_bias = pair_lanes(by_head(0))
    logs = pair_lanes(by_head(1))
    skip_wide = jnp.repeat(by_head(2), width, axis=1)
    w_steps = small[:, 21 : 21 + step_rows].reshape(parts, model, heads_shard)
    w_steps = jnp.swapaxes(w_steps, 0, 1).reshape(model, heads)
    w_misc = jnp.concatenate([w_shared, pair_lanes(w_steps)], axis=1)
    misc_width = w_misc.shape[1]

    block_start = column * rows + jnp.arange(blocks + 1, dtype=jnp.int32) * LEN
    inside = (
        (seq_device[None, :] == dp)
        & (block_start[:, None] >= seq_offset[None, :])
        & (block_start[:, None] < seq_offset[None, :] + seq_lengths[None, :])
    )
    offset = jnp.sum(jnp.where(inside, block_start[:, None] - seq_offset[None, :], 0), axis=1)
    keep = (offset > 0).astype(jnp.int32)
    live_blocks = jnp.sum(inside.astype(F32), axis=1)[:blocks]
    live = jnp.repeat(live_blocks, LEN)[:, None]
    dev_start = jnp.arange(rows_dev // LEN, dtype=jnp.int32) * LEN
    dev_inside = (
        (seq_device[None, :] == dp)
        & (dev_start[:, None] >= seq_offset[None, :])
        & (dev_start[:, None] < seq_offset[None, :] + seq_lengths[None, :])
    )
    live_dev = jnp.repeat(jnp.sum(dev_inside.astype(F32), axis=1), LEN)[:, None]

    lane_head = jnp.arange(inner, dtype=jnp.int32) // width
    half_index = jnp.arange(128, dtype=jnp.int32) % 64
    spread = (half_index[:, None] == lane_head[None, :]).astype(BF16)
    select = (lane_head[:, None] == jnp.arange(128, dtype=jnp.int32)[None, :]).astype(BF16)
    columns = (
        (jnp.arange(192, dtype=jnp.int32) % 64)[:, None]
        == (jnp.arange(heads * LEN, dtype=jnp.int32) // LEN)[None, :]
    ).astype(BF16)

    if aligned:
        hid, normed_all = join(norm_kernel, hid_pieces, norm_gain[None, :], False, 2)
    else:
        hid = join_plain(hid_pieces)
        wide_in = hid.astype(F32)
        mean = jnp.mean(wide_in * wide_in, axis=1, keepdims=True)
        normed_all = (wide_in * lax.rsqrt(mean + EPSILON) * norm_gain[None, :]).astype(BF16)
    normed = normed_all[:rows]
    misc = dot_nn(normed_all, w_misc)

    params = pltpu.CompilerParams(vmem_limit_bytes=VMEM)
    smem = pl.BlockSpec(memory_space=pltpu.SMEM)
    full = lambda *shape: pl.BlockSpec(shape, lambda g: (0,) * len(shape))
    up = lambda *shape: pl.BlockSpec(shape, lambda g: (g,) + (0,) * (len(shape) - 1))
    down = lambda *shape: pl.BlockSpec(
        shape, lambda g: (blocks - 1 - g,) + (0,) * (len(shape) - 1)
    )
    out = jax.ShapeDtypeStruct
    cost = lambda flops, size: pl.CostEstimate(
        flops=flops, bytes_accessed=size, transcendentals=rows * inner
    )
    halo_block = lambda cols: pl.BlockSpec((HALO, cols), lambda g: (rows // HALO, 0))
    wide_map = 2 * rows * inner * nstate
    lanes = out((rows, 128), F32)

    (
        shared_u, b_map, c_map, delta2, slope2, rate2, cum3, cum_t, grow2, fall2, coef2, dec2,
    ) = pl.pallas_call(
        maps_kernel,
        grid=(blocks,),
        in_specs=[
            smem, up(LEN, misc_width), halo_block(misc_width), full(4, 2 * nstate),
            full(1, 2 * nstate), full(1, 128), full(1, 128),
        ],
        out_specs=[up(LEN, 2 * nstate)]
        + [up(LEN, 128)] * 5
        + [up(LEN, 192), pl.BlockSpec((128, LEN), lambda g: (0, g))]
        + [up(LEN, 128)] * 3
        + [up(1, 1, 128)],
        out_shape=[out((rows, 2 * nstate), F32)]
        + [lanes] * 5
        + [out((rows, 192), F32), out((128, rows), F32)]
        + [lanes] * 3
        + [out((blocks, 1, 128), F32)],
        scratch_shapes=[pltpu.VMEM((LEN + 8, 2 * nstate), F32)],
        compiler_params=params,
        cost_estimate=cost(0, rows * 128 * 4 * 16),
        name="maps",
    )(keep, misc, misc, conv_shared, conv_shared_bias[None, :], steps_bias, logs)

    moves = []
    for i, (_, mask) in enumerate(in_pieces):
        c2, q2 = slices_of(dp ^ mask)
        row = c2 * (model // 2) + q2 * k_rows
        moves += [(i, d, None, 0, row, turn[d] * shard) for d in range(parts)]
    moves.append((len(in_pieces), 0, None, 0, 0, inner))
    (w_in,) = place(
        [a for a, _ in in_pieces] + [w_misc[None]], moves, [(model, inner + misc_width)], BF16
    )
    gate_slices = gather_all(after(my_rows(w_gate, k_rows), *first[1:]))
    out_slices = None
    if out_rows % 16 == 0:
        out_slices = gather_all(after(my_rows(w_output, out_rows), *first[1:]))
    grad_pieces = send_rows(out_grad, False)
    inner_proj = dot_nn(normed_all, w_in[:, :inner])


    u, local_states, chunk_state, dec_wide, pref_wide, through = pl.pallas_call(
        conv_states_kernel,
        grid=(blocks,),
        in_specs=[
            smem, up(LEN, inner), halo_block(inner), full(4, inner), full(1, inner),
            up(LEN, nstate), up(LEN, 128), up(1, 1, 128), full(128, inner),
        ],
        out_specs=[
            up(LEN, inner), up(1, nstate, inner), full(nstate, inner), up(1, 1, inner),
            up(1, 1, inner), full(1, inner),
        ],
        out_shape=[
            out((rows, inner), F32), out((blocks, nstate, inner), BF16), out((nstate, inner), F32),
            out((blocks, 1, inner), F32), out((blocks, 1, inner), F32), out((1, inner), F32),
        ],
        scratch_shapes=[
            pltpu.VMEM((LEN + 8, inner), F32), pltpu.VMEM((nstate, inner), F32),
            pltpu.VMEM((1, inner), F32),
        ],
        compiler_params=params,
        cost_estimate=cost(2 * wide_map, rows * inner * 12),
        name="conv_states",
    )(keep, inner_proj, inner_proj, taps, inner_bias, b_map, coef2, dec2, spread)

    to_right = [(i, i + 1) for i in range(parts - 1)]
    to_left = [(i + 1, i) for i in range(parts - 1)]
    entering = lax.ppermute(chunk_state.astype(BF16), "tensor", to_right)

    heads_t = pl.BlockSpec((128, LEN), lambda g: (0, g))
    y_within = pl.pallas_call(
        within_kernel,
        grid=(blocks,),
        in_specs=[
            up(LEN, inner), up(LEN, 192), heads_t, up(LEN, 128), up(LEN, nstate),
            up(LEN, nstate), full(192, heads * LEN), full(128, inner),
        ],
        out_specs=up(LEN, inner),
        out_shape=out((rows, inner), F32),
        compiler_params=params,
        cost_estimate=cost(8 * wide_map, rows * inner * 8),
        name="within",
    )(
        u, cum3, cum_t, delta2, b_map, c_map, columns, spread
    )

    w_gates = place_columns(gate_slices)
    gate_proj = dot_nn(normed, w_gates)
    beside = [y_within, gate_proj]
    for i in range(parts - 2):
        entering = after(entering, *beside[i : i + 1])
        entering = lax.ppermute(
            (chunk_state + through * entering.astype(F32)).astype(BF16), "tensor", to_right
        )
    if out_slices is None:
        w_out = lax.all_gather(w_output, "tensor", axis=0, tiled=True)
    else:
        w_out = place_output(out_slices)

    if aligned:
        (masked,) = join(join_kernel, grad_pieces, live, True, 1)
    else:
        masked = join_plain(grad_pieces) * live.astype(BF16)
    normed_y_grad = dot_nt(masked, w_out)

    normed_y, scan_grad, gate_grad, q_plus, dc_across, gain_out_grad, skip_lanes, chunk_grad = (
        pl.pallas_call(
            gate_kernel,
            grid=(blocks,),
            in_specs=[
                smem, down(LEN, inner), down(LEN, inner), down(LEN, inner), down(LEN, inner),
                down(1, nstate, inner), full(nstate, inner), down(1, 1, inner), down(LEN, nstate),
                down(LEN, 128), full(1, inner), full(1, inner), down(1, 1, inner),
                full(128, inner), full(inner, 128),
            ],
            out_specs=[
                down(LEN, inner), down(LEN, inner), down(LEN, inner), down(LEN, 128),
                down(LEN, nstate), full(1, inner), full(1, inner), full(nstate, inner),
            ],
            out_shape=[
                out((rows, inner), BF16), out((rows, inner), BF16), out((rows, inner), BF16),
                lanes, out((rows, nstate), F32), out((1, inner), F32),
                out((1, inner), F32), out((nstate, inner), F32),
            ],
            scratch_shapes=[
                pltpu.VMEM((LEN, inner), F32), pltpu.VMEM((nstate, inner), BF16),
                pltpu.VMEM((nstate, inner), F32),
            ]
            + [pltpu.VMEM((LEN, inner), BF16)] * 3,
            compiler_params=params,
            cost_estimate=cost(6 * wide_map, rows * inner * 24),
            name="gate",
        )(
            keep, y_within, u, gate_proj, normed_y_grad, local_states, entering, pref_wide, c_map,
            grow2, skip_wide, gain_out, dec_wide, spread, select,
        )
    )

    leaving = lax.ppermute(chunk_grad.astype(BF16), "tensor", to_left)

    def half_of(v, which):
        size = v.shape[1] // 2
        return lax.dynamic_slice_in_dim(v, which * size, size, 1)

    out_sent = swap(dot_tn(normed_y, half_of(masked, 1 - core)).astype(BF16), 1, dp_count)
    gate_sent = swap(dot_tn(half_of(normed, 1 - core), gate_grad).astype(BF16), 1, dp_count)
    gate_part = dot_nt(gate_grad, w_gates)
    mixed_rows = dot_nn(normed_y, w_out).astype(BF16)
    out_total = (dot_tn(normed_y, half_of(masked, core)) + out_sent.astype(F32)).astype(BF16)
    beside = [[gate_part], [out_total, mixed_rows]]
    for i in range(parts - 2):
        leaving = after(leaving, *(beside[i] if i < len(beside) else []))
        if i == 1:
            mixed_sent = after(send_back(mixed_rows), leaving)
        leaving = lax.ppermute(
            (chunk_grad + through * leaving.astype(F32)).astype(BF16), "tensor", to_left
        )
    gate_total = (dot_tn(half_of(normed, core), gate_grad) + gate_sent.astype(F32)).astype(BF16)
    out_group = shard // groups
    group_rows = model // dp_count
    half_model = model // 2

    def chip_sum(v):
        return lax.psum_scatter(
            v, "dp", scatter_dimension=0, axis_index_groups=same_core(dp_count), tiled=False
        )

    def shard_sum(v):
        mine = lax.psum_scatter(v, "tensor", scatter_dimension=0, tiled=False)
        return lax.all_gather(mine, "dp", axis=0)

    out_sum = chip_sum(
        jnp.swapaxes(out_total.reshape(parts, groups, out_group, half_model), 0, 1)
    )
    gate_sum = chip_sum(gate_total.reshape(groups, group_rows, inner))
    out_parts = shard_sum(out_sum)
    gate_parts = shard_sum(
        jnp.stack([gate_sum[:, t * shard : (t + 1) * shard] for t in range(parts)])
    )

    dv_within, db_within, dc_within = pl.pallas_call(
        unread(9, 1)(within_back_kernel),
        grid=(blocks,),
        in_specs=[
            up(LEN, inner), up(LEN, inner), up(LEN, 192), heads_t, up(LEN, 128), up(LEN, nstate),
            up(LEN, nstate), full(192, heads * LEN), full(128, inner), ANYWHERE,
        ],
        out_specs=[up(LEN, inner), up(LEN, nstate), up(LEN, nstate)],
        out_shape=[out((rows, inner), F32), out((rows, nstate), F32), out((rows, nstate), F32)],
        compiler_params=params,
        cost_estimate=cost(16 * wide_map, rows * inner * 10),
        name="within_back",
    )(u, scan_grad, cum3, cum_t, delta2, b_map, c_map, columns, spread, gate_part)


    grads, db_across, q_minus, step_sums, end_sums, taps_grad, bias_grad, head_rows = (
        pl.pallas_call(
            across_back_kernel,
            grid=(blocks,),
            in_specs=[
                smem, down(LEN, inner), down(LEN, inner), down(LEN, inner), down(LEN, inner),
                halo_block(inner), down(1, nstate, inner), full(nstate, inner), down(1, 1, inner),
                full(nstate, inner), down(LEN, nstate), down(LEN, nstate), down(LEN, 128),
                down(LEN, 128), down(LEN, 128), full(1, inner), down(1, 1, inner), full(4, inner),
                full(128, inner), full(inner, 128),
            ],
            out_specs=[
                down(LEN, inner), down(LEN, nstate), down(LEN, 128), down(LEN, 128),
                down(1, 8, 128), full(4, inner), full(1, inner), full(8, inner),
            ],
            out_shape=[
                out((rows, inner + misc_width), BF16), out((rows, nstate), F32), lanes, lanes,
                out((blocks, 8, 128), F32), out((4, inner), F32), out((1, inner), F32),
                out((8, inner), F32),
            ],
            scratch_shapes=[
                pltpu.VMEM((nstate, inner), F32), pltpu.VMEM((LEN + 8, inner), F32),
            ]
            + [pltpu.VMEM((LEN, inner), BF16)] * 5
            + [pltpu.VMEM((8, inner), F32)],
            compiler_params=params,
            cost_estimate=cost(6 * wide_map, rows * inner * 20),
            name="across_back",
        )(
            keep, u, scan_grad, dv_within, inner_proj, inner_proj, local_states,
            entering, pref_wide, after(leaving, dv_within, gate_total), b_map, c_map, grow2, fall2, delta2, skip_wide, dec_wide, taps,
            spread, select,
        )
    )

    misc_at = inner // misc_width
    mixer_part = exchange(mixed_sent)
    grads, shared_taps_grad, shared_bias_grad, shared_head, vectors = pl.pallas_call(
        unread(17, 1)(maps_back_kernel),
        grid=(blocks,),
        in_specs=[
            smem, down(LEN, nstate), down(LEN, nstate), down(LEN, nstate), down(LEN, nstate),
            down(LEN, 2 * nstate), down(LEN, misc_width), halo_block(misc_width),
            full(4, 2 * nstate), down(LEN, 128), down(LEN, 128), down(LEN, 128), down(1, 8, 128),
            down(LEN, 128), down(LEN, 128), full(1, 128), ANYWHERE, ANYWHERE,
        ],
        out_specs=[
            pl.BlockSpec((LEN, misc_width), lambda g: (blocks - 1 - g, misc_at)),
            full(4, 2 * nstate), full(1, 2 * nstate), full(8, 2 * nstate), full(8, 128),
        ],
        out_shape=[
            out((rows, inner + misc_width), BF16), out((4, 2 * nstate), F32),
            out((1, 2 * nstate), F32), out((8, 2 * nstate), F32), out((8, 128), F32),
        ],
        input_output_aliases={16: 0},
        scratch_shapes=[pltpu.VMEM((LEN + 8, 2 * nstate), F32)],
        compiler_params=params,
        cost_estimate=cost(0, rows * 128 * 4 * 16),
        name="maps_back",
    )(
        keep, db_within, db_across, dc_within, dc_across, shared_u, misc, misc, conv_shared,
        q_plus, q_minus, step_sums, end_sums, slope2, rate2, logs, grads, mixer_part,
    )
    mixer_part = mixer_part.reshape(rows_dev, piece).astype(F32)
    mixed_out = (hidden_in.astype(F32) + live_dev * mixer_part).astype(BF16)

    next_heads = lax.ppermute(
        jnp.concatenate([head_rows, shared_head], axis=1), "tensor", to_left
    )
    all_taps = jnp.concatenate([taps, conv_shared], axis=1)
    reach = inner + 2 * nstate
    last_rows = lax.dynamic_slice(grads, (rows - 16, 0), (16, reach)).astype(F32)
    for lag in range(1, 4):
        moved = jnp.pad(next_heads[:lag], ((16 - lag, 0), (0, 0)))
        last_rows = last_rows + all_taps[3 - lag][None, :] * moved
    grads = lax.dynamic_update_slice(grads, last_rows.astype(BF16), (rows - 16, 0))

    in_sent = swap(dot_tn(half_of(normed, 1 - core), grads).astype(BF16), 1, dp_count)
    normed_grad = gate_part + dot_nt(grads, w_in)
    input_grad, norm_gain_grad = pl.pallas_call(
        input_grad_kernel,
        grid=(blocks,),
        in_specs=[up(LEN, model), up(LEN, model), full(1, model)],
        out_specs=[up(LEN, model), full(1, model)],
        out_shape=[out((rows, model), BF16), out((1, model), F32)],
        compiler_params=params,
        cost_estimate=cost(0, rows * model * 8),
        name="input_grad",
    )(normed_grad, hid, norm_gain[None, :])

    tiny = jnp.concatenate(
        [
            shared_taps_grad.reshape(1, -1), shared_bias_grad, vectors[0:1], vectors[1:2],
            norm_gain_grad,
        ],
        axis=1,
    )
    tiny = jnp.pad(tiny, ((0, 0), (0, inner - tiny.shape[1])))
    tiny = jnp.concatenate([taps_grad, bias_grad, gain_out_grad, skip_lanes, tiny], axis=0)
    tiny = tiny + swap(tiny, 1, dp_count)

    def two_terms(v):
        high = lax.reduce_precision(v, 8, 7)
        return jnp.concatenate([high, v - high], axis=0).astype(BF16)

    def one_term(v):
        return v[:8].astype(F32) + v[8:].astype(F32)

    in_total = (dot_tn(half_of(normed, core), grads) + in_sent.astype(F32)).astype(BF16)
    tiny_low = jnp.pad(two_terms(tiny), ((0, 0), (0, misc_width)))
    in_part = lambda which: jnp.concatenate(
        [lax.dynamic_slice_in_dim(in_total, which * k_rows, k_rows, 0), tiny_low], axis=0
    )
    in_received = [in_part(q)]
    for mask in range(1, groups):
        in_received.append(swap(in_part(q ^ mask), 2 * mask, dp_count))
    tiny = [one_term(v[k_rows:, :inner]) for v in in_received]
    while len(tiny) > 1:
        tiny = [tiny[i] + tiny[i + 1] for i in range(0, len(tiny), 2)]
    tiny_low = two_terms(tiny[0])
    in_group = in_received[0][:k_rows].astype(F32)
    for v in in_received[1:]:
        in_group = in_group + v[:k_rows].astype(F32)
    in_group = in_group.astype(BF16)
    cols = shard + misc_width
    lengths = -(-inner // cols)
    tiny_low = jnp.pad(tiny_low, ((0, 0), (0, lengths * cols - inner)))
    tiny_low = jnp.concatenate([tiny_low[:, i * cols : (i + 1) * cols] for i in range(lengths)])
    in_sends = []
    for t in range(parts):
        mine = [in_group[:, t * shard : (t + 1) * shard], in_group[:, inner:]]
        in_sends.append(jnp.concatenate([jnp.concatenate(mine, axis=1), tiny_low], axis=0))
    hidden_sent = send_back(input_grad)
    hidden_part = exchange(hidden_sent)
    in_arrived = exchange(jnp.stack(in_sends))
    in_shard = jnp.sum(in_arrived[:, :k_rows].astype(F32), axis=0).astype(BF16)
    tiny_low = in_arrived[:, k_rows:].reshape(parts, lengths, 2, 8, cols).astype(F32)
    tiny = jnp.sum(tiny_low[:, :, 0] + tiny_low[:, :, 1], axis=0)
    tiny = jnp.concatenate([tiny[i] for i in range(lengths)], axis=1)
    own_columns = lax.dynamic_slice_in_dim(tiny[:7], column * shard, shard, 1)
    ends_at = [0]
    for size in (8 * nstate, 2 * nstate, 128, 128, model):
        ends_at.append(ends_at[-1] + size)
    part = lambda i: tiny[7, ends_at[i] : ends_at[i + 1]]
    own_heads = lambda v: lax.dynamic_slice_in_dim(v, column * heads_shard, heads_shard, 0)

    w_output_grad = (
        out_parts.reshape(groups, 2, out_group, half_model)
        .transpose(0, 2, 1, 3)
        .reshape(shard, model)
        .astype(F32)
    )
    w_gate_grad = (
        gate_parts.reshape(groups, 2, group_rows, shard)
        .transpose(1, 0, 2, 3)
        .reshape(model, shard)
        .astype(F32)
    )
    in_pieces = gather_pieces(in_shard[None], dp_count)
    moves = []
    for i, (_, mask) in enumerate(in_pieces):
        c2, q2 = slices_of(dp ^ mask)
        row = c2 * half_model + q2 * k_rows
        moves.append((i, 0, (0, k_rows, 0, shard), 0, row, 0))
        moves.append((i, 0, (0, k_rows, shard, 2 * nstate), 1, row, 0))
        moves.append((i, 0, (0, k_rows, shard + 2 * nstate, 128), 2, row, 0))
    w_input_grad, w_shared_grad, step_lanes = place(
        [a for a, _ in in_pieces],
        moves,
        [(model, shard), (model, 2 * nstate), (model, 128)],
        F32,
    )
    w_step_grad = lax.dynamic_slice_in_dim(step_lanes, column * heads_shard, heads_shard, 1)
    hidden_grad = hidden_part.reshape(rows_dev, piece).astype(F32) + out_grad.astype(F32)

    return (
        mixed_out,
        hidden_grad,
        part(4),
        w_gate_grad,
        w_input_grad,
        w_shared_grad,
        w_step_grad,
        own_columns[:4],
        part(0).reshape(4, 2 * nstate),
        own_columns[4],
        part(1),
        own_heads(part(2)),
        own_heads(part(3)),
        jnp.sum(own_columns[6].reshape(heads_shard, width), axis=1),
        own_columns[5],
        w_output_grad,
    )


def solution(mesh):
    split = P("tensor")
    in_specs = (
        P("dp", "tensor"), P("dp", "tensor"), P(), P(), P(), P(), P(None, "tensor"),
        P(None, "tensor"), P(), P(None, "tensor"), P(None, "tensor"), P(), split, P(), split,
        split, split, split, P("tensor", None),
    )
    out_specs = (
        P("dp", "tensor"), P("dp", "tensor"), P(), P(None, "tensor"), P(None, "tensor"), P(),
        P(None, "tensor"), P(None, "tensor"), P(), split, P(), split, split, split, split,
        P("tensor", None),
    )
    body = functools.partial(local, mesh.shape["dp"], mesh.shape["tensor"])
    return jax.shard_map(body, mesh=mesh, in_specs=in_specs, out_specs=out_specs, check_vma=False)
```

time: 1140 us -> 816 us (0.72)
  starting transfers between devices: 234 us -> 56.9 us
  local copies, waits for them, and re-layouts: 143 us -> 58.6 us
  Pallas kernels: 290 us -> 241 us
  other arithmetic: 82.3 us -> 48.2 us
  between operations: 3.61 us -> 16.4 us
    ppermute x36 -> x3, starting transfers between devices: 162 us -> 6.06 us  [rotate(): lax.ppermute(v, 'tensor', [(i, (i + by) % count) for i in range(count)])]
    ppermute x36 -> x3, waiting for transfers between devices: 141 us -> 28.9 us  [rotate(): lax.ppermute(v, 'tensor', [(i, (i + by) % count) for i in range(count)])]
    ppermute x73 -> x22, waiting for transfers between devices: 94.6 us -> 143 us  [the longest x21 127 us: swap(): return lax.ppermute(v, 'dp', [(i, i ^ mask) for i in range(count)])]
    all_to_all x0 -> x5, waiting for transfers between devices: none -> 44 us  [exchange(): return lax.all_to_all(v, 'tensor', 0, 0, tiled=True)]
    ppermute x73 -> x22, starting transfers between devices: 53.3 us -> 13.5 us  [the longest x21 12 us: swap(): return lax.ppermute(v, 'dp', [(i, i ^ mask) for i in range(count)])]
    slice x41 -> x14, local copies, waits for them, and re-layouts: 36.9 us -> 3.56 us  [the longest x1 1.05 us: local(): in_arrived[:, k_rows:].reshape(parts, lengths, 2, 8, cols).astype(F32)]
    all_to_all x0 -> x5, starting transfers between devices: none -> 22 us  [exchange(): return lax.all_to_all(v, 'tensor', 0, 0, tiled=True)]
    pallas_call x1, Pallas kernels: 64.9 us -> 50.3 us  [local(): pl.pallas_call(across_back_kernel, grid=(blocks,), in_specs=[smem, down(L...]
  transfers between devices with their start and end apart: 115 -> 44, of which waited for: 30 -> 21; matrix products, arithmetic and copies ran while one was open for 29% -> 26% of each run, Pallas kernels for 20% -> 24%
where the time goes in v2:
time: 816 us; the launch traced here: 810 us
  waiting for transfers between devices  256 us (31%)
  Pallas kernels  241 us (30%)
  matrix products  132 us (16%)
  local copies, waits for them, and re-layouts  58.6 us (7%)
  starting transfers between devices  56.9 us (7%)
  other arithmetic  48.2 us (6%)
  between operations  16.4 us (2%)
    ppermute x21, waiting for transfers between devices, swap(): return lax.ppermute(v, 'dp', [(i, i ^ mask) for i in range(count)])  127 us
    dot_general x6, matrix products, dot_tn(): lax.dot_general(a, b, (((0,), (0,)), ((), ())), preferred_element_type=F32)  55.5 us
    pallas_call x1, Pallas kernels, local(): pl.pallas_call(across_back_kernel, grid=(blocks,), in_specs=[smem, down(L...  50.3 us
    pallas_call x1, Pallas kernels, local(): pl.pallas_call(gate_kernel, grid=(blocks,), in_specs=[smem, down(LEN, inn...  44.5 us
    all_to_all x5, waiting for transfers between devices, exchange(): return lax.all_to_all(v, 'tensor', 0, 0, tiled=True)  44 us
    dot_general x3, matrix products, dot_nt(): lax.dot_general(a, b, (((1,), (1,)), ((), ())), preferred_element_type=F32)  38.5 us
    dot_general x4, matrix products, dot_nn(): return jnp.dot(a, b, preferred_element_type=F32)  38.2 us
    pallas_call x1, Pallas kernels, local(): pl.pallas_call(within_kernel, grid=(blocks,), in_specs=[up(LEN, inner), u...  32.9 us
  transfers between devices with their start and end apart: 44, of which 21 were waited for; matrix products, arithmetic and copies ran while one was open for 26% of the time, Pallas kernels for 24%

profile of v2, /device:TPU:0, one launch (start us, length us, event | category | flops | bytes accessed | tf_op | source)
XLA Modules:
  0.0 809.8 jit_solution(9835164667227811877)
XLA Ops:
  27.2 22.3 %collective-permute-done.1.refs_2_ = bf16[240,768]{1,0:T(8,128)(2,1)S(1)} collective-permute-done((bf16[240,768]{1,0:T(8,128)(2,1)}, bf16[240,768]{1,0:T(8,128)(2,1)S(1)}, u32[]{:S(2)}, u32[]{:S(2)}) %collective-permute-start.1) | collective-permute-done | bytes 368672 | tf_op jit(solution)/shard_map/ppermute | solution.py:576
  71.6 30.3 %collective-permute-done.3.refs_1_ = bf16[4,192,768]{2,1,0:T(8,128)(2,1)} collective-permute-done((bf16[4,192,768]{2,1,0:T(8,128)(2,1)S(1)}, bf16[4,192,768]{2,1,0:T(8,128)(2,1)}, u32[]{:S(2)}, u32[]{:S(2)}) %collective-permute-start.3) | collective-permute-done | bytes 1179680 | tf_op jit(solution)/shard_map/ppermute | solution.py:568
  102.4 27.0 %collective-permute-done.5.refs_3_ = bf16[4,192,768]{2,1,0:T(8,128)(2,1)} collective-permute-done((bf16[4,192,768]{2,1,0:T(8,128)(2,1)S(1)}, bf16[4,192,768]{2,1,0:T(8,128)(2,1)}, u32[]{:S(2)}, u32[]{:S(2)}) %collective-permute-start.5) | collective-permute-done | bytes 1179680 | tf_op jit(solution)/shard_map/ppermute | solution.py:568
  149.3 9.1 %place.4 = bf16[1536,3456]{1,0:T(8,128)(2,1)} custom-call(s32[66]{0:T(128)S(1)} %stack.98.where_ref, bf16[4,192,768]{2,1,0:T(8,128)(2,1)S(1)} %pad_maximum_fusion.6.refs_0_, bf16[4,192,768]{2,1,0:T(8,128)(2,1)} %collective-permute-done.3.refs_1_, bf16[4,192,768]{2,1,0:T(8,128)(2,1)} %collective-permute-done.4.refs_2_, ...), custom_call_target="tpu_custom_call" | custom-call | bytes 21233664 | tf_op jit(solution)/shard_map/place/pallas_call | solution.py:531
  174.5 13.0 %fusion.ip_ref.halo_ref = f32[784,3072]{1,0:T(8,128)} fusion(bf16[784,1536]{1,0:T(8,128)(2,1)S(1)} %copy-done.43, bf16[1536,3456]{1,0:T(8,128)(2,1)} %place.4), kind=kOutput, calls=%fused_computation.1 | convolution fusion | flops 7398752256 | bytes 21479424 | tf_op jit(solution)/shard_map/dot_general | solution.py:21
  187.6 19.3 %conv_states.1 = (f32[768,3072]{1,0:T(8,128)}, bf16[6,128,3072]{2,1,0:T(8,128)(2,1)}, f32[128,3072]{1,0:T(8,128)}, f32[6,1,3072]{2,1,0:T(1,128)S(1)}, f32[6,1,3072]{2,1,0:T(1,128)S(1)}, /*index=5*/f32[1,3072]{1,0:T(1,128)S(1)}) custom-call(s32[7]{0:T(128)S(1)} %compare_convert_fusion.2.keep_ref.refs_0_, f32[784,3072]{1,0:T(8,128)} %fusion.ip_ref.halo_ref, ...), custom_call_target="tpu_custom_call" | custom-call | flops 1207959552 | bytes 28311552 | tf_op jit(solution)/shard_map/conv_states/pallas_call | solution.py:847
  224.5 32.9 %within.1.refs_1_.y_ref = f32[768,3072]{1,0:T(8,128)} custom-call(f32[768,3072]{1,0:T(8,128)} %get-tuple-element.69.u_ref.refs_0_, f32[768,192]{1,0:T(8,128)} %get-tuple-element.70.cum_ref.refs_2_, f32[128,768]{1,0:T(8,128)S(1)} %copy-done.8, f32[768,128]{1,0:T(8,128)S(1)} %get-tuple-element.72.step_ref.refs_4_, ...), custom_call_target="tpu_custom_call" | custom-call | flops 4831838208 | bytes 18874368 | tf_op jit(solution)/shard_map/within/pallas_call | solution.py:876
  261.8 8.6 %place.5 = bf16[1536,3072]{1,0:T(8,128)(2,1)} custom-call(s32[64]{0:T(128)S(1)} %copy-done.19, bf16[32,192,768]{2,1,0:T(8,128)(2,1)} %bitcast.201), custom_call_target="tpu_custom_call" | custom-call | bytes 18874368 | tf_op jit(solution)/shard_map/place/pallas_call | solution.py:531
  270.5 12.1 %fusion.63.refs_1_.gate_ref = f32[768,3072]{1,0:T(8,128)} fusion(bf16[1536,3072]{1,0:T(8,128)(2,1)} %place.5, bf16[784,1536]{1,0:T(8,128)(2,1)S(1)} %copy-done.45), kind=kOutput, calls=%fused_computation.221 | convolution fusion | flops 7247757312 | bytes 21233664 | tf_op jit(solution)/shard_map/dot_general | solution.py:21
  296.3 8.6 %place.6 = bf16[3072,1536]{1,0:T(8,128)(2,1)} custom-call(s32[64]{0:T(128)S(1)} %copy-done.18, bf16[32,96,1536]{2,1,0:T(8,128)(2,1)} %bitcast.202), custom_call_target="tpu_custom_call" | custom-call | bytes 18874368 | tf_op jit(solution)/shard_map/place/pallas_call | solution.py:531
  304.9 12.3 %fusion.68.ng_ref = f32[768,3072]{1,0:T(8,128)} fusion(bf16[768,1536]{1,0:T(8,128)(2,1)S(1)} %copy-done.39, bf16[3072,1536]{1,0:T(8,128)(2,1)} %place.6), kind=kOutput, calls=%fused_computation.226 | convolution fusion | flops 7247757312 | bytes 21233664 | tf_op jit(solution)/shard_map/dot_general | solution.py:25
  318.1 44.5 %gate.1 = (bf16[768,3072]{1,0:T(8,128)(2,1)}, bf16[768,3072]{1,0:T(8,128)(2,1)}, bf16[768,3072]{1,0:T(8,128)(2,1)}, f32[768,128]{1,0:T(8,128)S(1)}, f32[768,128]...) custom-call(s32[7]{0:T(128)S(1)} %compare_convert_fusion.2.keep_ref.refs_0_, ...), custom_call_target="tpu_custom_call" | custom-call | flops 3623878656 | bytes 56623104 | tf_op jit(solution)/shard_map/gate/pallas_call | solution.py:912
  362.7 8.1 %convolution_convert_fusion.2 = bf16[3072,768]{1,0:T(8,128)(2,1)} fusion(bf16[768,3072]{1,0:T(8,128)(2,1)} %get-tuple-element.80, bf16[768,1536]{1,0:T(8,128)(2,1)S(1)} %copy-done.39, s32[]{:T(128)S(6)} %select_n.152), kind=kOutput, calls=%fused_computation.7 | convolution fusion | flops 3626237952 | bytes 10616836 | tf_op jit(solution)/shard_map/dot_general | solution.py:29
  373.0 8.8 %convolution_convert_fusion.3.refs_2_ = bf16[768,1536]{1,0:T(8,128)(2,1)} fusion(bf16[768,3072]{1,0:T(8,128)(2,1)S(1)} %copy-done.70, bf16[3072,1536]{1,0:T(8,128)(2,1)S(1)} %bitcast.206), kind=kOutput, calls=%fused_computation.16 | convolution fusion | flops 7248936960 | bytes 16515072 | tf_op jit(solution)/shard_map/dot_general | solution.py:21
  381.8 10.9 %fusion.69.refs_1_.refs_9_ = f32[768,1536]{1,0:T(8,128)} fusion(bf16[768,3072]{1,0:T(8,128)(2,1)} %get-tuple-element.82, bf16[1536,3072]{1,0:T(8,128)(2,1)S(1)} %bitcast.204), kind=kOutput, calls=%fused_computation.227 | convolution fusion | flops 7247757312 | bytes 18874368 | tf_op jit(solution)/shard_map/dot_general | solution.py:25
  392.7 7.9 convolution_convert_fusion.1
  405.3 9.1 %add_convert_fusion.2.refs_1_ = bf16[3072,768]{1,0:T(8,128)(2,1)} fusion(bf16[3072,768]{1,0:T(8,128)(2,1)} %collective-permute-done.15, bf16[768,3072]{1,0:T(8,128)(2,1)} %get-tuple-element.80, bf16[768,1536]{1,0:T(8,128)(2,1)S(1)} %copy-done.40, s32[]{:T(128)S(6)} %select_n.151), kind=kOutput, calls=%fused_computation.4 | convolution fusion | flops 3630956544 | bytes 15335428 | tf_op jit(solution)/shard_map/dot_general | solution.py:29
  414.3 11.9 %collective-permute-done.14.refs_0_ = bf16[128,3072]{1,0:T(8,128)(2,1)S(1)} collective-permute-done((bf16[128,3072]{1,0:T(8,128)(2,1)S(1)}, bf16[128,3072]{1,0:T(8,128)(2,1)S(1)}, u32[]{:S(2)}, u32[]{:S(2)}) %collective-permute-start.14) | collective-permute-done | bytes 786464 | tf_op jit(solution)/shard_map/ppermute | solution.py:960
  436.2 10.5 %add_convert_fusion.1.refs_2_ = bf16[768,3072]{1,0:T(8,128)(2,1)} fusion(bf16[768,3072]{1,0:T(8,128)(2,1)} %collective-permute-done.17, bf16[768,3072]{1,0:T(8,128)(2,1)} %get-tuple-element.82, bf16[768,1536]{1,0:T(8,128)(2,1)} %slice.297, s32[]{:T(128)S(6)} %select_n.151), kind=kOutput, calls=%fused_computation.3 | convolution fusion | flops 3630956544 | bytes 15335428 | tf_op jit(solution)/shard_map/dot_general | solution.py:29
  450.8 32.6 %within_back.1 = (f32[768,3072]{1,0:T(8,128)}, f32[768,128]{1,0:T(8,128)S(1)}, f32[768,128]{1,0:T(8,128)S(1)}) custom-call(f32[768,3072]{1,0:T(8,128)} %get-tuple-element.69.u_ref.refs_0_, bf16[768,3072]{1,0:T(8,128)(2,1)} %get-tuple-element.83.refs_1_.dy_ref, f32[768,192]{1,0:T(8,128)} %get-tuple-element.70.cum_ref.refs_2_, f32[128,768]{1,0:T(8,128)S(1)} %copy-done.8, ...), custom_call_target="tpu_custom_call" | custom-call | flops 9663676416 | bytes 23592960 | tf_op jit(solution)/shard_map/within_back/pallas_call | solution.py:986
  483.4 10.0 %collective-permute-done.16.refs_0_ = bf16[128,3072]{1,0:T(8,128)(2,1)} collective-permute-done((bf16[128,3072]{1,0:T(8,128)(2,1)S(1)}, bf16[128,3072]{1,0:T(8,128)(2,1)}, u32[]{:S(2)}, u32[]{:S(2)}) %collective-permute-start.16) | collective-permute-done | bytes 786464 | tf_op jit(solution)/shard_map/ppermute | solution.py:960
  493.3 50.3 %across_back.1 = (bf16[768,3456]{1,0:T(8,128)(2,1)}, f32[768,128]{1,0:T(8,128)S(1)}, f32[768,128]{1,0:T(8,128)S(1)}, f32[768,128]{1,0:T(8,128)S(1)}, f32[6,8,128...) custom-call(s32[7]{0:T(128)S(1)} %compare_convert_fusion.2.keep_ref.refs_0_, ...), custom_call_target="tpu_custom_call" | custom-call | flops 3623878656 | bytes 47185920 | tf_op jit(solution)/shard_map/across_back/pallas_call | solution.py:1002
  552.8 16.3 %collective-permute-done.18 = f32[8,3328]{1,0:T(8,128)S(1)} collective-permute-done((f32[8,3328]{1,0:T(8,128)S(1)}, f32[8,3328]{1,0:T(8,128)S(1)}, u32[]{:S(2)}, u32[]{:S(2)}) %collective-permute-start.18) | collective-permute-done | bytes 106528 | tf_op jit(solution)/shard_map/ppermute | solution.py:1067
  570.8 8.7 %convolution_convert_fusion = bf16[768,3456]{1,0:T(8,128)(2,1)} fusion(bf16[768,3456]{1,0:T(8,128)(2,1)} %fusion.28, bf16[768,1536]{1,0:T(8,128)(2,1)S(1)} %copy-done.42, s32[]{:T(128)S(6)} %select_n.152), kind=kOutput, calls=%fused_computation.5 | convolution fusion | flops 4079517696 | bytes 11796484 | tf_op jit(solution)/shard_map/dot_general | solution.py:29
  580.2 15.2 %convolution_add_fusion.ng_ref = f32[768,1536]{1,0:T(8,128)} fusion(f32[768,1536]{1,0:T(8,128)} %fusion.69.refs_1_.refs_9_, bf16[768,3456]{1,0:T(8,128)(2,1)} %fusion.28, bf16[1536,3456]{1,0:T(8,128)(2,1)} %place.4), kind=kOutput, calls=%fused_computation.15 | convolution fusion | flops 8154906624 | bytes 25362432 | tf_op jit(solution)/shard_map/dot_general | solution.py:25
  606.1 11.3 %add_convert_fusion = bf16[768,3456]{1,0:T(8,128)(2,1)} fusion(bf16[768,3456]{1,0:T(8,128)(2,1)} %collective-permute-done.19, bf16[768,3456]{1,0:T(8,128)(2,1)} %fusion.28, bf16[768,1536]{1,0:T(8,128)(2,1)} %slice.297, s32[]{:T(128)S(6)} %select_n.151), kind=kOutput, calls=%fused_computation | convolution fusion | flops 4084826112 | bytes 17104900 | tf_op jit(solution)/shard_map/dot_general | solution.py:29
  636.2 22.9 %collective-permute-done.21 = bf16[208,3456]{1,0:T(8,128)(2,1)} collective-permute-done((bf16[208,3456]{1,0:T(8,128)(2,1)}, bf16[208,3456]{1,0:T(8,128)(2,1)}, u32[]{:S(2)}, u32[]{:S(2)}) %collective-permute-start.21) | collective-permute-done | bytes 1437728 | tf_op jit(solution)/shard_map/ppermute | solution.py:568
  659.1 30.0 %collective-permute-done.22 = bf16[208,3456]{1,0:T(8,128)(2,1)} collective-permute-done((bf16[208,3456]{1,0:T(8,128)(2,1)}, bf16[208,3456]{1,0:T(8,128)(2,1)}, u32[]{:S(2)}, u32[]{:S(2)}) %collective-permute-start.22) | collective-permute-done | bytes 1437728 | tf_op jit(solution)/shard_map/ppermute | solution.py:568
  696.5 11.2 %all-to-all-done.3 = bf16[4,768,384]{2,1,0:T(8,128)(2,1)S(1)} async-done(((bf16[4,768,384]{2,1,0:T(8,128)(2,1)}), bf16[4,768,384]{2,1,0:T(8,128)(2,1)S(1)}, u32[]{:S(2)}, u32[]{:S(2)}) %all-to-all-start.3) | async-done | bytes 2359328 | tf_op jit(solution)/shard_map/all_to_all | solution.py:572
  720.2 10.2 %all-gather.9.cloned.1.call-done = bf16[8,192,768]{2,1,0:T(8,128)(2,1)} async-done(((bf16[1,192,768]{2,1,0:T(8,128)(2,1)}), bf16[8,192,768]{2,1,0:T(8,128)(2,1)}) %all-gather.9.cloned.1.call-update) | async-done | bytes 2359312 | tf_op jit(solution)/shard_map/all_gather | solution.py:975
  738.7 23.7 %all-to-all-done.4 = bf16[4,240,1152]{2,1,0:T(8,128)(2,1)} async-done(((bf16[4,240,1152]{2,1,0:T(8,128)(2,1)}), bf16[4,240,1152]{2,1,0:T(8,128)(2,1)}, u32[]{:S(2)}, u32[]{:S(2)}) %all-to-all-start.4) | async-done | bytes 2211872 | tf_op jit(solution)/shard_map/all_to_all | solution.py:572
  777.3 7.5 collective-permute-done.25.refs_2_
  (411 shorter events, 236.4 us)
Async XLA Ops:
  7.2 254.6 %all-gather.11.cloned.1.call-start = ((), (), s32[]{:S(2)}) async-start(), calls=%async_computation.12 | async-start | bytes 9732096 | tf_op jit(solution)/shard_map/all_gather | solution.py:698
  17.8 31.6 %collective-permute-start.1 = (bf16[240,768]{1,0:T(8,128)(2,1)}, bf16[240,768]{1,0:T(8,128)(2,1)S(1)}, u32[]{:S(2)}, u32[]{:S(2)}) collective-permute-start(bf16[240,768]{1,0:T(8,128)(2,1)} %pad_maximum_fusion.25), channel_id=1, source_target_pairs={{0,2},{1,3},{2,0},{3,1},{4,6},{5,7},{6,4},{7,5},{8,10},{9,11},{10,... | collective-permute-start | bytes 1105928 | tf_op jit(solution)/shard_map/ppermute | solution.py:576
  17.8 31.7 %collective-permute-start = (bf16[240,768]{1,0:T(8,128)(2,1)}, bf16[240,768]{1,0:T(8,128)(2,1)S(1)}, u32[]{:S(2)}, u32[]{:S(2)}) collective-permute-start(bf16[240,768]{1,0:T(8,128)(2,1)} %pad_maximum_fusion.25), channel_id=1, source_target_pairs={{0,1},{1,2},{2,3},{3,0},{4,5},{5,6},{6,7},{7,4},{8,9},{9,10},{10,1... | collective-permute-start | bytes 1105928 | tf_op jit(solution)/shard_map/ppermute | solution.py:576
  51.0 245.3 %all-gather.13.cloned.1.call-start = ((), (), s32[]{:S(2)}) async-start(), calls=%async_computation.13 | async-start | bytes 9732096 | tf_op jit(solution)/shard_map/all_gather | solution.py:698
  57.6 76.5 %all-to-all-start = ((bf16[4,784,384]{2,1,0:T(8,128)(2,1)}), bf16[4,784,384]{2,1,0:T(8,128)(2,1)}, u32[]{:S(2)}, u32[]{:S(2)}) async-start(bf16[4,784,384]{2,1,0:T(8,128)(2,1)} %bitcast.211), calls=%async_computation | async-start | bytes 4816896 | tf_op jit(solution)/shard_map/all_to_all | solution.py:572
  67.7 34.2 %collective-permute-start.3 = (bf16[4,192,768]{2,1,0:T(8,128)(2,1)S(1)}, bf16[4,192,768]{2,1,0:T(8,128)(2,1)}, u32[]{:S(2)}, u32[]{:S(2)}) collective-permute-start(bf16[4,192,768]{2,1,0:T(8,128)(2,1)S(1)} %pad_maximum_fusion.6.refs_0_), channel_id=1, source_target_pairs={{0,8},{4,12},{8,0},{12,4},{16,24},{20,28},{24,16},{28,20},{1,9},{5... | collective-permute-start | bytes 3538952 | tf_op jit(solution)/shard_map/ppermute | solution.py:568
  69.3 32.7 %collective-permute-start.4 = (bf16[4,192,768]{2,1,0:T(8,128)(2,1)S(1)}, bf16[4,192,768]{2,1,0:T(8,128)(2,1)}, u32[]{:S(2)}, u32[]{:S(2)}) collective-permute-start(bf16[4,192,768]{2,1,0:T(8,128)(2,1)S(1)} %pad_maximum_fusion.6.refs_0_), channel_id=1, source_target_pairs={{0,16},{4,20},{8,24},{12,28},{16,0},{20,4},{24,8},{28,12},{1,17},{... | collective-permute-start | bytes 3538952 | tf_op jit(solution)/shard_map/ppermute | solution.py:568
  70.8 58.6 %collective-permute-start.5 = (bf16[4,192,768]{2,1,0:T(8,128)(2,1)S(1)}, bf16[4,192,768]{2,1,0:T(8,128)(2,1)}, u32[]{:S(2)}, u32[]{:S(2)}) collective-permute-start(bf16[4,192,768]{2,1,0:T(8,128)(2,1)S(1)} %pad_maximum_fusion.6.refs_0_), channel_id=1, source_target_pairs={{0,24},{4,28},{8,16},{12,20},{16,8},{20,12},{24,0},{28,4},{1,25},{... | collective-permute-start | bytes 3538952 | tf_op jit(solution)/shard_map/ppermute | solution.py:568
  71.3 78.0 %collective-permute-start.6 = (bf16[4,192,768]{2,1,0:T(8,128)(2,1)S(1)}, bf16[4,192,768]{2,1,0:T(8,128)(2,1)}, u32[]{:S(2)}, u32[]{:S(2)}) collective-permute-start(bf16[4,192,768]{2,1,0:T(8,128)(2,1)S(1)} %pad_maximum_fusion.6.refs_0_), channel_id=1, source_target_pairs={{0,4},{4,0},{8,12},{12,8},{16,20},{20,16},{24,28},{28,24},{1,5},{5... | collective-permute-start | bytes 3538952 | tf_op jit(solution)/shard_map/ppermute | solution.py:568
  101.9 47.5 %collective-permute-start.7 = (bf16[4,192,768]{2,1,0:T(8,128)(2,1)}, bf16[4,192,768]{2,1,0:T(8,128)(2,1)}, u32[]{:S(2)}, u32[]{:S(2)}) collective-permute-start(bf16[4,192,768]{2,1,0:T(8,128)(2,1)} %collective-permute-done.3.refs_1_), channel_id=1, source_target_pairs={{0,4},{4,0},{8,12},{12,8},{16,20},{20,16},{24,28},{28,24},{1,5},{5... | collective-permute-start | bytes 3538952 | tf_op jit(solution)/shard_map/ppermute | solution.py:568
  102.0 47.3 %collective-permute-start.8 = (bf16[4,192,768]{2,1,0:T(8,128)(2,1)}, bf16[4,192,768]{2,1,0:T(8,128)(2,1)}, u32[]{:S(2)}, u32[]{:S(2)}) collective-permute-start(bf16[4,192,768]{2,1,0:T(8,128)(2,1)} %collective-permute-done.4.refs_2_), channel_id=1, source_target_pairs={{0,4},{4,0},{8,12},{12,8},{16,20},{20,16},{24,28},{28,24},{1,5},{5... | collective-permute-start | bytes 3538952 | tf_op jit(solution)/shard_map/ppermute | solution.py:568
  134.1 83.5 %all-to-all-start.1 = ((bf16[4,768,384]{2,1,0:T(8,128)(2,1)}), bf16[4,768,384]{2,1,0:T(8,128)(2,1)}, u32[]{:S(2)}, u32[]{:S(2)}) async-start(bf16[4,768,384]{2,1,0:T(8,128)(2,1)} %bitcast.207), calls=%async_computation.1 | async-start | bytes 4718592 | tf_op jit(solution)/shard_map/all_to_all | solution.py:572
  208.4 49.0 %collective-permute-start.10 = (bf16[128,3072]{1,0:T(8,128)(2,1)S(1)}, bf16[128,3072]{1,0:T(8,128)(2,1)S(1)}, u32[]{:S(2)}, u32[]{:S(2)}) collective-permute-start(bf16[128,3072]{1,0:T(8,128)(2,1)S(1)} %convert_element_type.227), channel_id=1, source_target_pairs={{0,1},{1,2},{2,3},{4,5},{5,6},{6,7},{8,9},{9,10},{10,11},{12,13},{... | collective-permute-start | bytes 2359304 | tf_op jit(solution)/shard_map/ppermute | solution.py:873
  260.2 29.0 %collective-permute-start.11 = (bf16[128,3072]{1,0:T(8,128)(2,1)S(1)}, bf16[128,3072]{1,0:T(8,128)(2,1)S(1)}, u32[]{:S(2)}, u32[]{:S(2)}) collective-permute-start(bf16[128,3072]{1,0:T(8,128)(2,1)S(1)} %add_convert_fusion.7), channel_id=1, source_target_pairs={{0,1},{1,2},{2,3},{4,5},{5,6},{6,7},{8,9},{9,10},{10,11},{12,13},{... | collective-permute-start | bytes 2359304 | tf_op jit(solution)/shard_map/ppermute | solution.py:897
  291.8 25.4 %collective-permute-start.12 = (bf16[128,3072]{1,0:T(8,128)(2,1)S(1)}, bf16[128,3072]{1,0:T(8,128)(2,1)S(1)}, u32[]{:S(2)}, u32[]{:S(2)}) collective-permute-start(bf16[128,3072]{1,0:T(8,128)(2,1)S(1)} %add_convert_fusion.6), channel_id=1, source_target_pairs={{0,1},{1,2},{2,3},{4,5},{5,6},{6,7},{8,9},{9,10},{10,11},{12,13},{... | collective-permute-start | bytes 2359304 | tf_op jit(solution)/shard_map/ppermute | solution.py:897
  370.8 34.5 %collective-permute-start.15 = (bf16[3072,768]{1,0:T(8,128)(2,1)}, bf16[3072,768]{1,0:T(8,128)(2,1)}, u32[]{:S(2)}, u32[]{:S(2)}) collective-permute-start(bf16[3072,768]{1,0:T(8,128)(2,1)} %convolution_convert_fusion.2), channel_id=1, source_target_pairs={{0,4},{4,0},{8,12},{12,8},{16,20},{20,16},{24,28},{28,24},{1,5},{5... | collective-permute-start | bytes 14155784 | tf_op jit(solution)/shard_map/ppermute | solution.py:568
  370.9 30.2 %collective-permute-start.13 = (bf16[128,3072]{1,0:T(8,128)(2,1)S(1)}, bf16[128,3072]{1,0:T(8,128)(2,1)S(1)}, u32[]{:S(2)}, u32[]{:S(2)}) collective-permute-start(bf16[128,3072]{1,0:T(8,128)(2,1)S(1)} %convert_element_type.234), channel_id=1, source_target_pairs={{1,0},{2,1},{3,2},{5,4},{6,5},{7,6},{9,8},{10,9},{11,10},{13,12},{... | collective-permute-start | bytes 2359304 | tf_op jit(solution)/shard_map/ppermute | solution.py:944
  400.6 35.6 %collective-permute-start.17 = (bf16[768,3072]{1,0:T(8,128)(2,1)}, bf16[768,3072]{1,0:T(8,128)(2,1)}, u32[]{:S(2)}, u32[]{:S(2)}) collective-permute-start(bf16[768,3072]{1,0:T(8,128)(2,1)} %convolution_convert_fusion.1), channel_id=1, source_target_pairs={{0,4},{4,0},{8,12},{12,8},{16,20},{20,16},{24,28},{28,24},{1,5},{5... | collective-permute-start | bytes 14155784 | tf_op jit(solution)/shard_map/ppermute | solution.py:568
  427.1 175.7 %all-reduce.14.cloned.1.call-start = ((), (), s32[]{:S(2)}) async-start(), calls=%async_computation.14 | async-start | bytes 9437184
  431.5 113.6 %all-to-all-start.2 = ((bf16[4,768,384]{2,1,0:T(8,128)(2,1)}), bf16[4,768,384]{2,1,0:T(8,128)(2,1)}, u32[]{:S(2)}, u32[]{:S(2)}) async-start(bf16[4,768,384]{2,1,0:T(8,128)(2,1)} %after.14), calls=%async_computation.2 | async-start | bytes 4718592 | tf_op jit(solution)/shard_map/all_to_all | solution.py:572
  436.0 181.3 %reduce-scatter.13.cloned.1.call-start = ((), (), s32[]{:S(2)}) async-start(), calls=%async_computation.15 | async-start | bytes 5898240
  446.7 189.5 %reduce-scatter.11.cloned.1.call-start = ((), (), s32[]{:S(2)}) async-start(), calls=%async_computation.10 | async-start | bytes 1474560 | tf_op jit(solution)/shard_map/reduce_scatter | solution.py:974
  449.5 43.8 %collective-permute-start.16 = (bf16[128,3072]{1,0:T(8,128)(2,1)S(1)}, bf16[128,3072]{1,0:T(8,128)(2,1)}, u32[]{:S(2)}, u32[]{:S(2)}) collective-permute-start(bf16[128,3072]{1,0:T(8,128)(2,1)S(1)} %add_convert_fusion.4), channel_id=1, source_target_pairs={{1,0},{2,1},{3,2},{5,4},{6,5},{7,6},{9,8},{10,9},{11,10},{13,12},{... | collective-permute-start | bytes 2359304 | tf_op jit(solution)/shard_map/ppermute | solution.py:960
  579.5 26.5 %collective-permute-start.19 = (bf16[768,3456]{1,0:T(8,128)(2,1)}, bf16[768,3456]{1,0:T(8,128)(2,1)}, u32[]{:S(2)}, u32[]{:S(2)}) collective-permute-start(bf16[768,3456]{1,0:T(8,128)(2,1)} %convolution_convert_fusion), channel_id=1, source_target_pairs={{0,4},{4,0},{8,12},{12,8},{16,20},{20,16},{24,28},{28,24},{1,5},{5... | collective-permute-start | bytes 15925256 | tf_op jit(solution)/shard_map/ppermute | solution.py:568
  605.9 106.7 %reduce-scatter.9.cloned.1.call-start = ((), (), s32[]{:S(2)}) async-start(), calls=%async_computation.8 | async-start | bytes 1474560 | tf_op jit(solution)/shard_map/reduce_scatter | solution.py:974
  624.4 34.7 %collective-permute-start.21 = (bf16[208,3456]{1,0:T(8,128)(2,1)}, bf16[208,3456]{1,0:T(8,128)(2,1)}, u32[]{:S(2)}, u32[]{:S(2)}) collective-permute-start(bf16[208,3456]{1,0:T(8,128)(2,1)} %get-tuple-element.213), channel_id=1, source_target_pairs={{0,8},{4,12},{8,0},{12,4},{16,24},{20,28},{24,16},{28,20},{1,9},{5... | collective-permute-start | bytes 4313096 | tf_op jit(solution)/shard_map/ppermute | solution.py:568
  626.0 63.2 %collective-permute-start.22 = (bf16[208,3456]{1,0:T(8,128)(2,1)}, bf16[208,3456]{1,0:T(8,128)(2,1)}, u32[]{:S(2)}, u32[]{:S(2)}) collective-permute-start(bf16[208,3456]{1,0:T(8,128)(2,1)} %get-tuple-element.214), channel_id=1, source_target_pairs={{0,16},{4,20},{8,24},{12,28},{16,0},{20,4},{24,8},{28,12},{1,17},{... | collective-permute-start | bytes 4313096 | tf_op jit(solution)/shard_map/ppermute | solution.py:568
  627.3 63.0 %collective-permute-start.23 = (bf16[208,3456]{1,0:T(8,128)(2,1)}, bf16[208,3456]{1,0:T(8,128)(2,1)}, u32[]{:S(2)}, u32[]{:S(2)}) collective-permute-start(bf16[208,3456]{1,0:T(8,128)(2,1)} %get-tuple-element.215), channel_id=1, source_target_pairs={{0,24},{4,28},{8,16},{12,20},{16,8},{20,12},{24,0},{28,4},{1,25},{... | collective-permute-start | bytes 4313096 | tf_op jit(solution)/shard_map/ppermute | solution.py:568
  631.6 76.1 %all-to-all-start.3 = ((bf16[4,768,384]{2,1,0:T(8,128)(2,1)}), bf16[4,768,384]{2,1,0:T(8,128)(2,1)S(1)}, u32[]{:S(2)}, u32[]{:S(2)}) async-start(bf16[4,768,384]{2,1,0:T(8,128)(2,1)} %pad_maximum_fusion.4), calls=%async_computation.3 | async-start | bytes 4718592 | tf_op jit(solution)/shard_map/all_to_all | solution.py:572
  635.2 95.2 %all-gather.9.cloned.1.call-start = ((), (), s32[]{:S(2)}) async-start(), calls=%async_computation.11 | async-start | bytes 2654208 | tf_op jit(solution)/shard_map/all_gather | solution.py:975
  707.7 54.7 %all-to-all-start.4 = ((bf16[4,240,1152]{2,1,0:T(8,128)(2,1)}), bf16[4,240,1152]{2,1,0:T(8,128)(2,1)}, u32[]{:S(2)}, u32[]{:S(2)}) async-start(bf16[4,240,1152]{2,1,0:T(8,128)(2,1)} %pad_maximum_fusion.5), calls=%async_computation.4 | async-start | bytes 4423680 | tf_op jit(solution)/shard_map/all_to_all | solution.py:572
  712.2 85.6 %all-gather.7.cloned.1.call-start = ((), (), s32[]{:S(2)}) async-start(), calls=%async_computation.9 | async-start | bytes 2654208 | tf_op jit(solution)/shard_map/all_gather | solution.py:975
  (92 other events, 1672.8 us)
Sparse Core Ops, SparseCore 0:
  51.1 133.3 all-gather.10
  187.3 96.0 all-gather.12
  431.2 112.4 all-reduce.13
  547.1 57.0 reduce-scatter.12
  607.0 29.1 reduce-scatter.10
  639.0 45.9 reduce-scatter.8
  686.8 43.5 all-gather.8
  732.3 29.0 all-gather.6

commit v3 on v2

--- a/solution.py
+++ b/solution.py
@@ -69,6 +69,13 @@
     for i in range(1, v.shape[1] // 128):
         total = total + v[:, i * 128 : (i + 1) * 128]
     return total
+
+
+def two_heads(first, v):
+    v = v.astype(F32)
+    return jnp.concatenate(
+        [jnp.where(first, v, 0.0).astype(BF16), jnp.where(first, 0.0, v).astype(BF16)], axis=0
+    )
 
 
 def chunk(i, width):
@@ -224,7 +231,7 @@
         spread = spread_ref[:, at]
         w = (u * sigmoid(u) * dot_nn(coef, spread)).astype(BF16)
         state = state_ref[:, at] * keep
-        local_ref[0, :, at] = state.astype(BF16)
+        local_ref[0, :, at] = state
         decay = dot_nn(dec, spread)[0:1, :]
         wide_ref[0, :, at] = decay
         pref = run_ref[:, at] * keep
@@ -262,10 +269,10 @@
         mixing = (jnp.exp(jnp.minimum(left - right, 0.0)) * scores).astype(BF16)
         u = u_ref[:, at]
         v = u * sigmoid(u) * dot_nn(steps, spread_ref[:, at])
-        stacked = jnp.concatenate(
-            [jnp.where(first, v, 0.0).astype(BF16), jnp.where(first, 0.0, v).astype(BF16)], axis=0
-        )
-        y_ref[:, at] = dot_nn(mixing, stacked)
+        v, v_rest = halves(v)
+        y_ref[:, at] = dot_nn(mixing, two_heads(first, v)) + dot_nn(
+            mixing, two_heads(first, v_rest)
+        )
         return carry
 
     lax.fori_loop(0, u_ref.shape[1] // 128, pair, 0, unroll=8)
@@ -275,7 +282,7 @@
     keep_ref, y_ref, u_ref, gate_ref, ng_ref, local_ref, enter_ref, pref_ref, c_ref, grow_ref,
     skip_ref, gain_ref, dec_ref, spread_ref, select_ref,
     ny_ref, dy_ref, gg_ref, q_ref, dc_ref, gain_grad_ref, skip_grad_ref, out_ref,
-    scan_ref, carried_ref, state_ref, high_ref, low_ref, z_ref,
+    scan_ref, carried_ref, state_ref, high_ref, low_ref, z_ref, rest_ref, z_low_ref,
 ):
     g = pl.program_id(0)
     c = pl.num_programs(0) - 1 - g
@@ -294,11 +301,14 @@
     def forward(i, sums):
         squares, stat = sums
         at = chunk(i, WIDE)
-        carried = (
-            local_ref[0, :, at].astype(F32) + pref_ref[0, :, at] * enter_ref[:, at].astype(F32)
-        ).astype(BF16)
+        carried, rest = halves(
+            local_ref[0, :, at] + pref_ref[0, :, at] * enter_ref[:, at].astype(F32)
+        )
         carried_ref[:, at] = carried
-        scanned = y_ref[:, at] + dot_nn(grow, spread_ref[:, at]) * (dot_nn(c_map, carried)+dot_nn(c_low,carried))
+        rest_ref[:, at] = rest
+        scanned = y_ref[:, at] + dot_nn(grow, spread_ref[:, at]) * (
+            dot_nn(c_map, carried) + (dot_nn(c_low, carried) + dot_nn(c_map, rest))
+        )
         scan_ref[:, at] = scanned
         u = u_ref[:, at]
         y = scanned + skip_ref[:, at] * (u * sigmoid(u))
@@ -330,20 +340,22 @@
         gain_grad_ref[:, at] += jnp.sum(ng * scaled, axis=0, keepdims=True)
         gated_grad = scale * (ng * gain) - gated * back
         gg_ref[:, at] = (gated_grad * y * open_ * (1.0 + gate * (1.0 - open_))).astype(BF16)
-        dy_low = (gated_grad * act).astype(BF16)
-        dy_ref[:, at] = dy_low
-        dy = dy_low.astype(F32)
+        dy = gated_grad * act
+        dy_ref[:, at] = dy
         skip_grad_ref[:, at] += jnp.sum(dy * x, axis=0, keepdims=True)
         high_ref[:, at], low_ref[:, at] = halves(dy * scanned)
-        z = (dot_nn(grow, spread_ref[:, at]) * dy).astype(BF16)
+        z, z_low = halves(dot_nn(grow, spread_ref[:, at]) * dy)
         z_ref[:, at] = z
-        state_ref[:, at] = keep * (dec_ref[0, :, at] * state_ref[:, at] + (dot_tn(c_map, z)+dot_tn(c_low,z)))
+        z_low_ref[:, at] = z_low
+        state_ref[:, at] = keep * (dec_ref[0, :, at] * state_ref[:, at] + (dot_tn(c_map, z) + (dot_tn(c_low, z) + dot_tn(c_map, z_low))))
         return carry
 
     lax.fori_loop(0, width // WIDE, backward, 0, unroll=3)
     select = select_ref[...]
     q_ref[...] = dot_nn(high_ref[...], select) + dot_nn(low_ref[...], select)
-    dc_ref[...] = dot_nt(z_ref[...], carried_ref[...])
+    z = z_ref[...]
+    carried = carried_ref[...]
+    dc_ref[...] = dot_nt(z, carried) + (dot_nt(z, rest_ref[...]) + dot_nt(z_low_ref[...], carried))
 
     @pl.when(c == 0)
     def _():
@@ -371,18 +383,14 @@
         )
         decay = jnp.exp(jnp.minimum(right - left, 0.0))
         mixing = (decay * scores).astype(BF16)
-        dy_low = dy_ref[:, at]
-        dy = dy_low.astype(F32)
-        dy_stack = jnp.concatenate(
-            [jnp.where(first, dy, 0.0).astype(BF16), jnp.where(first, 0.0, dy).astype(BF16)], axis=0
-        )
-        dv_ref[:, at] = dot_nn(mixing, dy_stack)
+        dy, dy_rest = halves(dy_ref[:, at])
+        dv_ref[:, at] = dot_nn(mixing, two_heads(first, dy)) + dot_nn(
+            mixing, two_heads(first, dy_rest)
+        )
         u = u_ref[:, at]
         v = u * sigmoid(u) * dot_nn(steps, spread_ref[:, at])
-        v_stack = jnp.concatenate(
-            [jnp.where(first, v, 0.0).astype(BF16), jnp.where(first, 0.0, v).astype(BF16)], axis=0
-        )
-        dw = dot_nt(v_stack, dy_low)
+        v_stack = two_heads(first, v)
+        dw = dot_nt(v_stack, dy) + dot_nt(v_stack, dy_rest)
         return total + decay[:, :LEN] * dw[:LEN] + decay[:, LEN:] * dw[LEN:]
 
     total = lax.fori_loop(
@@ -397,7 +405,7 @@
     keep_ref, u_ref, dy_ref, dv_ref, ip_ref, halo_ref, local_ref, enter_ref, pref_ref, leave_ref,
     b_ref, c_ref, grow_ref, fall_ref, step_ref, skip_ref, dec_ref, taps_ref, spread_ref, select_ref,
     ig_ref, db_ref, q_ref, r_ref, end_ref, taps_grad_ref, bias_grad_ref, head_ref,
-    state_ref, ext_ref, high_ref, low_ref, x_ref, fall_v_ref, state_low_ref, ends_ref,
+    state_ref, ext_ref, high_ref, low_ref, x_ref, fall_v_ref, state_low_ref, rest_ref, fall_rest_ref, ends_ref,
 ):
     g = pl.program_id(0)
     c = pl.num_programs(0) - 1 - g
@@ -425,38 +433,43 @@
         at = chunk(i, WIDE)
         spread = spread_ref[:, at]
         state = state_ref[:, at]
-        state_low = state.astype(BF16)
+        state_low, state_rest = halves(state)
         falling = dot_nn(fall, spread)
-        across = falling * (dot_nn(b_map, state_low)+dot_nn(b_low, state_low))
+        across = falling * (
+            dot_nn(b_map, state_low) + (dot_nn(b_low, state_low) + dot_nn(b_map, state_rest))
+        )
         dv = dv_ref[:, at] + across
         u = u_ref[:, at]
         open_ = sigmoid(u)
         x = u * open_
         delta = dot_nn(steps, spread)
         v = x * delta
-        v_low = v.astype(BF16).astype(F32)
+        v_low = v
         dy = dy_ref[:, at].astype(F32)
         dx = delta * dv + skip_ref[:, at] * dy
         ext_ref[0:LEN, at] = dx * (open_ * (1.0 + u * (1.0 - open_)))
         high_ref[:, at], low_ref[:, at] = halves(v_low * dv)
         x_ref[:, at] = (x * dv).astype(BF16)
-        carried = (
-            local_ref[0, :, at].astype(F32) + pref_ref[0, :, at] * enter_ref[:, at].astype(F32)
-        ).astype(BF16)
+        carried = local_ref[0, :, at] + pref_ref[0, :, at] * enter_ref[:, at].astype(F32)
         decay = dec_ref[0, :, at]
         end = jnp.sum(v_low * across, axis=0, keepdims=True) + decay * jnp.sum(
-            state * carried.astype(F32), axis=0, keepdims=True
+            state * carried, axis=0, keepdims=True
         )
         ends_ref[:, at] = jnp.broadcast_to(end, (8, WIDE))
-        fall_v_ref[:, at] = (falling * v).astype(BF16)
+        fall_v_ref[:, at], fall_rest_ref[:, at] = halves(falling * v)
         state_low_ref[:, at] = state_low
-        z = (dot_nn(grow, spread) * dy).astype(BF16)
-        state_ref[:, at] = keep * (decay * state + (dot_tn(c_map, z)+dot_tn(c_low,z)))
+        rest_ref[:, at] = state_rest
+        z, z_low = halves(dot_nn(grow, spread) * dy)
+        state_ref[:, at] = keep * (decay * state + (dot_tn(c_map, z) + (dot_tn(c_low, z) + dot_tn(c_map, z_low))))
         return carry
 
-    lax.fori_loop(0, width // WIDE, step, 0, unroll=2)
+    lax.fori_loop(0, width // WIDE, step, 0, unroll=3)
     select = select_ref[...]
-    db_ref[...] = dot_nt(fall_v_ref[...], state_low_ref[...])
+    fall_v = fall_v_ref[...]
+    state_low = state_low_ref[...]
+    db_ref[...] = dot_nt(fall_v, state_low) + (
+        dot_nt(fall_v, rest_ref[...]) + dot_nt(fall_rest_ref[...], state_low)
+    )
     q_ref[...] = dot_nn(high_ref[...], select) + dot_nn(low_ref[...], select)
     r_ref[...] = dot_nn(x_ref[...], select)
     end_ref[0] = head_sums(ends_ref[...], select)
@@ -475,7 +488,7 @@
         ig_ref[:, at] = total.astype(BF16)
         return carry
 
-    lax.fori_loop(0, width // WIDE, conv, 0, unroll=3)
+    lax.fori_loop(0, width // WIDE, conv, 0, unroll=4)
 
     @pl.when(c == 0)
     def _():
@@ -856,7 +869,7 @@
             up(1, 1, inner), full(1, inner),
         ],
         out_shape=[
-            out((rows, inner), F32), out((blocks, nstate, inner), BF16), out((nstate, inner), F32),
+            out((rows, inner), F32), out((blocks, nstate, inner), F32), out((nstate, inner), F32),
             out((blocks, 1, inner), F32), out((blocks, 1, inner), F32), out((1, inner), F32),
         ],
         scratch_shapes=[
@@ -923,7 +936,7 @@
                 down(LEN, nstate), full(1, inner), full(1, inner), full(nstate, inner),
             ],
             out_shape=[
-                out((rows, inner), BF16), out((rows, inner), BF16), out((rows, inner), BF16),
+                out((rows, inner), BF16), out((rows, inner), F32), out((rows, inner), BF16),
                 lanes, out((rows, nstate), F32), out((1, inner), F32),
                 out((1, inner), F32), out((nstate, inner), F32),
             ],
@@ -931,7 +944,7 @@
                 pltpu.VMEM((LEN, inner), F32), pltpu.VMEM((nstate, inner), BF16),
                 pltpu.VMEM((nstate, inner), F32),
             ]
-            + [pltpu.VMEM((LEN, inner), BF16)] * 3,
+            + [pltpu.VMEM((LEN, inner), BF16)] * 5,
             compiler_params=params,
             cost_estimate=cost(6 * wide_map, rows * inner * 24),
             name="gate",
@@ -1021,7 +1034,7 @@
             scratch_shapes=[
                 pltpu.VMEM((nstate, inner), F32), pltpu.VMEM((LEN + 8, inner), F32),
             ]
-            + [pltpu.VMEM((LEN, inner), BF16)] * 5
+            + [pltpu.VMEM((LEN, inner), BF16)] * 7
             + [pltpu.VMEM((8, inner), F32)],
             compiler_params=params,
             cost_estimate=cost(6 * wide_map, rows * inner * 20),

time: 816 us -> 830 us (1.017)
  Pallas kernels: 241 us -> 262 us
  transfers between devices with their start and end apart: 44 -> 44, of which waited for: 21 -> 18; matrix products, arithmetic and copies ran while one was open for 26% -> 26% of each run, Pallas kernels for 24% -> 26%
where the time goes in v3:
time: 830 us; the launch traced here: 823 us
  Pallas kernels  262 us (32%)
  waiting for transfers between devices  248 us (30%)
  matrix products  133 us (16%)
  local copies, waits for them, and re-layouts  58.5 us (7%)
  starting transfers between devices  57.3 us (7%)
  other arithmetic  48.3 us (6%)
  between operations  16.4 us (2%)
    ppermute x21, waiting for transfers between devices, swap(): return lax.ppermute(v, 'dp', [(i, i ^ mask) for i in range(count)])  127 us
    pallas_call x1, Pallas kernels, local(): pl.pallas_call(across_back_kernel, grid=(blocks,), in_specs=[smem, down(L...  56.2 us
    dot_general x6, matrix products, dot_tn(): lax.dot_general(a, b, (((0,), (0,)), ((), ())), preferred_element_type=F32)  55.6 us
    pallas_call x1, Pallas kernels, local(): pl.pallas_call(gate_kernel, grid=(blocks,), in_specs=[smem, down(LEN, inn...  50.4 us
    all_to_all x5, waiting for transfers between devices, exchange(): return lax.all_to_all(v, 'tensor', 0, 0, tiled=True)  44 us
    dot_general x3, matrix products, dot_nt(): lax.dot_general(a, b, (((1,), (1,)), ((), ())), preferred_element_type=F32)  39.2 us
    pallas_call x1, Pallas kernels, local(): pl.pallas_call(unread(9, 1)(within_back_kernel), grid=(blocks,), in_specs...  38.9 us
    dot_general x4, matrix products, dot_nn(): return jnp.dot(a, b, preferred_element_type=F32)  38.5 us
  transfers between devices with their start and end apart: 44, of which 18 were waited for; matrix products, arithmetic and copies ran while one was open for 26% of the time, Pallas kernels for 26%

profile of v3, /device:TPU:0, one launch (start us, length us, event | category | flops | bytes accessed | tf_op | source)
XLA Modules:
  0.0 823.2 jit_solution(4952036763703761590)
XLA Ops:
  27.2 22.3 %collective-permute-done.1.refs_2_ = bf16[240,768]{1,0:T(8,128)(2,1)S(1)} collective-permute-done((bf16[240,768]{1,0:T(8,128)(2,1)}, bf16[240,768]{1,0:T(8,128)(2,1)S(1)}, u32[]{:S(2)}, u32[]{:S(2)}) %collective-permute-start.1) | collective-permute-done | bytes 368672 | tf_op jit(solution)/shard_map/ppermute | solution.py:589
  71.6 30.3 %collective-permute-done.3.refs_1_ = bf16[4,192,768]{2,1,0:T(8,128)(2,1)} collective-permute-done((bf16[4,192,768]{2,1,0:T(8,128)(2,1)S(1)}, bf16[4,192,768]{2,1,0:T(8,128)(2,1)}, u32[]{:S(2)}, u32[]{:S(2)}) %collective-permute-start.3) | collective-permute-done | bytes 1179680 | tf_op jit(solution)/shard_map/ppermute | solution.py:581
  102.4 27.0 %collective-permute-done.5.refs_3_ = bf16[4,192,768]{2,1,0:T(8,128)(2,1)} collective-permute-done((bf16[4,192,768]{2,1,0:T(8,128)(2,1)S(1)}, bf16[4,192,768]{2,1,0:T(8,128)(2,1)}, u32[]{:S(2)}, u32[]{:S(2)}) %collective-permute-start.5) | collective-permute-done | bytes 1179680 | tf_op jit(solution)/shard_map/ppermute | solution.py:581
  149.4 9.1 %place.4 = bf16[1536,3456]{1,0:T(8,128)(2,1)} custom-call(s32[66]{0:T(128)S(1)} %stack.98.where_ref, bf16[4,192,768]{2,1,0:T(8,128)(2,1)S(1)} %pad_maximum_fusion.6.refs_0_, bf16[4,192,768]{2,1,0:T(8,128)(2,1)} %collective-permute-done.3.refs_1_, bf16[4,192,768]{2,1,0:T(8,128)(2,1)} %collective-permute-done.4.refs_2_, ...), custom_call_target="tpu_custom_call" | custom-call | bytes 21233664 | tf_op jit(solution)/shard_map/place/pallas_call | solution.py:544
  174.6 13.0 %fusion.ip_ref.halo_ref = f32[784,3072]{1,0:T(8,128)} fusion(bf16[784,1536]{1,0:T(8,128)(2,1)S(1)} %copy-done.43, bf16[1536,3456]{1,0:T(8,128)(2,1)} %place.4), kind=kOutput, calls=%fused_computation.1 | convolution fusion | flops 7398752256 | bytes 21479424 | tf_op jit(solution)/shard_map/dot_general | solution.py:21
  187.6 19.5 %conv_states.1 = (f32[768,3072]{1,0:T(8,128)}, f32[6,128,3072]{2,1,0:T(8,128)}, f32[128,3072]{1,0:T(8,128)}, f32[6,1,3072]{2,1,0:T(1,128)S(1)}, f32[6,1,3072]{2,1,0:T(1,128)S(1)}, /*index=5*/f32[1,3072]{1,0:T(1,128)S(1)}) custom-call(s32[7]{0:T(128)S(1)} %compare_convert_fusion.2.keep_ref.refs_0_, f32[784,3072]{1,0:T(8,128)} %fusion.ip_ref.halo_ref, ...), custom_call_target="tpu_custom_call" | custom-call | flops 1207959552 | bytes 28311552 | tf_op jit(solution)/shard_map/conv_states/pallas_call | solution.py:860
  224.5 34.6 %within.1.refs_1_.y_ref = f32[768,3072]{1,0:T(8,128)} custom-call(f32[768,3072]{1,0:T(8,128)} %get-tuple-element.69.u_ref.refs_0_, f32[768,192]{1,0:T(8,128)} %get-tuple-element.70.cum_ref.refs_2_, f32[128,768]{1,0:T(8,128)S(1)} %copy-done.8, f32[768,128]{1,0:T(8,128)S(1)} %get-tuple-element.72.step_ref.refs_4_, ...), custom_call_target="tpu_custom_call" | custom-call | flops 4831838208 | bytes 18874368 | tf_op jit(solution)/shard_map/within/pallas_call | solution.py:889
  263.4 8.8 %place.5 = bf16[1536,3072]{1,0:T(8,128)(2,1)} custom-call(s32[64]{0:T(128)S(1)} %copy-done.19, bf16[32,192,768]{2,1,0:T(8,128)(2,1)} %bitcast.201), custom_call_target="tpu_custom_call" | custom-call | bytes 18874368 | tf_op jit(solution)/shard_map/place/pallas_call | solution.py:544
  272.2 12.4 %fusion.63.refs_1_.gate_ref = f32[768,3072]{1,0:T(8,128)} fusion(bf16[1536,3072]{1,0:T(8,128)(2,1)} %place.5, bf16[784,1536]{1,0:T(8,128)(2,1)S(1)} %copy-done.45), kind=kOutput, calls=%fused_computation.221 | convolution fusion | flops 7247757312 | bytes 21233664 | tf_op jit(solution)/shard_map/dot_general | solution.py:21
  296.6 8.6 %place.6 = bf16[3072,1536]{1,0:T(8,128)(2,1)} custom-call(s32[64]{0:T(128)S(1)} %copy-done.18, bf16[32,96,1536]{2,1,0:T(8,128)(2,1)} %bitcast.202), custom_call_target="tpu_custom_call" | custom-call | bytes 18874368 | tf_op jit(solution)/shard_map/place/pallas_call | solution.py:544
  305.2 12.3 %fusion.68.ng_ref = f32[768,3072]{1,0:T(8,128)} fusion(bf16[768,1536]{1,0:T(8,128)(2,1)S(1)} %copy-done.39, bf16[3072,1536]{1,0:T(8,128)(2,1)} %place.6), kind=kOutput, calls=%fused_computation.226 | convolution fusion | flops 7247757312 | bytes 21233664 | tf_op jit(solution)/shard_map/dot_general | solution.py:25
  318.4 50.4 %gate.1 = (bf16[768,3072]{1,0:T(8,128)(2,1)}, f32[768,3072]{1,0:T(8,128)}, bf16[768,3072]{1,0:T(8,128)(2,1)}, f32[768,128]{1,0:T(8,128)S(1)}, f32[768,128]{1,0:T...) custom-call(s32[7]{0:T(128)S(1)} %compare_convert_fusion.2.keep_ref.refs_0_, ...), custom_call_target="tpu_custom_call" | custom-call | flops 3623878656 | bytes 56623104 | tf_op jit(solution)/shard_map/gate/pallas_call | solution.py:925
  368.8 8.0 convolution_convert_fusion.2
  379.1 8.8 %convolution_convert_fusion.3.refs_2_ = bf16[768,1536]{1,0:T(8,128)(2,1)} fusion(bf16[768,3072]{1,0:T(8,128)(2,1)S(1)} %copy-done.70, bf16[3072,1536]{1,0:T(8,128)(2,1)S(1)} %bitcast.206), kind=kOutput, calls=%fused_computation.16 | convolution fusion | flops 7248936960 | bytes 16515072 | tf_op jit(solution)/shard_map/dot_general | solution.py:21
  387.9 10.9 %fusion.69.refs_1_.refs_9_ = f32[768,1536]{1,0:T(8,128)} fusion(bf16[768,3072]{1,0:T(8,128)(2,1)} %get-tuple-element.82, bf16[1536,3072]{1,0:T(8,128)(2,1)S(1)} %bitcast.204), kind=kOutput, calls=%fused_computation.227 | convolution fusion | flops 7247757312 | bytes 18874368 | tf_op jit(solution)/shard_map/dot_general | solution.py:25
  398.8 7.9 convolution_convert_fusion.1
  411.5 8.9 %add_convert_fusion.2.refs_1_ = bf16[3072,768]{1,0:T(8,128)(2,1)} fusion(bf16[3072,768]{1,0:T(8,128)(2,1)} %collective-permute-done.15, bf16[768,3072]{1,0:T(8,128)(2,1)} %get-tuple-element.80, bf16[768,1536]{1,0:T(8,128)(2,1)S(1)} %copy-done.40, s32[]{:T(128)S(6)} %select_n.151), kind=kOutput, calls=%fused_computation.4 | convolution fusion | flops 3630956544 | bytes 15335428 | tf_op jit(solution)/shard_map/dot_general | solution.py:29
  420.4 12.1 %collective-permute-done.14.refs_0_ = bf16[128,3072]{1,0:T(8,128)(2,1)S(1)} collective-permute-done((bf16[128,3072]{1,0:T(8,128)(2,1)S(1)}, bf16[128,3072]{1,0:T(8,128)(2,1)S(1)}, u32[]{:S(2)}, u32[]{:S(2)}) %collective-permute-start.14) | collective-permute-done | bytes 786464 | tf_op jit(solution)/shard_map/ppermute | solution.py:973
  442.5 10.7 %add_convert_fusion.1.refs_2_ = bf16[768,3072]{1,0:T(8,128)(2,1)} fusion(bf16[768,3072]{1,0:T(8,128)(2,1)} %collective-permute-done.17, bf16[768,3072]{1,0:T(8,128)(2,1)} %get-tuple-element.82, bf16[768,1536]{1,0:T(8,128)(2,1)} %slice.297, s32[]{:T(128)S(6)} %select_n.151), kind=kOutput, calls=%fused_computation.3 | convolution fusion | flops 3630956544 | bytes 15335428 | tf_op jit(solution)/shard_map/dot_general | solution.py:29
  457.3 38.9 %within_back.1 = (f32[768,3072]{1,0:T(8,128)}, f32[768,128]{1,0:T(8,128)S(1)}, f32[768,128]{1,0:T(8,128)S(1)}) custom-call(f32[768,3072]{1,0:T(8,128)} %get-tuple-element.69.u_ref.refs_0_, f32[768,3072]{1,0:T(8,128)} %get-tuple-element.83.refs_1_.dy_ref, f32[768,192]{1,0:T(8,128)} %get-tuple-element.70.cum_ref.refs_2_, f32[128,768]{1,0:T(8,128)S(1)} %copy-done.8, ...), custom_call_target="tpu_custom_call" | custom-call | flops 9663676416 | bytes 23592960 | tf_op jit(solution)/shard_map/within_back/pallas_call | solution.py:999
  499.7 56.2 %across_back.1 = (bf16[768,3456]{1,0:T(8,128)(2,1)}, f32[768,128]{1,0:T(8,128)S(1)}, f32[768,128]{1,0:T(8,128)S(1)}, f32[768,128]{1,0:T(8,128)S(1)}, f32[6,8,128...) custom-call(s32[7]{0:T(128)S(1)} %compare_convert_fusion.2.keep_ref.refs_0_, ...), custom_call_target="tpu_custom_call" | custom-call | flops 3623878656 | bytes 47185920 | tf_op jit(solution)/shard_map/across_back/pallas_call | solution.py:1015
  565.4 16.3 %collective-permute-done.18 = f32[8,3328]{1,0:T(8,128)S(1)} collective-permute-done((f32[8,3328]{1,0:T(8,128)S(1)}, f32[8,3328]{1,0:T(8,128)S(1)}, u32[]{:S(2)}, u32[]{:S(2)}) %collective-permute-start.18) | collective-permute-done | bytes 106528 | tf_op jit(solution)/shard_map/ppermute | solution.py:1080
  583.3 8.7 %convolution_convert_fusion = bf16[768,3456]{1,0:T(8,128)(2,1)} fusion(bf16[768,3456]{1,0:T(8,128)(2,1)} %fusion.28, bf16[768,1536]{1,0:T(8,128)(2,1)S(1)} %copy-done.42, s32[]{:T(128)S(6)} %select_n.152), kind=kOutput, calls=%fused_computation.5 | convolution fusion | flops 4079517696 | bytes 11796484 | tf_op jit(solution)/shard_map/dot_general | solution.py:29
  592.7 15.9 %convolution_add_fusion.ng_ref = f32[768,1536]{1,0:T(8,128)} fusion(f32[768,1536]{1,0:T(8,128)} %fusion.69.refs_1_.refs_9_, bf16[768,3456]{1,0:T(8,128)(2,1)} %fusion.28, bf16[1536,3456]{1,0:T(8,128)(2,1)} %place.4), kind=kOutput, calls=%fused_computation.15 | convolution fusion | flops 8154906624 | bytes 25362432 | tf_op jit(solution)/shard_map/dot_general | solution.py:25
  608.6 6.7 input_grad.1
  619.1 11.3 %add_convert_fusion = bf16[768,3456]{1,0:T(8,128)(2,1)} fusion(bf16[768,3456]{1,0:T(8,128)(2,1)} %collective-permute-done.19, bf16[768,3456]{1,0:T(8,128)(2,1)} %fusion.28, bf16[768,1536]{1,0:T(8,128)(2,1)} %slice.297, s32[]{:T(128)S(6)} %select_n.151), kind=kOutput, calls=%fused_computation | convolution fusion | flops 4084826112 | bytes 17104900 | tf_op jit(solution)/shard_map/dot_general | solution.py:29
  649.0 23.2 %collective-permute-done.21 = bf16[208,3456]{1,0:T(8,128)(2,1)} collective-permute-done((bf16[208,3456]{1,0:T(8,128)(2,1)}, bf16[208,3456]{1,0:T(8,128)(2,1)}, u32[]{:S(2)}, u32[]{:S(2)}) %collective-permute-start.21) | collective-permute-done | bytes 1437728 | tf_op jit(solution)/shard_map/ppermute | solution.py:581
  672.2 31.1 %collective-permute-done.22 = bf16[208,3456]{1,0:T(8,128)(2,1)} collective-permute-done((bf16[208,3456]{1,0:T(8,128)(2,1)}, bf16[208,3456]{1,0:T(8,128)(2,1)}, u32[]{:S(2)}, u32[]{:S(2)}) %collective-permute-start.22) | collective-permute-done | bytes 1437728 | tf_op jit(solution)/shard_map/ppermute | solution.py:581
  709.4 11.2 %all-to-all-done.3 = bf16[4,768,384]{2,1,0:T(8,128)(2,1)S(1)} async-done(((bf16[4,768,384]{2,1,0:T(8,128)(2,1)}), bf16[4,768,384]{2,1,0:T(8,128)(2,1)S(1)}, u32[]{:S(2)}, u32[]{:S(2)}) %all-to-all-start.3) | async-done | bytes 2359328 | tf_op jit(solution)/shard_map/all_to_all | solution.py:585
  733.1 9.9 %all-gather.9.cloned.1.call-done = bf16[8,192,768]{2,1,0:T(8,128)(2,1)} async-done(((bf16[1,192,768]{2,1,0:T(8,128)(2,1)}), bf16[8,192,768]{2,1,0:T(8,128)(2,1)}) %all-gather.9.cloned.1.call-update) | async-done | bytes 2359312 | tf_op jit(solution)/shard_map/all_gather | solution.py:988
  751.3 24.0 %all-to-all-done.4 = bf16[4,240,1152]{2,1,0:T(8,128)(2,1)} async-done(((bf16[4,240,1152]{2,1,0:T(8,128)(2,1)}), bf16[4,240,1152]{2,1,0:T(8,128)(2,1)}, u32[]{:S(2)}, u32[]{:S(2)}) %all-to-all-start.4) | async-done | bytes 2211872 | tf_op jit(solution)/shard_map/all_to_all | solution.py:585
  790.2 8.7 %collective-permute-done.25.refs_2_ = bf16[1,192,1152]{2,1,0:T(8,128)(2,1)S(1)} collective-permute-done((bf16[1,192,1152]{2,1,0:T(8,128)(2,1)S(1)}, bf16[1,192,1152]{2,1,0:T(8,128)(2,1)S(1)}, u32[]{:S(2)}, u32[]{:S(2)}) %collective-permute-start.25) | collective-permute-done | bytes 442400 | tf_op jit(solution)/shard_map/ppermute | solution.py:581
  (411 shorter events, 229.2 us)
Async XLA Ops:
  7.2 256.2 %all-gather.11.cloned.1.call-start = ((), (), s32[]{:S(2)}) async-start(), calls=%async_computation.12 | async-start | bytes 9732096 | tf_op jit(solution)/shard_map/all_gather | solution.py:711
  17.8 31.6 %collective-permute-start.1 = (bf16[240,768]{1,0:T(8,128)(2,1)}, bf16[240,768]{1,0:T(8,128)(2,1)S(1)}, u32[]{:S(2)}, u32[]{:S(2)}) collective-permute-start(bf16[240,768]{1,0:T(8,128)(2,1)} %pad_maximum_fusion.25), channel_id=1, source_target_pairs={{0,2},{1,3},{2,0},{3,1},{4,6},{5,7},{6,4},{7,5},{8,10},{9,11},{10,... | collective-permute-start | bytes 1105928 | tf_op jit(solution)/shard_map/ppermute | solution.py:589
  17.8 31.7 %collective-permute-start = (bf16[240,768]{1,0:T(8,128)(2,1)}, bf16[240,768]{1,0:T(8,128)(2,1)S(1)}, u32[]{:S(2)}, u32[]{:S(2)}) collective-permute-start(bf16[240,768]{1,0:T(8,128)(2,1)} %pad_maximum_fusion.25), channel_id=1, source_target_pairs={{0,1},{1,2},{2,3},{3,0},{4,5},{5,6},{6,7},{7,4},{8,9},{9,10},{10,1... | collective-permute-start | bytes 1105928 | tf_op jit(solution)/shard_map/ppermute | solution.py:589
  51.0 245.6 %all-gather.13.cloned.1.call-start = ((), (), s32[]{:S(2)}) async-start(), calls=%async_computation.13 | async-start | bytes 9732096 | tf_op jit(solution)/shard_map/all_gather | solution.py:711
  57.6 76.5 %all-to-all-start = ((bf16[4,784,384]{2,1,0:T(8,128)(2,1)}), bf16[4,784,384]{2,1,0:T(8,128)(2,1)}, u32[]{:S(2)}, u32[]{:S(2)}) async-start(bf16[4,784,384]{2,1,0:T(8,128)(2,1)} %bitcast.211), calls=%async_computation | async-start | bytes 4816896 | tf_op jit(solution)/shard_map/all_to_all | solution.py:585
  67.7 34.2 %collective-permute-start.3 = (bf16[4,192,768]{2,1,0:T(8,128)(2,1)S(1)}, bf16[4,192,768]{2,1,0:T(8,128)(2,1)}, u32[]{:S(2)}, u32[]{:S(2)}) collective-permute-start(bf16[4,192,768]{2,1,0:T(8,128)(2,1)S(1)} %pad_maximum_fusion.6.refs_0_), channel_id=1, source_target_pairs={{0,8},{4,12},{8,0},{12,4},{16,24},{20,28},{24,16},{28,20},{1,9},{5... | collective-permute-start | bytes 3538952 | tf_op jit(solution)/shard_map/ppermute | solution.py:581
  69.3 32.7 %collective-permute-start.4 = (bf16[4,192,768]{2,1,0:T(8,128)(2,1)S(1)}, bf16[4,192,768]{2,1,0:T(8,128)(2,1)}, u32[]{:S(2)}, u32[]{:S(2)}) collective-permute-start(bf16[4,192,768]{2,1,0:T(8,128)(2,1)S(1)} %pad_maximum_fusion.6.refs_0_), channel_id=1, source_target_pairs={{0,16},{4,20},{8,24},{12,28},{16,0},{20,4},{24,8},{28,12},{1,17},{... | collective-permute-start | bytes 3538952 | tf_op jit(solution)/shard_map/ppermute | solution.py:581
  70.8 58.6 %collective-permute-start.5 = (bf16[4,192,768]{2,1,0:T(8,128)(2,1)S(1)}, bf16[4,192,768]{2,1,0:T(8,128)(2,1)}, u32[]{:S(2)}, u32[]{:S(2)}) collective-permute-start(bf16[4,192,768]{2,1,0:T(8,128)(2,1)S(1)} %pad_maximum_fusion.6.refs_0_), channel_id=1, source_target_pairs={{0,24},{4,28},{8,16},{12,20},{16,8},{20,12},{24,0},{28,4},{1,25},{... | collective-permute-start | bytes 3538952 | tf_op jit(solution)/shard_map/ppermute | solution.py:581
  71.3 78.1 %collective-permute-start.6 = (bf16[4,192,768]{2,1,0:T(8,128)(2,1)S(1)}, bf16[4,192,768]{2,1,0:T(8,128)(2,1)}, u32[]{:S(2)}, u32[]{:S(2)}) collective-permute-start(bf16[4,192,768]{2,1,0:T(8,128)(2,1)S(1)} %pad_maximum_fusion.6.refs_0_), channel_id=1, source_target_pairs={{0,4},{4,0},{8,12},{12,8},{16,20},{20,16},{24,28},{28,24},{1,5},{5... | collective-permute-start | bytes 3538952 | tf_op jit(solution)/shard_map/ppermute | solution.py:581
  101.9 47.4 %collective-permute-start.7 = (bf16[4,192,768]{2,1,0:T(8,128)(2,1)}, bf16[4,192,768]{2,1,0:T(8,128)(2,1)}, u32[]{:S(2)}, u32[]{:S(2)}) collective-permute-start(bf16[4,192,768]{2,1,0:T(8,128)(2,1)} %collective-permute-done.3.refs_1_), channel_id=1, source_target_pairs={{0,4},{4,0},{8,12},{12,8},{16,20},{20,16},{24,28},{28,24},{1,5},{5... | collective-permute-start | bytes 3538952 | tf_op jit(solution)/shard_map/ppermute | solution.py:581
  102.0 47.3 %collective-permute-start.8 = (bf16[4,192,768]{2,1,0:T(8,128)(2,1)}, bf16[4,192,768]{2,1,0:T(8,128)(2,1)}, u32[]{:S(2)}, u32[]{:S(2)}) collective-permute-start(bf16[4,192,768]{2,1,0:T(8,128)(2,1)} %collective-permute-done.4.refs_2_), channel_id=1, source_target_pairs={{0,4},{4,0},{8,12},{12,8},{16,20},{20,16},{24,28},{28,24},{1,5},{5... | collective-permute-start | bytes 3538952 | tf_op jit(solution)/shard_map/ppermute | solution.py:581
  134.1 83.5 %all-to-all-start.1 = ((bf16[4,768,384]{2,1,0:T(8,128)(2,1)}), bf16[4,768,384]{2,1,0:T(8,128)(2,1)}, u32[]{:S(2)}, u32[]{:S(2)}) async-start(bf16[4,768,384]{2,1,0:T(8,128)(2,1)} %bitcast.207), calls=%async_computation.1 | async-start | bytes 4718592 | tf_op jit(solution)/shard_map/all_to_all | solution.py:585
  208.7 50.3 %collective-permute-start.10 = (bf16[128,3072]{1,0:T(8,128)(2,1)S(1)}, bf16[128,3072]{1,0:T(8,128)(2,1)S(1)}, u32[]{:S(2)}, u32[]{:S(2)}) collective-permute-start(bf16[128,3072]{1,0:T(8,128)(2,1)S(1)} %convert_element_type.227), channel_id=1, source_target_pairs={{0,1},{1,2},{2,3},{4,5},{5,6},{6,7},{8,9},{9,10},{10,11},{12,13},{... | collective-permute-start | bytes 2359304 | tf_op jit(solution)/shard_map/ppermute | solution.py:886
  261.7 27.7 %collective-permute-start.11 = (bf16[128,3072]{1,0:T(8,128)(2,1)S(1)}, bf16[128,3072]{1,0:T(8,128)(2,1)S(1)}, u32[]{:S(2)}, u32[]{:S(2)}) collective-permute-start(bf16[128,3072]{1,0:T(8,128)(2,1)S(1)} %add_convert_fusion.7), channel_id=1, source_target_pairs={{0,1},{1,2},{2,3},{4,5},{5,6},{6,7},{8,9},{9,10},{10,11},{12,13},{... | collective-permute-start | bytes 2359304 | tf_op jit(solution)/shard_map/ppermute | solution.py:910
  292.1 25.4 %collective-permute-start.12 = (bf16[128,3072]{1,0:T(8,128)(2,1)S(1)}, bf16[128,3072]{1,0:T(8,128)(2,1)S(1)}, u32[]{:S(2)}, u32[]{:S(2)}) collective-permute-start(bf16[128,3072]{1,0:T(8,128)(2,1)S(1)} %add_convert_fusion.6), channel_id=1, source_target_pairs={{0,1},{1,2},{2,3},{4,5},{5,6},{6,7},{8,9},{9,10},{10,11},{12,13},{... | collective-permute-start | bytes 2359304 | tf_op jit(solution)/shard_map/ppermute | solution.py:910
  376.9 34.6 %collective-permute-start.15 = (bf16[3072,768]{1,0:T(8,128)(2,1)}, bf16[3072,768]{1,0:T(8,128)(2,1)}, u32[]{:S(2)}, u32[]{:S(2)}) collective-permute-start(bf16[3072,768]{1,0:T(8,128)(2,1)} %convolution_convert_fusion.2), channel_id=1, source_target_pairs={{0,4},{4,0},{8,12},{12,8},{16,20},{20,16},{24,28},{28,24},{1,5},{5... | collective-permute-start | bytes 14155784 | tf_op jit(solution)/shard_map/ppermute | solution.py:581
  377.0 30.2 %collective-permute-start.13 = (bf16[128,3072]{1,0:T(8,128)(2,1)S(1)}, bf16[128,3072]{1,0:T(8,128)(2,1)S(1)}, u32[]{:S(2)}, u32[]{:S(2)}) collective-permute-start(bf16[128,3072]{1,0:T(8,128)(2,1)S(1)} %convert_element_type.234), channel_id=1, source_target_pairs={{1,0},{2,1},{3,2},{5,4},{6,5},{7,6},{9,8},{10,9},{11,10},{13,12},{... | collective-permute-start | bytes 2359304 | tf_op jit(solution)/shard_map/ppermute | solution.py:957
  406.7 35.8 %collective-permute-start.17 = (bf16[768,3072]{1,0:T(8,128)(2,1)}, bf16[768,3072]{1,0:T(8,128)(2,1)}, u32[]{:S(2)}, u32[]{:S(2)}) collective-permute-start(bf16[768,3072]{1,0:T(8,128)(2,1)} %convolution_convert_fusion.1), channel_id=1, source_target_pairs={{0,4},{4,0},{8,12},{12,8},{16,20},{20,16},{24,28},{28,24},{1,5},{5... | collective-permute-start | bytes 14155784 | tf_op jit(solution)/shard_map/ppermute | solution.py:581
  433.4 182.5 %all-reduce.14.cloned.1.call-start = ((), (), s32[]{:S(2)}) async-start(), calls=%async_computation.14 | async-start | bytes 9437184
  437.8 119.7 %all-to-all-start.2 = ((bf16[4,768,384]{2,1,0:T(8,128)(2,1)}), bf16[4,768,384]{2,1,0:T(8,128)(2,1)}, u32[]{:S(2)}, u32[]{:S(2)}) async-start(bf16[4,768,384]{2,1,0:T(8,128)(2,1)} %after.14), calls=%async_computation.2 | async-start | bytes 4718592 | tf_op jit(solution)/shard_map/all_to_all | solution.py:585
  442.3 188.1 %reduce-scatter.13.cloned.1.call-start = ((), (), s32[]{:S(2)}) async-start(), calls=%async_computation.15 | async-start | bytes 5898240
  453.3 195.3 %reduce-scatter.11.cloned.1.call-start = ((), (), s32[]{:S(2)}) async-start(), calls=%async_computation.10 | async-start | bytes 1474560 | tf_op jit(solution)/shard_map/reduce_scatter | solution.py:987
  456.0 43.7 %collective-permute-start.16 = (bf16[128,3072]{1,0:T(8,128)(2,1)S(1)}, bf16[128,3072]{1,0:T(8,128)(2,1)}, u32[]{:S(2)}, u32[]{:S(2)}) collective-permute-start(bf16[128,3072]{1,0:T(8,128)(2,1)S(1)} %add_convert_fusion.4), channel_id=1, source_target_pairs={{1,0},{2,1},{3,2},{5,4},{6,5},{7,6},{9,8},{10,9},{11,10},{13,12},{... | collective-permute-start | bytes 2359304 | tf_op jit(solution)/shard_map/ppermute | solution.py:973
  592.0 27.1 %collective-permute-start.19 = (bf16[768,3456]{1,0:T(8,128)(2,1)}, bf16[768,3456]{1,0:T(8,128)(2,1)}, u32[]{:S(2)}, u32[]{:S(2)}) collective-permute-start(bf16[768,3456]{1,0:T(8,128)(2,1)} %convolution_convert_fusion), channel_id=1, source_target_pairs={{0,4},{4,0},{8,12},{12,8},{16,20},{20,16},{24,28},{28,24},{1,5},{5... | collective-permute-start | bytes 15925256 | tf_op jit(solution)/shard_map/ppermute | solution.py:581
  619.0 106.5 %reduce-scatter.9.cloned.1.call-start = ((), (), s32[]{:S(2)}) async-start(), calls=%async_computation.8 | async-start | bytes 1474560 | tf_op jit(solution)/shard_map/reduce_scatter | solution.py:987
  637.5 34.7 %collective-permute-start.21 = (bf16[208,3456]{1,0:T(8,128)(2,1)}, bf16[208,3456]{1,0:T(8,128)(2,1)}, u32[]{:S(2)}, u32[]{:S(2)}) collective-permute-start(bf16[208,3456]{1,0:T(8,128)(2,1)} %get-tuple-element.213), channel_id=1, source_target_pairs={{0,8},{4,12},{8,0},{12,4},{16,24},{20,28},{24,16},{28,20},{1,9},{5... | collective-permute-start | bytes 4313096 | tf_op jit(solution)/shard_map/ppermute | solution.py:581
  638.9 64.3 %collective-permute-start.22 = (bf16[208,3456]{1,0:T(8,128)(2,1)}, bf16[208,3456]{1,0:T(8,128)(2,1)}, u32[]{:S(2)}, u32[]{:S(2)}) collective-permute-start(bf16[208,3456]{1,0:T(8,128)(2,1)} %get-tuple-element.214), channel_id=1, source_target_pairs={{0,16},{4,20},{8,24},{12,28},{16,0},{20,4},{24,8},{28,12},{1,17},{... | collective-permute-start | bytes 4313096 | tf_op jit(solution)/shard_map/ppermute | solution.py:581
  639.9 63.3 %collective-permute-start.23 = (bf16[208,3456]{1,0:T(8,128)(2,1)}, bf16[208,3456]{1,0:T(8,128)(2,1)}, u32[]{:S(2)}, u32[]{:S(2)}) collective-permute-start(bf16[208,3456]{1,0:T(8,128)(2,1)} %get-tuple-element.215), channel_id=1, source_target_pairs={{0,24},{4,28},{8,16},{12,20},{16,8},{20,12},{24,0},{28,4},{1,25},{... | collective-permute-start | bytes 4313096 | tf_op jit(solution)/shard_map/ppermute | solution.py:581
  644.6 76.0 %all-to-all-start.3 = ((bf16[4,768,384]{2,1,0:T(8,128)(2,1)}), bf16[4,768,384]{2,1,0:T(8,128)(2,1)S(1)}, u32[]{:S(2)}, u32[]{:S(2)}) async-start(bf16[4,768,384]{2,1,0:T(8,128)(2,1)} %pad_maximum_fusion.4), calls=%async_computation.3 | async-start | bytes 4718592 | tf_op jit(solution)/shard_map/all_to_all | solution.py:585
  648.2 94.8 %all-gather.9.cloned.1.call-start = ((), (), s32[]{:S(2)}) async-start(), calls=%async_computation.11 | async-start | bytes 2654208 | tf_op jit(solution)/shard_map/all_gather | solution.py:988
  720.6 54.7 %all-to-all-start.4 = ((bf16[4,240,1152]{2,1,0:T(8,128)(2,1)}), bf16[4,240,1152]{2,1,0:T(8,128)(2,1)}, u32[]{:S(2)}, u32[]{:S(2)}) async-start(bf16[4,240,1152]{2,1,0:T(8,128)(2,1)} %pad_maximum_fusion.5), calls=%async_computation.4 | async-start | bytes 4423680 | tf_op jit(solution)/shard_map/all_to_all | solution.py:585
  725.1 86.1 %all-gather.7.cloned.1.call-start = ((), (), s32[]{:S(2)}) async-start(), calls=%async_computation.9 | async-start | bytes 2654208 | tf_op jit(solution)/shard_map/all_gather | solution.py:988
  (92 other events, 1700.2 us)
Sparse Core Ops, SparseCore 0:
  51.1 133.3 all-gather.10
  187.3 96.2 all-gather.12
  438.1 112.1 all-reduce.13
  553.7 57.1 reduce-scatter.12
  619.1 28.2 reduce-scatter.10
  650.2 45.9 reduce-scatter.8
  698.1 44.9 all-gather.8
  745.0 29.0 all-gather.6
